TPU v7x, 256 devices: a whole 4x4x8 slice. The times are simulated.
256 devices in a mesh: frm: 4 (over x), row: 16 (over z_lo, y, core), ch: 4 (over z_hi).
Axes of the slice: x: 4, y: 4, z: 8 (z_hi: 4, z_lo: 2; z = z_hi * 2 + z_lo), core: 2. Of those that a mesh axis runs over, the one named last changes fastest.
Arguments:
- latents: bfloat16 [65280, 16], P(('frm', 'row', 'ch')), may hold values from -40 to 40
- in_weight: bfloat16 [27, 16, 512], P(None, None, 'ch'), may hold values from -0.3125 to 0.3125
- in_gain: float32 [512], P('ch'), may hold values from 0.5 to 1.5
- in_shift: float32 [512], P('ch'), may hold values from -0.5 to 0.5
- mid_weight: bfloat16 [27, 512, 512], P(None, None, 'ch'), may hold values from -0.0546875 to 0.0546875
- mid_gain: float32 [512], P('ch'), may hold values from 0.5 to 1.5
- mid_shift: float32 [512], P('ch'), may hold values from -0.5 to 0.5
Outputs:
- decoded: bfloat16 [4, 96, 170, 512], P('frm', 'row', None, 'ch')
All inputs are finite; a program needn't handle non-finite values.
Results may differ from a plain program's by a relative error of at most 0.015.
Values may be sent and summed in bfloat16 or wider, within the bound.
No kernel may reach another device: no remote copies, remote signals or barrier semaphores. Data moves between devices by JAX's collectives and lax.ppermute only.
A program may use at most 128 MiB of HBM per device.

v0:
```python
import jax
import jax.numpy as jnp
from jax import lax
from jax.sharding import PartitionSpec as P

CH = 512
GROUPS = 32
W = 170
ROWS_DEV = 6


EPSILON = 1e-06


def padded_2(shard, sides, width):
    for axis, dim in sides:
        size, length = (lax.axis_size(axis), shard.shape[dim])
        up = [(i, (i + 1) % size) for i in range(size - 1)]
        down = [(j, i) for i, j in up]
        last = lax.slice_in_dim(shard, length - width, length, axis=dim)
        initial = lax.slice_in_dim(shard, 0, width, axis=dim)
        before = lax.ppermute(last, axis, up)
        after = lax.ppermute(initial, axis, down)
        shard = jnp.concatenate([before, shard, after], axis=dim)
    return shard


def shifted(value, axis, steps):
    count = lax.axis_size(axis)
    initial, last = (max(0, -steps), min(count, count - steps))
    return lax.ppermute(value, axis, [(source, source + steps) for source in range(initial, last)])


def conv_block(source, weight, out_frames, out_rows):
    in_chans = source.shape[3]
    columns = source.shape[2]
    out_chans = weight.shape[2]
    padded = jnp.pad(source, ((0, 0), (0, 0), (1, 1), (0, 0)))
    stacked = jnp.concatenate(
        [padded[0:out_frames], padded[1 : out_frames + 1], padded[2 : out_frames + 2]], axis=3
    )
    kernels = weight.reshape(3, 3, 3, in_chans, out_chans)
    running = jnp.zeros((out_frames * out_rows * columns, out_chans), jnp.float32)
    for row_tap in range(3):
        for col_tap in range(3):
            window = stacked[
                :, row_tap : row_tap + out_rows, col_tap : col_tap + columns, :
            ].reshape(-1, 3 * in_chans)
            kernel = jnp.concatenate(
                [
                    kernels[0, row_tap, col_tap],
                    kernels[1, row_tap, col_tap],
                    kernels[2, row_tap, col_tap],
                ],
                axis=0,
            )
            running = running + jnp.dot(window, kernel, preferred_element_type=jnp.float32)
    return running.reshape(out_frames, out_rows, columns, out_chans)


def group_moments(own_values, total_cells):
    local_chans = own_values.shape[-1]
    group_width = CH // GROUPS
    grouped = own_values.reshape(-1, local_chans // group_width, group_width)
    count = total_cells * group_width
    sums = lax.psum(jnp.sum(grouped, axis=(0, 2)), ("frm", "row"))
    centre = sums / count
    offsets = grouped - centre[None, :, None]
    squares = lax.psum(jnp.sum(offsets * offsets, axis=(0, 2)), ("frm", "row"))
    spread = squares / count
    return (centre, spread)


def apply_norm(values, centre, spread, gain_vec, bias_term):
    group_width = CH // GROUPS
    inv_spread = lax.rsqrt(spread + EPSILON)
    centre_chan = jnp.repeat(centre, group_width)
    scale_chan = jnp.repeat(inv_spread, group_width)
    return jax.nn.silu((values - centre_chan) * scale_chan * gain_vec + bias_term)


def per_device(latents, in_weight, in_gain, in_shift, mid_weight, mid_gain, mid_shift):
    slab = lax.all_gather(latents, "ch", axis=0, tiled=True).reshape(
        1, ROWS_DEV, W, latents.shape[1]
    )
    total_cells = ROWS_DEV * W * lax.axis_size("frm") * lax.axis_size("row")
    rimmed = padded_2(slab, (("row", 1),), 1)
    history = [shifted(rimmed, "frm", offset) for offset in (2, 1)]
    hidden = conv_block(jnp.concatenate(history + [rimmed], axis=0), in_weight, 1, ROWS_DEV)
    centre, spread = group_moments(hidden, total_cells)
    activated = apply_norm(hidden, centre, spread, in_gain, in_shift).astype(jnp.bfloat16)
    framed = padded_2(activated, (("row", 1),), 1)
    earlier = [shifted(framed, "frm", offset) for offset in (2, 1)]
    stacked_in = jnp.concatenate(earlier + [framed], axis=0)
    mixed = conv_block(
        lax.all_gather(stacked_in, "ch", axis=3, tiled=True), mid_weight, 1, ROWS_DEV
    )
    centre, spread = group_moments(mixed, total_cells)
    return apply_norm(mixed, centre, spread, mid_gain, mid_shift).astype(jnp.bfloat16)


def solution(mesh):
    return jax.shard_map(
        per_device,
        mesh=mesh,
        in_specs=(
            P(("frm", "row", "ch"), None),
            P(None, None, "ch"),
            P("ch"),
            P("ch"),
            P(None, None, "ch"),
            P("ch"),
            P("ch"),
        ),
        out_specs=P("frm", "row", None, "ch"),
        check_vma=False,
    )
```

profile of v0, /device:TPU:1, one launch (start us, length us, event | category | flops | bytes accessed | tf_op | source)
XLA Modules:
  0.0 789.7 jit_solution(1920448441920554730)
XLA Ops:
  6.5 15.6 %all-gather = bf16[4,255,16]{1,2,0:T(8,128)(2,1)S(1)} all-gather(bf16[1,255,16]{1,2,0:T(8,128)(2,1)} %bitcast.153), channel_id=1, replica_groups=mesh['frm'=4,'row'=16,'ch'=4] {'ch'}, dimensions={0}, use_global_device_ids=true | all-gather | bytes 40800 | tf_op jit(solution)/shard_map/all_gather | solution.py:83
  22.3 6.6 collective-permute-start
  34.0 4.7 collective-permute-start.2
  47.4 137.0 %psum.28 = f32[8]{0:T(128)S(1)} all-reduce(f32[8]{0:T(128)S(1)} %reduce_sum.51), channel_id=1, replica_groups=mesh['frm'=4,'row'=16,'ch'=4] {'frm','row'}, use_global_device_ids=true, to_apply=%region_2.3 | all-reduce | flops 8 | bytes 64 | tf_op jit(solution)/shard_map/psum | solution.py:66
  185.8 140.7 %psum.29 = f32[8]{0:T(128)} all-reduce(f32[8]{0:T(128)S(1)} %reduce_sum.54), channel_id=1, replica_groups=mesh['frm'=4,'row'=16,'ch'=4] {'frm','row'}, use_global_device_ids=true, to_apply=%region_5.6 | all-reduce | flops 8 | bytes 64 | tf_op jit(solution)/shard_map/psum | solution.py:69
  330.5 2.4 collective-permute-start.5
  332.9 2.9 collective-permute-done.5
  338.7 6.8 collective-permute-done.6
  345.5 6.1 collective-permute-done.7
  355.2 85.1 %all-gather.3.cloned.1.call-done = bf16[3,8,170,512]{3,2,1,0:T(8,128)(2,1)} async-done(((bf16[3,8,170,128]{3,2,1,0:T(8,128)(2,1)}), bf16[3,8,170,512]{3,2,1,0:T(8,128)(2,1)}) %all-gather.3.cloned.1.call-update) | async-done | bytes 4177936 | tf_op jit(solution)/shard_map/all_gather | solution.py:96
  440.4 4.3 pad_slice_fusion.2
  445.1 9.5 %fusion.115 = (bf16[1,6,170,1536]{3,2,1,0:T(8,128)(2,1)}, bf16[1,6,170,1536]{3,2,1,0:T(8,128)(2,1)}, bf16[1,6,170,1536]{3,2,1,0:T(8,128)(2,1)S(1)}, bf16[1,6,170...) fusion(bf16[1,8,172,1536]{3,2,1,0:T(8,128)(2,1)S(1)} %pad_maxim, ...), kind=kLoop, calls=%fused_computation.205 | loop fusion | bytes 56401920 | tf_op jit(solution)/shard_map/slice | solution.py:46
  454.6 3.8 reshape.209
  458.4 3.9 reshape.211
  462.3 3.9 reshape.212
  466.1 3.8 reshape.213
  470.0 3.8 reshape.214
  473.8 3.9 reshape.215
  477.6 2.5 reshape.216
  480.1 2.4 reshape.217
  482.6 3.9 reshape.218
  486.5 3.0 fusion
  501.6 138.6 %psum.30 = f32[8]{0:T(128)S(1)} all-reduce(f32[8]{0:T(128)S(1)} %reduce_sum.72), channel_id=1, replica_groups=mesh['frm'=4,'row'=16,'ch'=4] {'frm','row'}, use_global_device_ids=true, to_apply=%region_8.9 | all-reduce | flops 8 | bytes 64 | tf_op jit(solution)/shard_map/psum | solution.py:66
  640.8 141.0 %psum.31 = f32[8]{0:T(128)S(1)} all-reduce(f32[8]{0:T(128)S(1)} %reduce_sum.75), channel_id=1, replica_groups=mesh['frm'=4,'row'=16,'ch'=4] {'frm','row'}, use_global_device_ids=true, to_apply=%region_11.12 | all-reduce | flops 8 | bytes 64 | tf_op jit(solution)/shard_map/psum | solution.py:69
  (156 shorter events, 39.5 us)
Async XLA Ops:
  6.5 433.8 %all-gather.3.cloned.1.call-start = ((), (), s32[]{:S(2)}) async-start(), calls=%async_computation | async-start | bytes 5406720 | tf_op jit(solution)/shard_map/all_gather | solution.py:96
  22.3 9.4 %collective-permute-start = (bf16[1,1,170,16]{2,1,3,0:T(2,128)(2,1)S(1)}, bf16[1,1,170,16]{2,1,3,0:T(2,128)(2,1)S(1)}, u32[]{:S(2)}, u32[]{:S(2)}) collective-permute-start(bf16[1,1,170,16]{2,1,3,0:T(2,128)(2,1)S(1)} %get-tuple-element.85), channel_id=1, source_target_pairs={{0,4},{4,8},{8,12},{12,16},{16,20},{20,24},{24,28},{28,32},{32,36}... | collective-permute-start | bytes 16328 | tf_op jit(solution)/shard_map/ppermute | solution.py:22
  28.8 5.1 collective-permute-start.1
  34.0 7.7 collective-permute-start.2
  38.6 3.5 collective-permute-start.3
  46.1 281.2 %copy-start.35 = (f32[128]{0:T(128)S(1)}, f32[128]{0:T(128)}, u32[]{:S(2)}) copy-start(f32[128]{0:T(128)} %param.10) | copy-start | bytes 1540
  185.8 167.0 %copy-start.6 = (bf16[27,512,128]{2,1,0:T(8,128)(2,1)S(1)}, bf16[27,512,128]{2,1,0:T(8,128)(2,1)}, u32[]{:S(2)}) copy-start(bf16[27,512,128]{2,1,0:T(8,128)(2,1)} %param.11) | copy-start | bytes 10616836
  328.5 4.3 collective-permute-start.4
  330.5 5.4 collective-permute-start.5
  335.9 9.6 %collective-permute-start.6 = (bf16[1,8,170,128]{3,2,1,0:T(8,128)(2,1)S(1)}, bf16[1,8,170,128]{3,2,1,0:T(8,128)(2,1)S(1)}, u32[]{:S(2)}, u32[]{:S(2)}) collective-permute-start(bf16[1,8,170,128]{3,2,1,0:T(8,128)(2,1)S(1)} %pad_maximum_fusion.1), channel_id=1, source_target_pairs={{0,128},{64,192},{1,129},{65,193},{2,130},{66,194},{3,131},{67,195... | collective-permute-start | bytes 1044488 | tf_op jit(solution)/shard_map/ppermute | solution.py:31
  337.2 14.3 %collective-permute-start.7 = (bf16[1,8,170,128]{3,2,1,0:T(8,128)(2,1)S(1)}, bf16[1,8,170,128]{3,2,1,0:T(8,128)(2,1)S(1)}, u32[]{:S(2)}, u32[]{:S(2)}) collective-permute-start(bf16[1,8,170,128]{3,2,1,0:T(8,128)(2,1)S(1)} %pad_maximum_fusion.1), channel_id=1, source_target_pairs={{0,64},{64,128},{128,192},{1,65},{65,129},{129,193},{2,66},{66,130... | collective-permute-start | bytes 1044488 | tf_op jit(solution)/shard_map/ppermute | solution.py:31
  482.5 4.0 copy-start.32
  482.5 4.0 copy-start.33
  482.5 4.0 copy-start.34
  486.5 3.1 copy-start.5
  486.5 3.1 copy-start.26
  486.5 3.1 copy-start.27
  486.5 3.1 copy-start.28
  490.6 2.1 copy-start.3
  490.6 2.1 copy-start.20
  490.6 2.1 copy-start.21
  490.6 2.1 copy-start.22
  500.4 281.6 %copy-start.36 = (f32[128]{0:T(128)S(1)}, f32[128]{0:T(128)}, u32[]{:S(2)}) copy-start(f32[128]{0:T(128)} %param.13) | copy-start | bytes 1540
  500.4 281.6 %copy-start.37 = (f32[128]{0:T(128)S(1)}, f32[128]{0:T(128)}, u32[]{:S(2)}) copy-start(f32[128]{0:T(128)} %param.12) | copy-start | bytes 1540
  (23 other events, 44.4 us)
Sparse Core Ops, SparseCore 0:
  352.9 87.4 all-gather.2
where the time goes:
time: 790 us
  blocking collectives  573 us (73%)
  waiting for transfers between devices  104 us (13%)
  local copies, waits for them, and re-layouts  57.8 us (7%)
  starting transfers between devices  22.5 us (3%)
  between operations  14.1 us (2%)
  matrix products  13.3 us (2%)
    psum x2, blocking collectives, group_moments(): squares = lax.psum(jnp.sum(offsets * offsets, axis=(0, 2)), ('frm', 'row'))  282 us
    psum x2, blocking collectives, group_moments(): sums = lax.psum(jnp.sum(grouped, axis=(0, 2)), ('frm', 'row'))  276 us
    all_gather x1, waiting for transfers between devices, per_device(): lax.all_gather(stacked_in, 'ch', axis=3, tiled=True)  85.1 us
    reshape x18, local copies, waits for them, and re-layouts, conv_block(): window = stacked[:, row_tap:row_tap + out_rows, col_tap:col_tap + columns...  33.6 us
  transfers between devices with their start and end apart: 9, of which 6 were waited for; matrix products, arithmetic and copies ran while one was open for 1% of the time, Pallas kernels for 0%

commit v1 on v0

v1 whole, which is shorter than its diff:
```python
import jax
import jax.numpy as jnp
from jax import lax
from jax.experimental import pallas as pl
from jax.experimental.pallas import tpu as pltpu
from jax.sharding import PartitionSpec as P

CH = 512
GROUP = 16
W = 170
ROWS = 6
C_LAT = 16
FRAMES = 4
EPSILON = 1e-06

STRIDE = 176
SPAN = 8 * STRIDE
OWN = ROWS * STRIDE
TAPS = 9 * C_LAT
LEAD = 128
XLANES = 2048
WROWS = 448
CHUNKS = ((0, 384), (384, 384), (768, 384), (1152, 256))
CELLS = ROWS * W
VMEM = 48 * 1024 * 1024


def pieces3(v):
    high = lax.reduce_precision(v, 8, 7)
    mid = lax.reduce_precision(v - high, 8, 7)
    low = lax.reduce_precision(v - high - mid, 8, 7)
    return jnp.stack([high, mid, low]).astype(jnp.bfloat16)


def silu(u):
    half = 0.5 * u
    return half + half * jnp.tanh(half)


def group_mean(v):
    r = lax.broadcasted_iota(jnp.int32, (128, 128), 0) // GROUP
    c = lax.broadcasted_iota(jnp.int32, (128, 128), 1) // GROUP
    same = jnp.where(r == c, 1.0 / GROUP, 0.0).astype(jnp.float32)
    parts = [
        jnp.dot(
            v[:, i : i + 128],
            same,
            precision=lax.Precision.HIGHEST,
            preferred_element_type=jnp.float32,
        )
        for i in range(0, v.shape[1], 128)
    ]
    return parts[0] if len(parts) == 1 else jnp.concatenate(parts, axis=1)


def combine(means, squares, cells):
    n, lanes = means.shape
    mean = jnp.sum(means, axis=0, keepdims=True) / n
    off = means - mean
    var = (jnp.sum(squares, axis=0, keepdims=True) / cells + jnp.sum(off * off, axis=0, keepdims=True)) / n
    mean_g = group_mean(jnp.broadcast_to(mean, (8, lanes)))
    off_g = mean - mean_g
    var_g = group_mean(var + off_g * off_g)
    return mean_g[:1], var_g[:1]


def k1(pos_ref, g_ref, w0, w1, w2, w3, pt_ref, wall_ref, st_ref, x_ref):
    c = pos_ref[0]
    for j, w in enumerate((w0, w1, w2, w3)):
        wall_ref[lax.rem(c + j, 4)] = w[...]
    x_ref[...] = jnp.zeros_like(x_ref)
    pt_ref[: 2 * TAPS, :] = jnp.zeros((2 * TAPS, SPAN), jnp.bfloat16)

    def src(f, kind, j, lo, hi):
        return g_ref[4 * f + j, 16 * kind : 16 * kind + 16, lo:hi]

    own, nbr = 0, 1
    plan = (
        ((nbr, 2, 170, 255), (nbr, 3, 0, 85)),
        ((nbr, 3, 85, 255),),
        ((own, 0, 0, 170),),
        ((own, 0, 170, 255), (own, 1, 0, 85)),
        ((own, 1, 85, 255),),
        ((own, 2, 0, 170),),
        ((own, 2, 170, 255), (own, 3, 0, 85)),
        ((own, 3, 85, 255),),
        ((nbr, 0, 0, 170),),
        ((nbr, 0, 170, 255), (nbr, 1, 0, 85)),
    )
    for f in range(FRAMES):
        for row, parts in enumerate(plan):
            lane = LEAD + STRIDE * row
            for kind, j, lo, hi in parts:
                x_ref[16 * f : 16 * f + 16, lane : lane + hi - lo] = src(f, kind, j, lo, hi)
                lane += hi - lo
    for f in range(FRAMES):
        for b in range(3):
            for e in range(3):
                at = (f + 2) * TAPS + (3 * b + e) * 16
                lane = LEAD + STRIDE * b + e - 1
                pt_ref[at : at + 16, :] = x_ref[16 * f : 16 * f + 16, lane : lane + SPAN]

    weight = jnp.concatenate([wall_ref[j, :432, :] for j in range(4)], axis=1)

    def hidden(g, lo, size):
        at = pl.multiple_of(g * TAPS, 16)
        return lax.dot_general(
            pt_ref[pl.ds(at, 3 * TAPS), lo : lo + size],
            weight,
            (((0,), (0,)), ((), ())),
            preferred_element_type=jnp.float32,
        )

    def valid(lo, size):
        at = lo + lax.broadcasted_iota(jnp.int32, (size, 128), 0)
        ok = (at >= STRIDE) & (at < STRIDE + OWN)
        for row in range(1, 7):
            gap = STRIDE * row + W
            if lo < gap + STRIDE - W and gap < lo + size:
                ok = ok & ((at < gap) | (at >= gap + STRIDE - W))
        return jnp.concatenate([ok] * 4, axis=1)

    first = hidden(0, 256, 128)
    pilot = jnp.sum(jnp.where(valid(256, 128), first, 0.0), axis=0, keepdims=True) * (1.0 / 122)

    def frame(g, carry):
        s1, s2 = carry
        for lo, size in CHUNKS:
            h = hidden(g, lo, size)
            d = jnp.where(valid(lo, size), h - pilot, 0.0)
            d = d.reshape(size // 8, 8, CH)
            s1 = s1 + jnp.sum(d, axis=0)
            s2 = s2 + jnp.sum(d * d, axis=0)
        return s1, s2

    zero = jnp.zeros((8, CH), jnp.float32)
    s1, s2 = lax.fori_loop(0, FRAMES, frame, (zero, zero))
    n = FRAMES * CELLS
    s1 = jnp.sum(s1, axis=0, keepdims=True)
    s2 = jnp.sum(s2, axis=0, keepdims=True)
    d = s1 / n
    st_ref[:, 0:1, :] = jnp.broadcast_to((pilot + d)[None], (16, 1, CH))
    st_ref[:, 1:2, :] = jnp.broadcast_to((s2 - s1 * d)[None], (16, 1, CH))


def k2(pos_ref, pt_ref, wall_ref, st_ref, w2_hbm, mix_ref, so_ref, a_ref, w2_ref, y_ref, sem):
    copy = pltpu.make_async_copy(w2_hbm, w2_ref, sem)
    copy.start()
    f, top, bottom = pos_ref[1], pos_ref[2], pos_ref[3]
    weight = jnp.concatenate([wall_ref[j, :432, :] for j in range(4)], axis=1)
    extra = jnp.concatenate([wall_ref[j, 432:, :] for j in range(4)], axis=1).astype(jnp.float32)
    gain = extra[0:1] + extra[1:2] + extra[2:3]
    shift = extra[3:4] + extra[4:5] + extra[5:6]
    mean, var = combine(st_ref[:, 0, :], st_ref[:, 1, :], FRAMES * CELLS)
    scale = lax.rsqrt(var + EPSILON) * gain

    a_ref[0:16, :] = jnp.zeros((16, 3 * CH), jnp.bfloat16)
    a_ref[16 + SPAN :, :] = jnp.zeros((16, 3 * CH), jnp.bfloat16)
    for k in range(3):
        g = f - 2 + k

        @pl.when(g >= 0)
        def _():
            at = pl.multiple_of(g * TAPS, 16)
            for lo, size in CHUNKS:
                h = lax.dot_general(
                    pt_ref[pl.ds(at, 3 * TAPS), lo : lo + size],
                    weight,
                    (((0,), (0,)), ((), ())),
                    preferred_element_type=jnp.float32,
                )
                u = (h - mean) * scale + shift
                a_ref[16 + lo : 16 + lo + size, k * CH : (k + 1) * CH] = silu(u).astype(jnp.bfloat16)

        @pl.when(g < 0)
        def _():
            a_ref[16 : 16 + SPAN, k * CH : (k + 1) * CH] = jnp.zeros((SPAN, CH), jnp.bfloat16)

    keep = lax.broadcasted_iota(jnp.int32, (16, 3 * CH), 0) < 10
    for row in range(8):
        at = 16 + STRIDE * row + 160
        a_ref[at : at + 16, :] = jnp.where(keep, a_ref[at : at + 16, :], 0).astype(jnp.bfloat16)

    @pl.when(top == 1)
    def _():
        a_ref[16 : 16 + STRIDE, :] = jnp.zeros((STRIDE, 3 * CH), jnp.bfloat16)

    @pl.when(bottom == 1)
    def _():
        a_ref[16 + 7 * STRIDE : 16 + SPAN, :] = jnp.zeros((STRIDE, 3 * CH), jnp.bfloat16)

    copy.wait()

    def taps(b, e):
        return jnp.concatenate([w2_ref[9 * a + 3 * b + e] for a in range(3)], axis=0)

    def product(start, step, steps, kernel):
        lanes = kernel.shape[1]

        def one(i, _):
            at = pl.multiple_of(i * step, 16)
            y_ref[pl.ds(at, step), :lanes] = jnp.dot(
                a_ref[pl.ds(start + at, step), :], kernel, preferred_element_type=jnp.float32
            )
            return 0

        lax.fori_loop(0, steps, one, 0)

    for b in range(3):
        product(STRIDE * b, 272, 4, jnp.concatenate([taps(b, 0), taps(b, 2)], axis=1))
        part = y_ref[15 : 15 + OWN, :128] + y_ref[17 : 17 + OWN, 128:]
        mix_ref[...] = part if b == 0 else mix_ref[...] + part
    product(16, 352, 4, jnp.concatenate([taps(0, 1), taps(2, 1)], axis=1))
    mix_ref[...] += y_ref[0:OWN, :128] + y_ref[2 * STRIDE : 2 * STRIDE + OWN, 128:]
    product(16 + STRIDE, 352, 3, taps(1, 1))
    v = (mix_ref[...] + y_ref[0:OWN, :128]).reshape(ROWS, STRIDE, 128)
    mix_ref[...] = v.reshape(OWN, 128)
    ok = lax.broadcasted_iota(jnp.int32, (ROWS, STRIDE, 128), 1) < W
    total = jnp.sum(jnp.sum(jnp.where(ok, v, 0.0), axis=0), axis=0, keepdims=True)
    centre = total / CELLS
    off = jnp.where(ok, v - centre[None], 0.0)
    squares = jnp.sum(jnp.sum(off * off, axis=0), axis=0, keepdims=True)
    so_ref[:, 0:1, :] = jnp.broadcast_to(centre[None], (64, 1, 128))
    so_ref[:, 1:2, :] = jnp.broadcast_to(squares[None], (64, 1, 128))


def k3(mix_ref, st_ref, gain_ref, shift_ref, out_ref):
    mean, var = combine(st_ref[:, 0, :], st_ref[:, 1, :], CELLS)
    scale = lax.rsqrt(var + EPSILON) * gain_ref[...]
    for row in range(ROWS):
        v = mix_ref[STRIDE * row : STRIDE * (row + 1), :]
        u = silu((v - mean) * scale + shift_ref[...])
        out_ref[0, row] = u[:W].astype(jnp.bfloat16)


def shape(dims, kind):
    return jax.ShapeDtypeStruct(dims, kind)


SMEM = pl.BlockSpec(memory_space=pltpu.SMEM)
INVMEM = pl.BlockSpec(memory_space=pltpu.VMEM)


def call_k1(pos, g, ws):
    return pl.pallas_call(
        k1,
        out_shape=(
            shape((6 * TAPS, SPAN), jnp.bfloat16),
            shape((4, WROWS, 128), jnp.bfloat16),
            shape((16, 2, CH), jnp.float32),
        ),
        in_specs=[SMEM] + [INVMEM] * 5,
        out_specs=(INVMEM,) * 3,
        scratch_shapes=[pltpu.VMEM((16 * FRAMES, XLANES), jnp.bfloat16)],
        compiler_params=pltpu.CompilerParams(vmem_limit_bytes=VMEM),
    )(pos, g, *ws)


def call_k2(pos, pt, wall, st, w2):
    return pl.pallas_call(
        k2,
        out_shape=(shape((OWN, 128), jnp.float32), shape((64, 2, 128), jnp.float32)),
        in_specs=[SMEM] + [INVMEM] * 3 + [pl.BlockSpec(memory_space=pl.ANY)],
        out_specs=(INVMEM,) * 2,
        scratch_shapes=[
            pltpu.VMEM((SPAN + 32, 3 * CH), jnp.bfloat16),
            pltpu.VMEM((27, CH, 128), jnp.bfloat16),
            pltpu.VMEM((SPAN, 256), jnp.float32),
            pltpu.SemaphoreType.DMA,
        ],
        compiler_params=pltpu.CompilerParams(vmem_limit_bytes=VMEM),
    )(pos, pt, wall, st, w2)


def call_k3(mix, st, gain, bias):
    return pl.pallas_call(
        k3,
        out_shape=shape((1, ROWS, W, 128), jnp.bfloat16),
        in_specs=[INVMEM] * 4,
        out_specs=INVMEM,
        compiler_params=pltpu.CompilerParams(vmem_limit_bytes=VMEM),
    )(mix, st, gain, bias)


def per_device(latents, in_weight, in_gain, in_shift, mid_weight, mid_gain, mid_shift):
    f, r, c = (lax.axis_index(axis) for axis in ("frm", "row", "ch"))
    pos = jnp.stack([c, f, r == 0, r == 15]).astype(jnp.int32)
    nbrs = [(4 * (i + 1) + j, 4 * i + j) for i in range(15) for j in (0, 1)]
    nbrs += [(4 * i + j, 4 * (i + 1) + j) for i in range(15) for j in (2, 3)]
    tokens = latents.T
    nbr = lax.ppermute(tokens, ("row", "ch"), nbrs)
    held = jnp.concatenate(
        [
            in_weight.reshape(27 * C_LAT, 128),
            pieces3(in_gain),
            pieces3(in_shift),
            jnp.zeros((WROWS - 438, 128), jnp.bfloat16),
        ]
    )
    ws = [held] + [lax.ppermute(held, "ch", [((i + k) % 4, i) for i in range(4)]) for k in (1, 2, 3)]
    payload = jnp.concatenate([tokens, nbr], axis=0)
    g = lax.all_to_all(jnp.broadcast_to(payload[None], (16, 32, 255)), ("frm", "ch"), 0, 0)
    pt, wall, st = call_k1(pos, g, ws)
    st = lax.all_to_all(st, "row", 0, 0)
    mix, st = call_k2(pos, pt, wall, st, mid_weight)
    st = lax.all_to_all(st, ("frm", "row"), 0, 0)
    return call_k3(mix, st, mid_gain.reshape(1, 128), mid_shift.reshape(1, 128))


def solution(mesh):
    return jax.shard_map(
        per_device,
        mesh=mesh,
        in_specs=(
            P(("frm", "row", "ch"), None),
            P(None, None, "ch"),
            P("ch"),
            P("ch"),
            P(None, None, "ch"),
            P("ch"),
            P("ch"),
        ),
        out_specs=P("frm", "row", None, "ch"),
        check_vma=False,
    )
```

time: 790 us -> 83.8 us (0.11)
  blocking collectives: 573 us -> 27.5 us
  waiting for transfers between devices: 104 us -> 10.8 us
  local copies, waits for them, and re-layouts: 57.8 us -> 1.8 us
  Pallas kernels: 0 us -> 17.6 us
  between operations: 14.1 us -> 0.07 us
  matrix products: 13.3 us -> 0 us
    psum x4 -> x0, blocking collectives: 557 us -> none  [the longest x2 282 us: group_moments(): squares = lax.psum(jnp.sum(offsets * offsets, axis=(0, 2)), ('frm', 'row'))]
    all_gather x1 -> x0, waiting for transfers between devices: 85.1 us -> none  [per_device(): lax.all_gather(stacked_in, 'ch', axis=3, tiled=True)]
    reshape x21 -> x0, local copies, waits for them, and re-layouts: 34.6 us -> none  [the longest x18 33.6 us: conv_block(): window = stacked[:, row_tap:row_tap + out_rows, col_tap:col_tap + columns...]
    all_to_all x0 -> x2, blocking collectives: none -> 27.5 us  [the longest x1 15.9 us: per_device(): st = lax.all_to_all(st, ('frm', 'row'), 0, 0)]
    pallas_call x0 -> x3, Pallas kernels: none -> 17.6 us  [the longest x1 10.9 us: call_k2(): pl.pallas_call(k2, out_shape=(shape((OWN, 128), jnp.float32), shape((64,...]
    all_gather x1 -> x0, blocking collectives: 15.6 us -> none  [per_device(): lax.all_gather(latents, 'ch', axis=0, tiled=True)]
    slice x6 -> x0, local copies, waits for them, and re-layouts: 14.4 us -> none  [the longest x2 10.1 us: conv_block(): stacked[:, row_tap:row_tap + out_rows, col_tap:col_tap + columns, :]]
    dot_general x18 -> x0, matrix products: 13.3 us -> none  [conv_block(): jnp.dot(window, kernel, preferred_element_type=jnp.float32)]
  transfers between devices with their start and end apart: 9 -> 5, of which waited for: 6 -> 3; matrix products, arithmetic and copies ran while one was open for 1% -> 2% of each run, Pallas kernels for 0% -> 0%
where the time goes in v1:
time: 83.8 us; the launch traced here: 83.4 us
  blocking collectives  27.5 us (33%)
  starting transfers between devices  24.2 us (29%)
  Pallas kernels  17.6 us (21%)
  waiting for transfers between devices  10.8 us (13%)
  local copies, waits for them, and re-layouts  1.8 us (2%)
  other arithmetic  1.46 us (2%)
    all_to_all x1, blocking collectives, per_device(): st = lax.all_to_all(st, ('frm', 'row'), 0, 0)  15.9 us
    all_to_all x1, blocking collectives, per_device(): st = lax.all_to_all(st, 'row', 0, 0)  11.6 us
    pallas_call x1, Pallas kernels, call_k2(): pl.pallas_call(k2, out_shape=(shape((OWN, 128), jnp.float32), shape((64,...  10.9 us
    all_to_all x1, starting transfers between devices, per_device(): lax.all_to_all(jnp.broadcast_to(payload[None], (16, 32, 255)), ('frm', 'c...  10.2 us
    ppermute x3, waiting for transfers between devices, per_device(): lax.ppermute(held, 'ch', [((i + k) % 4, i) for i in range(4)])  9.77 us
    ppermute x3, starting transfers between devices, per_device(): lax.ppermute(held, 'ch', [((i + k) % 4, i) for i in range(4)])  8.92 us
    pallas_call x1, Pallas kernels, call_k1(): pl.pallas_call(k1, out_shape=(shape((6 * TAPS, SPAN), jnp.bfloat16), shap...  5.34 us
    ppermute x1, starting transfers between devices, per_device(): nbr = lax.ppermute(tokens, ('row', 'ch'), nbrs)  5.14 us
  transfers between devices with their start and end apart: 5, of which 3 were waited for; matrix products, arithmetic and copies ran while one was open for 2% of the time, Pallas kernels for 0%

profile of v1, /device:TPU:1, one launch (start us, length us, event | category | flops | bytes accessed | tf_op | source)
XLA Modules:
  0.0 83.4 jit_solution(9760567295078687469)
XLA Ops:
  0.0 5.1 %collective-permute-start = (bf16[16,255]{1,0:T(8,128)(2,1)}, bf16[16,255]{1,0:T(8,128)(2,1)S(1)}, u32[]{:S(2)}, u32[]{:S(2)}) collective-permute-start(bf16[16,255]{1,0:T(8,128)(2,1)} %bitcast.23), channel_id=1, source_target_pairs={{4,0},{5,1},{8,4},{9,5},{12,8},{13,9},{16,12},{17,13},{20,16},{21,... | collective-permute-start | bytes 24488 | tf_op jit(solution)/shard_map/ppermute | solution.py:291
  5.1 1.0 %collective-permute-done = bf16[16,255]{1,0:T(8,128)(2,1)S(1)} collective-permute-done((bf16[16,255]{1,0:T(8,128)(2,1)}, bf16[16,255]{1,0:T(8,128)(2,1)S(1)}, u32[]{:S(2)}, u32[]{:S(2)}) %collective-permute-start) | collective-permute-done | bytes 8192 | tf_op jit(solution)/shard_map/ppermute | solution.py:291
  6.2 0.7 pad_maximum_fusion
  6.9 0.7 broadcast_in_dim.4
  7.6 10.2 %all-to-all-start = ((bf16[16,32,255]{2,1,0:T(8,128)(2,1)}), bf16[16,32,255]{2,1,0:T(8,128)(2,1)S(1)}, u32[]{:S(2)}, u32[]{:S(2)}) async-start(bf16[16,32,255]{2,1,0:T(8,128)(2,1)} %broadcast_in_dim.4), calls=%async_computation | async-start | bytes 524288 | tf_op jit(solution)/shard_map/all_to_all | solution.py:302
  17.8 0.7 fusion.4
  18.5 1.1 %concatenate.8.w0 = bf16[448,128]{1,0:T(8,128)(2,1)S(1)} concatenate(bf16[432,128]{1,0:T(8,128)(2,1)} %bitcast.22, bf16[1,128]{1,0:T(2,128)(2,1)S(1)} %get-tuple-element.20, bf16[1,128]{1,0:T(2,128)(2,1)S(1)} %get-tuple-element.19, bf16[1,128]{1,0:T(2,128)(2,1)S(1)} %get-tuple-element.18, bf16[1,128]{1,0:T(2,128)(2,1)S(1)} %get-tuple-element.21, ...), dimensions={0} | concatenate | bytes 229376 | tf_op jit(solution)/shard_map/concatenate | solution.py:292
  19.5 2.3 %collective-permute-start.3 = (bf16[448,128]{1,0:T(8,128)(2,1)S(1)}, bf16[448,128]{1,0:T(8,128)(2,1)S(1)}, u32[]{:S(2)}, u32[]{:S(2)}) collective-permute-start(bf16[448,128]{1,0:T(8,128)(2,1)S(1)} %concatenate.8.w0), channel_id=1, source_target_pairs={{3,0},{0,1},{1,2},{2,3},{7,4},{4,5},{5,6},{6,7},{11,8},{8,9},{9,10... | collective-permute-start | bytes 344072 | tf_op jit(solution)/shard_map/ppermute | solution.py:300
  21.9 3.3 %collective-permute-start.2 = (bf16[448,128]{1,0:T(8,128)(2,1)S(1)}, bf16[448,128]{1,0:T(8,128)(2,1)S(1)}, u32[]{:S(2)}, u32[]{:S(2)}) collective-permute-start(bf16[448,128]{1,0:T(8,128)(2,1)S(1)} %concatenate.8.w0), channel_id=1, source_target_pairs={{2,0},{3,1},{0,2},{1,3},{6,4},{7,5},{4,6},{5,7},{10,8},{11,9},{8,1... | collective-permute-start | bytes 344072 | tf_op jit(solution)/shard_map/ppermute | solution.py:300
  25.1 3.3 %collective-permute-start.1 = (bf16[448,128]{1,0:T(8,128)(2,1)S(1)}, bf16[448,128]{1,0:T(8,128)(2,1)S(1)}, u32[]{:S(2)}, u32[]{:S(2)}) collective-permute-start(bf16[448,128]{1,0:T(8,128)(2,1)S(1)} %concatenate.8.w0), channel_id=1, source_target_pairs={{1,0},{2,1},{3,2},{0,3},{5,4},{6,5},{7,6},{4,7},{9,8},{10,9},{11,1... | collective-permute-start | bytes 344072 | tf_op jit(solution)/shard_map/ppermute | solution.py:300
  28.4 0.1 pad_add_fusion.pos_ref
  28.5 1.9 %collective-permute-done.3.w3 = bf16[448,128]{1,0:T(8,128)(2,1)S(1)} collective-permute-done((bf16[448,128]{1,0:T(8,128)(2,1)S(1)}, bf16[448,128]{1,0:T(8,128)(2,1)S(1)}, u32[]{:S(2)}, u32[]{:S(2)}) %collective-permute-start.3) | collective-permute-done | bytes 114720 | tf_op jit(solution)/shard_map/ppermute | solution.py:300
  30.4 7.8 %collective-permute-done.2.w2 = bf16[448,128]{1,0:T(8,128)(2,1)S(1)} collective-permute-done((bf16[448,128]{1,0:T(8,128)(2,1)S(1)}, bf16[448,128]{1,0:T(8,128)(2,1)S(1)}, u32[]{:S(2)}, u32[]{:S(2)}) %collective-permute-start.2) | collective-permute-done | bytes 114720 | tf_op jit(solution)/shard_map/ppermute | solution.py:300
  38.3 0.0 collective-permute-done.1.w1
  38.3 0.0 all-to-all-done.g_ref
  38.3 5.3 %shard_map.73 = (bf16[864,1408]{1,0:T(8,128)(2,1)S(1)}, bf16[4,448,128]{2,1,0:T(8,128)(2,1)S(1)}, f32[16,2,512]{2,1,0:T(2,128)S(1)}) custom-call(s32[4]{0:T(128)S(1)} %pad_add_fusion.pos_ref, bf16[16,32,255]{2,1,0:T(8,128)(2,1)S(1)} %all-to-all-done.g_ref, bf16[448,128]{1,0:T(8,128)(2,1)S(1)} %concatenate.8.w0, ...), custom_call_target="tpu_custom_call" | custom-call | tf_op jit(solution)/shard_map/pallas_call | solution.py:245
  43.6 0.0 copy-start
  43.7 0.0 copy-start.1
  43.7 11.6 %all_to_all.15.st_ref = f32[16,2,512]{2,1,0:T(2,128)S(1)} all-to-all(f32[16,2,512]{2,1,0:T(2,128)S(1)} %get-tuple-element.12), channel_id=1, replica_groups=mesh['frm'=4,'row'=16,'ch'=4] {'row'}, dimensions={0} | all-to-all | bytes 131072 | tf_op jit(solution)/shard_map/all_to_all | solution.py:304
  55.2 10.9 %shard_map.74 = (f32[1056,128]{1,0:T(8,128)S(1)}, f32[64,2,128]{2,1,0:T(2,128)S(1)}) custom-call(s32[4]{0:T(128)S(1)} %pad_add_fusion.pos_ref, bf16[864,1408]{1,0:T(8,128)(2,1)S(1)} %get-tuple-element.10.pt_ref, bf16[4,448,128]{2,1,0:T(8,128)(2,1)S(1)} %get-tuple-element.11.wall_ref, f32[16,2,512]{2,1,0:T(2,128)S(1)} %all_to_all.15.st_ref, ...), custom_call_target="tpu_custom_call" | custom-call | tf_op jit(solution)/shard_map/pallas_call | solution.py:260
  66.2 15.9 %all_to_all.16.st_ref = f32[64,2,128]{2,1,0:T(2,128)S(1)} all-to-all(f32[64,2,128]{2,1,0:T(2,128)S(1)} %get-tuple-element.14), channel_id=1, replica_groups=mesh['frm'=4,'row'=16,'ch'=4] {'frm','row'}, dimensions={0} | all-to-all | bytes 131072 | tf_op jit(solution)/shard_map/all_to_all | solution.py:306
  82.1 0.0 copy-done
  82.1 0.0 copy-done.1
  82.1 1.3 %shard_map.75 = bf16[1,6,170,128]{3,2,1,0:T(8,128)(2,1)} custom-call(f32[1056,128]{1,0:T(8,128)S(1)} %get-tuple-element.13.mix_ref, f32[64,2,128]{2,1,0:T(2,128)S(1)} %all_to_all.16.st_ref, f32[1,128]{1,0:T(1,128)S(1)} %bitcast.20, f32[1,128]{1,0:T(1,128)S(1)} %bitcast.21), custom_call_target="tpu_custom_call" | custom-call | tf_op jit(solution)/shard_map/pallas_call | solution.py:276
  (1 shorter events, 0.0 us)
Async XLA Ops:
  0.0 6.2 %collective-permute-start = (bf16[16,255]{1,0:T(8,128)(2,1)}, bf16[16,255]{1,0:T(8,128)(2,1)S(1)}, u32[]{:S(2)}, u32[]{:S(2)}) collective-permute-start(bf16[16,255]{1,0:T(8,128)(2,1)} %bitcast.23), channel_id=1, source_target_pairs={{4,0},{5,1},{8,4},{9,5},{12,8},{13,9},{16,12},{17,13},{20,16},{21,... | collective-permute-start | bytes 24488 | tf_op jit(solution)/shard_map/ppermute | solution.py:291
  7.6 30.7 %all-to-all-start = ((bf16[16,32,255]{2,1,0:T(8,128)(2,1)}), bf16[16,32,255]{2,1,0:T(8,128)(2,1)S(1)}, u32[]{:S(2)}, u32[]{:S(2)}) async-start(bf16[16,32,255]{2,1,0:T(8,128)(2,1)} %broadcast_in_dim.4), calls=%async_computation | async-start | bytes 524288 | tf_op jit(solution)/shard_map/all_to_all | solution.py:302
  19.5 10.9 %collective-permute-start.3 = (bf16[448,128]{1,0:T(8,128)(2,1)S(1)}, bf16[448,128]{1,0:T(8,128)(2,1)S(1)}, u32[]{:S(2)}, u32[]{:S(2)}) collective-permute-start(bf16[448,128]{1,0:T(8,128)(2,1)S(1)} %concatenate.8.w0), channel_id=1, source_target_pairs={{3,0},{0,1},{1,2},{2,3},{7,4},{4,5},{5,6},{6,7},{11,8},{8,9},{9,10... | collective-permute-start | bytes 344072 | tf_op jit(solution)/shard_map/ppermute | solution.py:300
  21.9 16.4 %collective-permute-start.2 = (bf16[448,128]{1,0:T(8,128)(2,1)S(1)}, bf16[448,128]{1,0:T(8,128)(2,1)S(1)}, u32[]{:S(2)}, u32[]{:S(2)}) collective-permute-start(bf16[448,128]{1,0:T(8,128)(2,1)S(1)} %concatenate.8.w0), channel_id=1, source_target_pairs={{2,0},{3,1},{0,2},{1,3},{6,4},{7,5},{4,6},{5,7},{10,8},{11,9},{8,1... | collective-permute-start | bytes 344072 | tf_op jit(solution)/shard_map/ppermute | solution.py:300
  25.1 13.1 %collective-permute-start.1 = (bf16[448,128]{1,0:T(8,128)(2,1)S(1)}, bf16[448,128]{1,0:T(8,128)(2,1)S(1)}, u32[]{:S(2)}, u32[]{:S(2)}) collective-permute-start(bf16[448,128]{1,0:T(8,128)(2,1)S(1)} %concatenate.8.w0), channel_id=1, source_target_pairs={{1,0},{2,1},{3,2},{0,3},{5,4},{6,5},{7,6},{4,7},{9,8},{10,9},{11,1... | collective-permute-start | bytes 344072 | tf_op jit(solution)/shard_map/ppermute | solution.py:300
  43.6 38.5 %copy-start = (f32[128]{0:T(128)S(1)}, f32[128]{0:T(128)}, u32[]{:S(2)}) copy-start(f32[128]{0:T(128)} %param.12) | copy-start | bytes 1540
  43.7 38.5 %copy-start.1 = (f32[128]{0:T(128)S(1)}, f32[128]{0:T(128)}, u32[]{:S(2)}) copy-start(f32[128]{0:T(128)} %param.13) | copy-start | bytes 1540

commit v2 on v1

v2 whole, which is shorter than its diff:
```python
import jax
import jax.numpy as jnp
from jax import lax
from jax.experimental import pallas as pl
from jax.experimental.pallas import tpu as pltpu
from jax.sharding import PartitionSpec as P

CH = 512
GROUP = 16
W = 170
ROWS = 6
C_LAT = 16
FRAMES = 4
EPSILON = 1e-06

STRIDE = 176
SPAN = 8 * STRIDE
OWN = ROWS * STRIDE
TAPS = 9 * C_LAT
LEAD = 128
XLANES = 2048
K1_CHUNKS = ((128, 384), (512, 384), (896, 384))
CHUNKS = ((0, 384), (384, 384), (768, 384), (1152, 256))
CELLS = ROWS * W
TAPROWS = 27 * C_LAT
HELD = 448
PIECE = 64
PIECES = tuple(i * 24 // 7 * 16 for i in range(8))
VMEM = 48 * 1024 * 1024


def silu_of_twice(half):
    return half + half * jnp.tanh(half)


def group_mean(v):
    r = lax.broadcasted_iota(jnp.int32, (128, 128), 0) // GROUP
    c = lax.broadcasted_iota(jnp.int32, (128, 128), 1) // GROUP
    same = jnp.where(r == c, 1.0 / GROUP, 0.0).astype(jnp.bfloat16)
    high = v.astype(jnp.bfloat16).astype(jnp.float32)
    mid = (v - high).astype(jnp.bfloat16).astype(jnp.float32)
    low = v - high - mid
    y = jnp.dot(
        jnp.concatenate([high, mid, low], axis=0).astype(jnp.bfloat16),
        same,
        preferred_element_type=jnp.float32,
    )
    return y[0:8] + y[8:16] + y[16:24]


def eight(v):
    return jnp.concatenate([v, jnp.zeros((8 - v.shape[0], 128), jnp.float32)], axis=0)


def group_moments(mean, var):
    mean_g = group_mean(mean)
    off = mean - mean_g
    return mean_g, group_mean(var + off * off)


def parts3(v):
    high = v.astype(jnp.bfloat16).astype(jnp.float32)
    mid = (v - high).astype(jnp.bfloat16).astype(jnp.float32)
    return [high, mid, v - high - mid]


def piece_start(core, f):
    low, high = PIECES[3], PIECES[7]
    for i in (2, 1, 0):
        low, high = jnp.where(f == i, PIECES[i], low), jnp.where(f == i, PIECES[4 + i], high)
    return pl.multiple_of(jnp.where(core == 0, low, high), 16)


def k0(tokens_hbm, w_hbm, p0, p1, p2, p3, out_ref, par_ref, tokens_ref, held_ref, in_ref, sems):
    copies = [
        pltpu.make_async_copy(tokens_hbm, tokens_ref, sems.at[0]),
        pltpu.make_async_copy(w_hbm, held_ref.at[:TAPROWS], sems.at[1]),
        pltpu.make_async_copy(p0, in_ref.at[0], sems.at[2]),
        pltpu.make_async_copy(p1, in_ref.at[1], sems.at[3]),
        pltpu.make_async_copy(p2, par_ref.at[0], sems.at[4]),
        pltpu.make_async_copy(p3, par_ref.at[1], sems.at[5]),
    ]
    for copy in copies:
        copy.start()
    for copy in copies:
        copy.wait()
    rows = parts3(in_ref[0]) + parts3(in_ref[1]) + [jnp.zeros((10, 128), jnp.float32)]
    held_ref[TAPROWS:, :] = jnp.concatenate(rows, axis=0).astype(jnp.bfloat16)
    start = piece_start(lax.rem(lax.axis_index("row"), 2), lax.axis_index("frm"))
    piece = jnp.concatenate([held_ref[pl.ds(start, 32), :], held_ref[pl.ds(start + 32, 32), :]], axis=1)
    out_ref[:, :C_LAT, :255] = jnp.broadcast_to(tokens_ref[...][None], (16, C_LAT, 255))
    out_ref[:, C_LAT:, :] = jnp.broadcast_to(piece[None], (16, PIECE // 2, 256))


def k1a(g_ref, up_ref, down_ref, mine_ref):
    for f in range(FRAMES):
        at = slice(16 * f, 16 * f + 16)

        def src(j, lo, hi):
            return g_ref[4 * f + j, :C_LAT, lo:hi]

        up_ref[at, 0:170] = src(0, 0, 170)
        up_ref[at, 176:261] = src(0, 170, 255)
        up_ref[at, 261:346] = src(1, 0, 85)
        down_ref[at, 0:85] = src(2, 170, 255)
        down_ref[at, 85:170] = src(3, 0, 85)
        down_ref[at, 176:346] = src(3, 85, 255)
    for i in range(16):
        mine_ref[i, :32] = g_ref[i, C_LAT:, :128]
        mine_ref[i, 32:] = g_ref[i, C_LAT:, 128:]


def k1(g_ref, above_ref, below_ref, mine_ref, other_ref, pt_ref, wall_ref, st_ref, x_ref):
    core = lax.rem(lax.axis_index("row"), 2)
    for i in range(FRAMES):
        mine, other = piece_start(core, i), piece_start(1 - core, i)
        for j in range(4):
            wall_ref[j, pl.ds(mine, PIECE), :] = mine_ref[4 * i + j]
            wall_ref[j, pl.ds(other, PIECE), :] = other_ref[4 * i + j]
    weight = jnp.concatenate([wall_ref[j, :TAPROWS, :] for j in range(4)], axis=1)
    x_ref[...] = jnp.zeros_like(x_ref)
    pt_ref[: 2 * TAPS, :] = jnp.zeros((2 * TAPS, SPAN), jnp.bfloat16)

    plan = (
        ((0, 0, 170),),
        ((0, 170, 255), (1, 0, 85)),
        ((1, 85, 255),),
        ((2, 0, 170),),
        ((2, 170, 255), (3, 0, 85)),
        ((3, 85, 255),),
    )
    for f in range(FRAMES):
        at = slice(16 * f, 16 * f + 16)
        for row, parts in enumerate(plan):
            lane = LEAD + STRIDE * (row + 2)
            for j, lo, hi in parts:
                x_ref[at, lane : lane + hi - lo] = g_ref[4 * f + j, :C_LAT, lo:hi]
                lane += hi - lo
        for row in range(2):
            lane = LEAD + STRIDE * row
            x_ref[at, lane : lane + W] = above_ref[at, STRIDE * row : STRIDE * row + W]
            lane = LEAD + STRIDE * (row + 8)
            x_ref[at, lane : lane + W] = below_ref[at, STRIDE * row : STRIDE * row + W]
    for f in range(FRAMES):
        for b in range(3):
            for e in range(3):
                at = (f + 2) * TAPS + (3 * b + e) * 16
                lane = LEAD + STRIDE * b + e - 1
                pt_ref[at : at + 16, :] = x_ref[16 * f : 16 * f + 16, lane : lane + SPAN]

    def hidden(g, lo, size):
        return lax.dot_general(
            pt_ref[g * TAPS : (g + 3) * TAPS, lo : lo + size],
            weight,
            (((0,), (0,)), ((), ())),
            preferred_element_type=jnp.float32,
        )

    def valid(lo, size):
        at = lo + lax.broadcasted_iota(jnp.int32, (size, 128), 0)
        ok = (at >= STRIDE) & (at < STRIDE + OWN)
        for row in range(1, 7):
            gap = STRIDE * row + W
            if lo < gap + STRIDE - W and gap < lo + size:
                ok = ok & ((at < gap) | (at >= gap + STRIDE - W))
        return jnp.concatenate([ok] * 4, axis=1)

    pilot = jnp.sum(jnp.where(valid(256, 128), hidden(0, 256, 128), 0.0), axis=0, keepdims=True) * (1.0 / 122)
    s1 = s2 = jnp.zeros((8, CH), jnp.float32)
    for g in range(FRAMES):
        for lo, size in K1_CHUNKS:
            d = jnp.where(valid(lo, size), hidden(g, lo, size) - pilot, 0.0)
            d = d.reshape(size // 8, 8, CH)
            s1 = s1 + jnp.sum(d, axis=0)
            s2 = s2 + jnp.sum(d * d, axis=0)
    n = FRAMES * CELLS
    s1 = jnp.sum(s1, axis=0, keepdims=True)
    s2 = jnp.sum(s2, axis=0, keepdims=True)
    d = s1 / n
    for i, v in enumerate((pilot + d, s2 - s1 * d)):
        for j in range(4):
            part = v[:, 128 * j : 128 * (j + 1)]
            st_ref[:, 4 * i + j : 4 * i + j + 1, :] = jnp.broadcast_to(part[None], (16, 1, 128))


def k2(pt_ref, wall_ref, st_ref, w2_hbm, mix_ref, so_ref, a_ref, w2_ref, y_ref, sem):
    copy = pltpu.make_async_copy(w2_hbm, w2_ref, sem)
    copy.start()
    f, r = lax.axis_index("frm"), lax.axis_index("row")
    weight = jnp.concatenate([wall_ref[j, :TAPROWS, :] for j in range(4)], axis=1)

    def spread3(at):
        rows = [wall_ref[j, TAPROWS:, :].astype(jnp.float32)[at : at + 3] for j in range(4)]
        return jnp.concatenate([jnp.sum(r, axis=0, keepdims=True) for r in rows], axis=1)

    n = FRAMES * CELLS
    st = st_ref[...]
    sums = jnp.sum(st, axis=0)
    means = sums[:4] * (1.0 / 16)
    off = st[:, :4, :] - means[None]
    spread = jnp.sum(off * off, axis=0)
    mean, var = group_moments(eight(means), eight((sums[4:] * (1.0 / n) + spread) * (1.0 / 16)))
    inverse = lax.rsqrt(var + EPSILON)

    def wide(v):
        return jnp.concatenate([v[j : j + 1] for j in range(4)], axis=1)

    mean, scale, shift = wide(mean), 0.5 * wide(inverse) * spread3(0), 0.5 * spread3(3)

    a_ref[0:16, :] = jnp.zeros((16, 3 * CH), jnp.bfloat16)
    a_ref[16 + SPAN :, :] = jnp.zeros((16, 3 * CH), jnp.bfloat16)
    for k in range(3):
        g = f - 2 + k

        @pl.when(g >= 0)
        def _():
            at = pl.multiple_of(g * TAPS, 16)
            for lo, size in CHUNKS:
                h = lax.dot_general(
                    pt_ref[pl.ds(at, 3 * TAPS), lo : lo + size],
                    weight,
                    (((0,), (0,)), ((), ())),
                    preferred_element_type=jnp.float32,
                )
                u = silu_of_twice((h - mean) * scale + shift)
                a_ref[16 + lo : 16 + lo + size, k * CH : (k + 1) * CH] = u.astype(jnp.bfloat16)

        @pl.when(g < 0)
        def _():
            a_ref[16 : 16 + SPAN, k * CH : (k + 1) * CH] = jnp.zeros((SPAN, CH), jnp.bfloat16)

    keep = lax.broadcasted_iota(jnp.int32, (16, 3 * CH), 0) < 10
    for row in range(8):
        at = 16 + STRIDE * row + 160
        a_ref[at : at + 16, :] = jnp.where(keep, a_ref[at : at + 16, :], 0).astype(jnp.bfloat16)

    @pl.when(r == 0)
    def _():
        a_ref[16 : 16 + STRIDE, :] = jnp.zeros((STRIDE, 3 * CH), jnp.bfloat16)

    @pl.when(r == 15)
    def _():
        a_ref[16 + 7 * STRIDE : 16 + SPAN, :] = jnp.zeros((STRIDE, 3 * CH), jnp.bfloat16)

    copy.wait()

    def product(start, rows, *taps):
        kernel = jnp.concatenate(
            [jnp.concatenate([w2_ref[9 * a + 3 * b + e] for a in range(3)], axis=0) for b, e in taps], axis=1
        )
        y_ref[:rows, : 128 * len(taps)] = jnp.dot(
            a_ref[start : start + rows, :], kernel, preferred_element_type=jnp.float32
        )

    for b in range(3):
        product(STRIDE * b, OWN + 32, (b, 0), (b, 2))
        part = y_ref[15 : 15 + OWN, :128] + y_ref[17 : 17 + OWN, 128:]
        mix_ref[...] = part if b == 0 else mix_ref[...] + part
    product(16, SPAN, (0, 1), (2, 1))
    mix_ref[...] += y_ref[0:OWN, :128] + y_ref[2 * STRIDE : 2 * STRIDE + OWN, 128:]
    product(16 + STRIDE, OWN, (1, 1))
    v = (mix_ref[...] + y_ref[0:OWN, :128]).reshape(ROWS, STRIDE, 128)
    mix_ref[...] = v.reshape(OWN, 128)
    ok = lax.broadcasted_iota(jnp.int32, (ROWS, STRIDE, 128), 1) < W
    total = jnp.sum(jnp.sum(jnp.where(ok, v, 0.0), axis=0), axis=0, keepdims=True)
    centre = total / CELLS
    off = jnp.where(ok, v - centre[None], 0.0)
    squares = jnp.sum(jnp.sum(off * off, axis=0), axis=0, keepdims=True)
    so_ref[:, 0:1, :] = jnp.broadcast_to(centre[None], (64, 1, 128))
    so_ref[:, 1:2, :] = jnp.broadcast_to(squares[None], (64, 1, 128))


def k3(mix_ref, st_ref, par_ref, out_ref):
    st = st_ref[...]
    sums = jnp.sum(st, axis=0)
    means = sums * (1.0 / 64)
    off = st - means[None]
    spread = jnp.sum(off * off, axis=0)
    var = (sums[1:2] * (1.0 / CELLS) + spread[0:1]) * (1.0 / 64)
    mean, var = group_moments(eight(means[0:1]), eight(var))
    mean = mean[:1]
    scale = 0.5 * lax.rsqrt(var[:1] + EPSILON) * par_ref[0]
    shift = 0.5 * par_ref[1]
    for row in range(ROWS):
        v = mix_ref[STRIDE * row : STRIDE * (row + 1), :]
        u = silu_of_twice((v - mean) * scale + shift)
        out_ref[0, row] = u[:W].astype(jnp.bfloat16)


def shape(dims, kind):
    return jax.ShapeDtypeStruct(dims, kind)


INHBM = pl.BlockSpec(memory_space=pltpu.HBM)
INVMEM = pl.BlockSpec(memory_space=pltpu.VMEM)


def call_k0(*arrays):
    return pl.pallas_call(
        k0,
        out_shape=(
            shape((16, C_LAT + PIECE // 2, 256), jnp.bfloat16),
            shape((2, 1, 128), jnp.float32),
        ),
        in_specs=[INHBM] * 6,
        out_specs=(INVMEM,) * 2,
        scratch_shapes=[
            pltpu.VMEM((C_LAT, 255), jnp.bfloat16),
            pltpu.VMEM((HELD, 128), jnp.bfloat16),
            pltpu.VMEM((2, 1, 128), jnp.float32),
            pltpu.SemaphoreType.DMA((6,)),
        ],
        compiler_params=pltpu.CompilerParams(vmem_limit_bytes=VMEM),
        name="k0",
    )(*[pltpu.with_memory_space_constraint(v, pltpu.HBM) for v in arrays])


def call_k1a(g):
    return pl.pallas_call(
        k1a,
        out_shape=(
            shape((16 * FRAMES, 2 * STRIDE), jnp.bfloat16),
            shape((16 * FRAMES, 2 * STRIDE), jnp.bfloat16),
            shape((16, PIECE, 128), jnp.bfloat16),
        ),
        in_specs=[INVMEM],
        out_specs=(INVMEM,) * 3,
        compiler_params=pltpu.CompilerParams(vmem_limit_bytes=VMEM),
        name="k1a",
    )(g)


def call_k1(*arrays):
    return pl.pallas_call(
        k1,
        out_shape=(
            shape((6 * TAPS, SPAN), jnp.bfloat16),
            shape((4, HELD, 128), jnp.bfloat16),
            shape((16, 8, 128), jnp.float32),
        ),
        in_specs=[INVMEM] * 5,
        out_specs=(INVMEM,) * 3,
        scratch_shapes=[pltpu.VMEM((16 * FRAMES, XLANES), jnp.bfloat16)],
        compiler_params=pltpu.CompilerParams(vmem_limit_bytes=VMEM),
        name="k1",
    )(*arrays)


def call_k2(pt, wall, st, w2):
    return pl.pallas_call(
        k2,
        out_shape=(shape((OWN, 128), jnp.float32), shape((64, 2, 128), jnp.float32)),
        in_specs=[INVMEM] * 3 + [INHBM],
        out_specs=(INVMEM,) * 2,
        scratch_shapes=[
            pltpu.VMEM((SPAN + 32, 3 * CH), jnp.bfloat16),
            pltpu.VMEM((27, CH, 128), jnp.bfloat16),
            pltpu.VMEM((SPAN, 256), jnp.float32),
            pltpu.SemaphoreType.DMA,
        ],
        compiler_params=pltpu.CompilerParams(vmem_limit_bytes=VMEM),
        name="k2",
    )(pt, wall, st, pltpu.with_memory_space_constraint(w2, pltpu.HBM))


def call_k3(mix, st, par):
    return pl.pallas_call(
        k3,
        out_shape=shape((1, ROWS, W, 128), jnp.bfloat16),
        in_specs=[INVMEM] * 3,
        out_specs=INVMEM,
        compiler_params=pltpu.CompilerParams(vmem_limit_bytes=VMEM),
        name="k3",
    )(mix, st, par)


def per_device(latents, in_weight, in_gain, in_shift, mid_weight, mid_gain, mid_shift):
    params = [v.reshape(1, 128) for v in (in_gain, in_shift, mid_gain, mid_shift)]
    payload, par = call_k0(latents.T, in_weight.reshape(TAPROWS, 128), *params)
    g = lax.all_to_all(payload, ("frm", "ch"), 0, 0)
    up, down, mine = call_k1a(g)
    below = lax.ppermute(up, "row", [(i + 1, i) for i in range(15)])
    above = lax.ppermute(down, "row", [(i, i + 1) for i in range(15)])
    other = lax.ppermute(mine, "row", [(i, i ^ 1) for i in range(16)])
    pt, wall, st = call_k1(g, above, below, mine, other)
    st = lax.all_to_all(st, "row", 0, 0)
    mix, st = call_k2(pt, wall, st, mid_weight)
    st = lax.all_to_all(st, ("frm", "row"), 0, 0)
    return call_k3(mix, st, par)


def solution(mesh):
    return jax.shard_map(
        per_device,
        mesh=mesh,
        in_specs=(
            P(("frm", "row", "ch"), None),
            P(None, None, "ch"),
            P("ch"),
            P("ch"),
            P(None, None, "ch"),
            P("ch"),
            P("ch"),
        ),
        out_specs=P("frm", "row", None, "ch"),
        check_vma=False,
    )
```

time: 83.8 us -> 75.5 us (0.901)
  blocking collectives: 27.5 us -> 50.5 us
  starting transfers between devices: 24.2 us -> 7.37 us
  waiting for transfers between devices: 10.8 us -> 3.48 us
  Pallas kernels: 17.6 us -> 13.7 us
  local copies, waits for them, and re-layouts: 1.8 us -> 0 us
  other arithmetic: 1.46 us -> 0 us
    all_to_all x0 -> x1, blocking collectives: none -> 26 us  [per_device(): g = lax.all_to_all(payload, ('frm', 'ch'), 0, 0)]
    all_to_all x1 -> x0, starting transfers between devices: 10.2 us -> none  [per_device(): lax.all_to_all(jnp.broadcast_to(payload[None], (16, 32, 255)), ('frm', 'c...]
    ppermute x4 -> x3, waiting for transfers between devices: 10.8 us -> 3.48 us  [the longest x1 3.47 us: per_device(): below = lax.ppermute(up, 'row', [(i + 1, i) for i in range(15)])]
    ppermute x4 -> x3, starting transfers between devices: 14.1 us -> 7.37 us  [the longest x1 3.1 us: per_device(): above = lax.ppermute(down, 'row', [(i, i + 1) for i in range(15)])]
    pallas_call x1, Pallas kernels: 10.9 us -> 7.16 us  [call_k2(): pl.pallas_call(k2, out_shape=(shape((OWN, 128), jnp.float32), shape((64,...]
    all_to_all x1, blocking collectives: 15.9 us -> 13.2 us  [per_device(): st = lax.all_to_all(st, ('frm', 'row'), 0, 0)]
    pallas_call x0 -> x2, Pallas kernels: none -> 1.11 us  [the longest x1 1 us: call_k0(): pl.pallas_call(k0, out_shape=(shape((16, C_LAT + PIECE // 2, 256), jnp.bf...]
    concatenate x1 -> x0, local copies, waits for them, and re-layouts: 1.06 us -> none  [per_device(): jnp.concatenate([in_weight.reshape(27 * C_LAT, 128), pieces3(in_gain), pi...]
  transfers between devices with their start and end apart: 5 -> 3, of which waited for: 3 -> 1; matrix products, arithmetic and copies ran while one was open for 2% -> 0% of each run, Pallas kernels for 0% -> 0%
where the time goes in v2:
time: 75.5 us; the launch traced here: 75.2 us
  blocking collectives  50.5 us (67%)
  Pallas kernels  13.7 us (18%)
  starting transfers between devices  7.37 us (10%)
  waiting for transfers between devices  3.48 us (5%)
    all_to_all x1, blocking collectives, per_device(): g = lax.all_to_all(payload, ('frm', 'ch'), 0, 0)  26 us
    all_to_all x1, blocking collectives, per_device(): st = lax.all_to_all(st, ('frm', 'row'), 0, 0)  13.2 us
    all_to_all x1, blocking collectives, per_device(): st = lax.all_to_all(st, 'row', 0, 0)  11.3 us
    pallas_call x1, Pallas kernels, call_k2(): pl.pallas_call(k2, out_shape=(shape((OWN, 128), jnp.float32), shape((64,...  7.16 us
    pallas_call x1, Pallas kernels, call_k1(): pl.pallas_call(k1, out_shape=(shape((6 * TAPS, SPAN), jnp.bfloat16), shap...  4.29 us
    ppermute x1, waiting for transfers between devices, per_device(): below = lax.ppermute(up, 'row', [(i + 1, i) for i in range(15)])  3.47 us
    ppermute x1, starting transfers between devices, per_device(): above = lax.ppermute(down, 'row', [(i, i + 1) for i in range(15)])  3.1 us
    ppermute x1, starting transfers between devices, per_device(): other = lax.ppermute(mine, 'row', [(i, i ^ 1) for i in range(16)])  2.35 us
  transfers between devices with their start and end apart: 3, of which 1 were waited for; matrix products, arithmetic and copies ran while one was open for 0% of the time, Pallas kernels for 0%

profile of v2, /device:TPU:1, one launch (start us, length us, event | category | flops | bytes accessed | tf_op | source)
XLA Modules:
  0.0 75.2 jit_solution(11057931880022187414)
XLA Ops:
  0.0 1.0 %k0.1 = (bf16[16,48,256]{2,1,0:T(8,128)(2,1)S(1)}, f32[2,1,128]{2,1,0:T(1,128)S(1)}) custom-call(bf16[16,255]{1,0:T(8,128)(2,1)} %bitcast.7, bf16[432,128]{1,0:T(8,128)(2,1)} %bitcast.6, f32[1,128]{1,0:T(1,128)} %bitcast.8, f32[1,128]{1,0:T(1,128)} %bitcast.9, f32[1,128]{1,0:T(1,128)} %bitcast.10, f32[1,128]{1,0:T(1,128)} %bitcast.11), custom_call_target="tpu_custom_call" | custom-call | tf_op jit(solution)/shard_map/k0/pallas_call | solution.py:299
  1.0 26.0 %all_to_all.15.g_ref = bf16[16,48,256]{2,1,0:T(8,128)(2,1)S(1)} all-to-all(bf16[16,48,256]{2,1,0:T(8,128)(2,1)S(1)} %get-tuple-element.15), channel_id=1, replica_groups=mesh['frm'=4,'row'=16,'ch'=4] {'frm','ch'}, dimensions={0} | all-to-all | bytes 786432 | tf_op jit(solution)/shard_map/all_to_all | solution.py:380
  27.1 0.1 k1a.1
  27.2 2.4 %collective-permute-start.2 = (bf16[16,64,128]{2,1,0:T(8,128)(2,1)S(1)}, bf16[16,64,128]{2,1,0:T(8,128)(2,1)S(1)}, u32[]{:S(2)}, u32[]{:S(2)}) collective-permute-start(bf16[16,64,128]{2,1,0:T(8,128)(2,1)S(1)} %get-tuple-element.18.mine_ref), channel_id=1, source_target_pairs={{0,4},{4,0},{8,12},{12,8},{16,20},{20,16},{24,28},{28,24},{32,36},... | collective-permute-start | bytes 786440 | tf_op jit(solution)/shard_map/ppermute | solution.py:384
  29.5 3.1 %collective-permute-start = (bf16[64,352]{1,0:T(8,128)(2,1)S(1)}, bf16[64,352]{1,0:T(8,128)(2,1)S(1)}, u32[]{:S(2)}, u32[]{:S(2)}) collective-permute-start(bf16[64,352]{1,0:T(8,128)(2,1)S(1)} %get-tuple-element.16), channel_id=1, source_target_pairs={{0,4},{4,8},{8,12},{12,16},{16,20},{20,24},{24,28},{28,32},{32,36}... | collective-permute-start | bytes 135176 | tf_op jit(solution)/shard_map/ppermute | solution.py:383
  32.6 1.9 %collective-permute-start.1 = (bf16[64,352]{1,0:T(8,128)(2,1)S(1)}, bf16[64,352]{1,0:T(8,128)(2,1)S(1)}, u32[]{:S(2)}, u32[]{:S(2)}) collective-permute-start(bf16[64,352]{1,0:T(8,128)(2,1)S(1)} %get-tuple-element.17), channel_id=1, source_target_pairs={{4,0},{8,4},{12,8},{16,12},{20,16},{24,20},{28,24},{32,28},{36,32}... | collective-permute-start | bytes 135176 | tf_op jit(solution)/shard_map/ppermute | solution.py:382
  34.6 0.0 collective-permute-done.above_ref
  34.6 3.5 %collective-permute-done.1.below_ref = bf16[64,352]{1,0:T(8,128)(2,1)S(1)} collective-permute-done((bf16[64,352]{1,0:T(8,128)(2,1)S(1)}, bf16[64,352]{1,0:T(8,128)(2,1)S(1)}, u32[]{:S(2)}, u32[]{:S(2)}) %collective-permute-start.1) | collective-permute-done | bytes 45088 | tf_op jit(solution)/shard_map/ppermute | solution.py:382
  38.0 0.0 collective-permute-done.2.other_ref
  38.0 4.3 %k1.1 = (bf16[864,1408]{1,0:T(8,128)(2,1)S(1)}, bf16[4,448,128]{2,1,0:T(8,128)(2,1)S(1)}, f32[16,8,128]{2,1,0:T(8,128)S(1)}) custom-call(bf16[16,48,256]{2,1,0:T(8,128)(2,1)S(1)} %all_to_all.15.g_ref, bf16[64,352]{1,0:T(8,128)(2,1)S(1)} %collective-permute-done.above_ref, bf16[64,352]{1,0:T(8,128)(2,1)S(1)} %collective-permute-done.1.below_ref, ...), custom_call_target="tpu_custom_call" | custom-call | tf_op jit(solution)/shard_map/k1/pallas_call | solution.py:334
  42.3 11.3 %all_to_all.16.st_ref = f32[16,8,128]{2,1,0:T(8,128)S(1)} all-to-all(f32[16,8,128]{2,1,0:T(8,128)S(1)} %get-tuple-element.21), channel_id=1, replica_groups=mesh['frm'=4,'row'=16,'ch'=4] {'row'}, dimensions={0} | all-to-all | bytes 131072 | tf_op jit(solution)/shard_map/all_to_all | solution.py:386
  53.7 7.2 %k2.1 = (f32[1056,128]{1,0:T(8,128)S(1)}, f32[64,2,128]{2,1,0:T(2,128)S(1)}) custom-call(bf16[864,1408]{1,0:T(8,128)(2,1)S(1)} %get-tuple-element.19.pt_ref, bf16[4,448,128]{2,1,0:T(8,128)(2,1)S(1)} %get-tuple-element.20.wall_ref, f32[16,8,128]{2,1,0:T(8,128)S(1)} %all_to_all.16.st_ref, bf16[27,512,128]{2,1,0:T(8,128)(2,1)} %w2_hbm.1), custom_call_target="tpu_custom_call" | custom-call | tf_op jit(solution)/shard_map/k2/pallas_call | solution.py:350
  60.8 13.2 %all_to_all.17.st_ref = f32[64,2,128]{2,1,0:T(2,128)S(1)} all-to-all(f32[64,2,128]{2,1,0:T(2,128)S(1)} %get-tuple-element.23), channel_id=1, replica_groups=mesh['frm'=4,'row'=16,'ch'=4] {'frm','row'}, dimensions={0} | all-to-all | bytes 131072 | tf_op jit(solution)/shard_map/all_to_all | solution.py:388
  74.0 1.2 %k3.1 = bf16[1,6,170,128]{3,2,1,0:T(8,128)(2,1)} custom-call(f32[1056,128]{1,0:T(8,128)S(1)} %get-tuple-element.22.mix_ref, f32[64,2,128]{2,1,0:T(2,128)S(1)} %all_to_all.17.st_ref, f32[2,1,128]{2,1,0:T(1,128)S(1)} %get-tuple-element.24.par_ref), custom_call_target="tpu_custom_call" | custom-call | tf_op jit(solution)/shard_map/k3/pallas_call | solution.py:367
Async XLA Ops:
  27.2 10.9 %collective-permute-start.2 = (bf16[16,64,128]{2,1,0:T(8,128)(2,1)S(1)}, bf16[16,64,128]{2,1,0:T(8,128)(2,1)S(1)}, u32[]{:S(2)}, u32[]{:S(2)}) collective-permute-start(bf16[16,64,128]{2,1,0:T(8,128)(2,1)S(1)} %get-tuple-element.18.mine_ref), channel_id=1, source_target_pairs={{0,4},{4,0},{8,12},{12,8},{16,20},{20,16},{24,28},{28,24},{32,36},... | collective-permute-start | bytes 786440 | tf_op jit(solution)/shard_map/ppermute | solution.py:384
  29.5 5.0 %collective-permute-start = (bf16[64,352]{1,0:T(8,128)(2,1)S(1)}, bf16[64,352]{1,0:T(8,128)(2,1)S(1)}, u32[]{:S(2)}, u32[]{:S(2)}) collective-permute-start(bf16[64,352]{1,0:T(8,128)(2,1)S(1)} %get-tuple-element.16), channel_id=1, source_target_pairs={{0,4},{4,8},{8,12},{12,16},{16,20},{20,24},{24,28},{28,32},{32,36}... | collective-permute-start | bytes 135176 | tf_op jit(solution)/shard_map/ppermute | solution.py:383
  32.6 5.4 %collective-permute-start.1 = (bf16[64,352]{1,0:T(8,128)(2,1)S(1)}, bf16[64,352]{1,0:T(8,128)(2,1)S(1)}, u32[]{:S(2)}, u32[]{:S(2)}) collective-permute-start(bf16[64,352]{1,0:T(8,128)(2,1)S(1)} %get-tuple-element.17), channel_id=1, source_target_pairs={{4,0},{8,4},{12,8},{16,12},{20,16},{24,20},{28,24},{32,28},{36,32}... | collective-permute-start | bytes 135176 | tf_op jit(solution)/shard_map/ppermute | solution.py:382

commit v3 on v2

--- a/solution.py
+++ b/solution.py
@@ -92,31 +92,48 @@
     out_ref[:, C_LAT:, :] = jnp.broadcast_to(piece[None], (16, PIECE // 2, 256))
 
 
-def k1a(g_ref, up_ref, down_ref, mine_ref):
+def k1a(g_ref, mate_ref, next_ref, first_ref, last_ref):
+    first_ref[...] = jnp.zeros_like(first_ref)
+    last_ref[...] = jnp.zeros_like(last_ref)
     for f in range(FRAMES):
         at = slice(16 * f, 16 * f + 16)
 
         def src(j, lo, hi):
             return g_ref[4 * f + j, :C_LAT, lo:hi]
 
-        up_ref[at, 0:170] = src(0, 0, 170)
-        up_ref[at, 176:261] = src(0, 170, 255)
-        up_ref[at, 261:346] = src(1, 0, 85)
-        down_ref[at, 0:85] = src(2, 170, 255)
-        down_ref[at, 85:170] = src(3, 0, 85)
-        down_ref[at, 176:346] = src(3, 85, 255)
+        first_ref[at, 0:170] = src(0, 0, 170)
+        first_ref[at, 176:261] = src(0, 170, 255)
+        first_ref[at, 261:346] = src(1, 0, 85)
+        last_ref[at, 0:85] = src(2, 170, 255)
+        last_ref[at, 85:170] = src(3, 0, 85)
+        last_ref[at, 176:346] = src(3, 85, 255)
     for i in range(16):
-        mine_ref[i, :32] = g_ref[i, C_LAT:, :128]
-        mine_ref[i, 32:] = g_ref[i, C_LAT:, 128:]
-
-
-def k1(g_ref, above_ref, below_ref, mine_ref, other_ref, pt_ref, wall_ref, st_ref, x_ref):
+        mate_ref[PIECE * i : PIECE * i + 32] = g_ref[i, C_LAT:, :128]
+        mate_ref[PIECE * i + 32 : PIECE * (i + 1)] = g_ref[i, C_LAT:, 128:]
+
+    def send(to_mate, to_next):
+        for i in range(3):
+            mate_ref[16 * PIECE + 64 * i : 16 * PIECE + 64 * (i + 1)] = to_mate[:, 128 * i : 128 * (i + 1)]
+        next_ref[...] = to_next[...]
+
+    core = lax.rem(lax.axis_index("row"), 2)
+
+    @pl.when(core == 0)
+    def _():
+        send(last_ref, first_ref)
+
+    @pl.when(core == 1)
+    def _():
+        send(first_ref, last_ref)
+
+
+def k1(g_ref, mine_ref, other_ref, next_ref, pt_ref, wall_ref, st_ref, x_ref):
     core = lax.rem(lax.axis_index("row"), 2)
     for i in range(FRAMES):
         mine, other = piece_start(core, i), piece_start(1 - core, i)
         for j in range(4):
-            wall_ref[j, pl.ds(mine, PIECE), :] = mine_ref[4 * i + j]
-            wall_ref[j, pl.ds(other, PIECE), :] = other_ref[4 * i + j]
+            wall_ref[j, pl.ds(mine, PIECE), :] = mine_ref[PIECE * (4 * i + j) : PIECE * (4 * i + j + 1)]
+            wall_ref[j, pl.ds(other, PIECE), :] = other_ref[PIECE * (4 * i + j) : PIECE * (4 * i + j + 1)]
     weight = jnp.concatenate([wall_ref[j, :TAPROWS, :] for j in range(4)], axis=1)
     x_ref[...] = jnp.zeros_like(x_ref)
     pt_ref[: 2 * TAPS, :] = jnp.zeros((2 * TAPS, SPAN), jnp.bfloat16)
@@ -136,11 +153,29 @@
             for j, lo, hi in parts:
                 x_ref[at, lane : lane + hi - lo] = g_ref[4 * f + j, :C_LAT, lo:hi]
                 lane += hi - lo
-        for row in range(2):
-            lane = LEAD + STRIDE * row
-            x_ref[at, lane : lane + W] = above_ref[at, STRIDE * row : STRIDE * row + W]
-            lane = LEAD + STRIDE * (row + 8)
-            x_ref[at, lane : lane + W] = below_ref[at, STRIDE * row : STRIDE * row + W]
+
+    def edges(above, below):
+        for f in range(FRAMES):
+            at = slice(16 * f, 16 * f + 16)
+            for v, row in ((above, 0), (below, 8)):
+                lane = LEAD + STRIDE * row
+                x_ref[at, lane : lane + 2 * STRIDE] = v(at)
+
+    def from_mate(at):
+        parts = [other_ref[16 * PIECE + 64 * i :][at] for i in range(3)]
+        return jnp.concatenate(parts, axis=1)[:, : 2 * STRIDE]
+
+    def from_next(at):
+        return next_ref[at, : 2 * STRIDE]
+
+    @pl.when(core == 0)
+    def _():
+        edges(from_next, from_mate)
+
+    @pl.when(core == 1)
+    def _():
+        edges(from_mate, from_next)
+
     for f in range(FRAMES):
         for b in range(3):
             for e in range(3):
@@ -316,15 +351,16 @@
 
 
 def call_k1a(g):
+    edge = (16 * FRAMES, 384)
     return pl.pallas_call(
         k1a,
         out_shape=(
-            shape((16 * FRAMES, 2 * STRIDE), jnp.bfloat16),
-            shape((16 * FRAMES, 2 * STRIDE), jnp.bfloat16),
-            shape((16, PIECE, 128), jnp.bfloat16),
+            shape((16 * PIECE + 3 * 64, 128), jnp.bfloat16),
+            shape(edge, jnp.bfloat16),
         ),
         in_specs=[INVMEM],
-        out_specs=(INVMEM,) * 3,
+        out_specs=(INVMEM,) * 2,
+        scratch_shapes=[pltpu.VMEM(edge, jnp.bfloat16)] * 2,
         compiler_params=pltpu.CompilerParams(vmem_limit_bytes=VMEM),
         name="k1a",
     )(g)
@@ -338,7 +374,7 @@
             shape((4, HELD, 128), jnp.bfloat16),
             shape((16, 8, 128), jnp.float32),
         ),
-        in_specs=[INVMEM] * 5,
+        in_specs=[INVMEM] * 4,
         out_specs=(INVMEM,) * 3,
         scratch_shapes=[pltpu.VMEM((16 * FRAMES, XLANES), jnp.bfloat16)],
         compiler_params=pltpu.CompilerParams(vmem_limit_bytes=VMEM),
@@ -378,11 +414,10 @@
     params = [v.reshape(1, 128) for v in (in_gain, in_shift, mid_gain, mid_shift)]
     payload, par = call_k0(latents.T, in_weight.reshape(TAPROWS, 128), *params)
     g = lax.all_to_all(payload, ("frm", "ch"), 0, 0)
-    up, down, mine = call_k1a(g)
-    below = lax.ppermute(up, "row", [(i + 1, i) for i in range(15)])
-    above = lax.ppermute(down, "row", [(i, i + 1) for i in range(15)])
+    mine, edge = call_k1a(g)
     other = lax.ppermute(mine, "row", [(i, i ^ 1) for i in range(16)])
-    pt, wall, st = call_k1(g, above, below, mine, other)
+    edge = lax.ppermute(edge, "row", [(i, i + 2 * (i % 2) - 1) for i in range(1, 15)])
+    pt, wall, st = call_k1(g, mine, other, edge)
     st = lax.all_to_all(st, "row", 0, 0)
     mix, st = call_k2(pt, wall, st, mid_weight)
     st = lax.all_to_all(st, ("frm", "row"), 0, 0)

time: 75.5 us -> 72.4 us (0.959)
  starting transfers between devices: 7.37 us -> 5.46 us
  waiting for transfers between devices: 3.48 us -> 2.29 us
  blocking collectives: 50.5 us -> 51.4 us
    ppermute x2 -> x1, starting transfers between devices: 5.02 us -> 3.1 us  [per_device(): lax.ppermute(edge, 'row', [(i, i + 2 * (i % 2) - 1) for i in range(1, 15)])]
    ppermute x2 -> x1, waiting for transfers between devices: 3.47 us -> 2.29 us  [per_device(): lax.ppermute(edge, 'row', [(i, i + 2 * (i % 2) - 1) for i in range(1, 15)])]
    all_to_all x1, blocking collectives: 11.3 us -> 12.1 us  [per_device(): st = lax.all_to_all(st, 'row', 0, 0)]
  transfers between devices with their start and end apart: 3 -> 2, of which waited for: 1 -> 1; matrix products, arithmetic and copies ran while one was open for 0% -> 0% of each run, Pallas kernels for 0% -> 0%
where the time goes in v3:
time: 72.4 us; the launch traced here: 72.2 us
  blocking collectives  51.4 us (71%)
  Pallas kernels  13 us (18%)
  starting transfers between devices  5.46 us (8%)
  waiting for transfers between devices  2.29 us (3%)
    all_to_all x1, blocking collectives, per_device(): g = lax.all_to_all(payload, ('frm', 'ch'), 0, 0)  26 us
    all_to_all x1, blocking collectives, per_device(): st = lax.all_to_all(st, ('frm', 'row'), 0, 0)  13.2 us
    all_to_all x1, blocking collectives, per_device(): st = lax.all_to_all(st, 'row', 0, 0)  12.1 us
    pallas_call x1, Pallas kernels, call_k2(): pl.pallas_call(k2, out_shape=(shape((OWN, 128), jnp.float32), shape((64,...  7.16 us
    pallas_call x1, Pallas kernels, call_k1(): pl.pallas_call(k1, out_shape=(shape((6 * TAPS, SPAN), jnp.bfloat16), shap...  3.58 us
    ppermute x1, starting transfers between devices, per_device(): lax.ppermute(edge, 'row', [(i, i + 2 * (i % 2) - 1) for i in range(1, 15)])  3.1 us
    ppermute x1, starting transfers between devices, per_device(): other = lax.ppermute(mine, 'row', [(i, i ^ 1) for i in range(16)])  2.35 us
    ppermute x1, waiting for transfers between devices, per_device(): lax.ppermute(edge, 'row', [(i, i + 2 * (i % 2) - 1) for i in range(1, 15)])  2.29 us
  transfers between devices with their start and end apart: 2, of which 1 were waited for; matrix products, arithmetic and copies ran while one was open for 0% of the time, Pallas kernels for 0%

profile of v3, /device:TPU:1, one launch (start us, length us, event | category | flops | bytes accessed | tf_op | source)
XLA Modules:
  0.0 72.2 jit_solution(3036064991321986783)
XLA Ops:
  0.0 1.0 %k0.1 = (bf16[16,48,256]{2,1,0:T(8,128)(2,1)S(1)}, f32[2,1,128]{2,1,0:T(1,128)S(1)}) custom-call(bf16[16,255]{1,0:T(8,128)(2,1)} %bitcast.7, bf16[432,128]{1,0:T(8,128)(2,1)} %bitcast.6, f32[1,128]{1,0:T(1,128)} %bitcast.8, f32[1,128]{1,0:T(1,128)} %bitcast.9, f32[1,128]{1,0:T(1,128)} %bitcast.10, f32[1,128]{1,0:T(1,128)} %bitcast.11), custom_call_target="tpu_custom_call" | custom-call | tf_op jit(solution)/shard_map/k0/pallas_call | solution.py:334
  1.0 26.0 %all_to_all.15.g_ref = bf16[16,48,256]{2,1,0:T(8,128)(2,1)S(1)} all-to-all(bf16[16,48,256]{2,1,0:T(8,128)(2,1)S(1)} %get-tuple-element.14), channel_id=1, replica_groups=mesh['frm'=4,'row'=16,'ch'=4] {'frm','ch'}, dimensions={0} | all-to-all | bytes 786432 | tf_op jit(solution)/shard_map/all_to_all | solution.py:416
  27.1 0.1 k1a.1
  27.2 2.4 %collective-permute-start = (bf16[1216,128]{1,0:T(8,128)(2,1)S(1)}, bf16[1216,128]{1,0:T(8,128)(2,1)S(1)}, u32[]{:S(2)}, u32[]{:S(2)}) collective-permute-start(bf16[1216,128]{1,0:T(8,128)(2,1)S(1)} %get-tuple-element.15.mine_ref), channel_id=1, source_target_pairs={{0,4},{4,0},{8,12},{12,8},{16,20},{20,16},{24,28},{28,24},{32,36},... | collective-permute-start | bytes 933896 | tf_op jit(solution)/shard_map/ppermute | solution.py:418
  29.5 3.1 %collective-permute-start.1 = (bf16[64,384]{1,0:T(8,128)(2,1)S(1)}, bf16[64,384]{1,0:T(8,128)(2,1)S(1)}, u32[]{:S(2)}, u32[]{:S(2)}) collective-permute-start(bf16[64,384]{1,0:T(8,128)(2,1)S(1)} %get-tuple-element.16), channel_id=1, source_target_pairs={{4,8},{8,4},{12,16},{16,12},{20,24},{24,20},{28,32},{32,28},{36,40... | collective-permute-start | bytes 147464 | tf_op jit(solution)/shard_map/ppermute | solution.py:419
  32.6 2.3 %collective-permute-done.1.next_ref = bf16[64,384]{1,0:T(8,128)(2,1)S(1)} collective-permute-done((bf16[64,384]{1,0:T(8,128)(2,1)S(1)}, bf16[64,384]{1,0:T(8,128)(2,1)S(1)}, u32[]{:S(2)}, u32[]{:S(2)}) %collective-permute-start.1) | collective-permute-done | bytes 49184 | tf_op jit(solution)/shard_map/ppermute | solution.py:419
  34.9 0.0 collective-permute-done.other_ref
  34.9 3.6 %k1.1 = (bf16[864,1408]{1,0:T(8,128)(2,1)S(1)}, bf16[4,448,128]{2,1,0:T(8,128)(2,1)S(1)}, f32[16,8,128]{2,1,0:T(8,128)S(1)}) custom-call(bf16[16,48,256]{2,1,0:T(8,128)(2,1)S(1)} %all_to_all.15.g_ref, bf16[1216,128]{1,0:T(8,128)(2,1)S(1)} %get-tuple-element.15.mine_ref, bf16[1216,128]{1,0:T(8,128)(2,1)S(1)} %collective-permute-done.other_ref, ...), custom_call_target="tpu_custom_call" | custom-call | tf_op jit(solution)/shard_map/k1/pallas_call | solution.py:370
  38.5 12.1 %all_to_all.16.st_ref = f32[16,8,128]{2,1,0:T(8,128)S(1)} all-to-all(f32[16,8,128]{2,1,0:T(8,128)S(1)} %get-tuple-element.19), channel_id=1, replica_groups=mesh['frm'=4,'row'=16,'ch'=4] {'row'}, dimensions={0} | all-to-all | bytes 131072 | tf_op jit(solution)/shard_map/all_to_all | solution.py:421
  50.7 7.2 %k2.1 = (f32[1056,128]{1,0:T(8,128)S(1)}, f32[64,2,128]{2,1,0:T(2,128)S(1)}) custom-call(bf16[864,1408]{1,0:T(8,128)(2,1)S(1)} %get-tuple-element.17.pt_ref, bf16[4,448,128]{2,1,0:T(8,128)(2,1)S(1)} %get-tuple-element.18.wall_ref, f32[16,8,128]{2,1,0:T(8,128)S(1)} %all_to_all.16.st_ref, bf16[27,512,128]{2,1,0:T(8,128)(2,1)} %w2_hbm.1), custom_call_target="tpu_custom_call" | custom-call | tf_op jit(solution)/shard_map/k2/pallas_call | solution.py:386
  57.8 13.2 %all_to_all.17.st_ref = f32[64,2,128]{2,1,0:T(2,128)S(1)} all-to-all(f32[64,2,128]{2,1,0:T(2,128)S(1)} %get-tuple-element.21), channel_id=1, replica_groups=mesh['frm'=4,'row'=16,'ch'=4] {'frm','row'}, dimensions={0} | all-to-all | bytes 131072 | tf_op jit(solution)/shard_map/all_to_all | solution.py:423
  71.0 1.2 %k3.1 = bf16[1,6,170,128]{3,2,1,0:T(8,128)(2,1)} custom-call(f32[1056,128]{1,0:T(8,128)S(1)} %get-tuple-element.20.mix_ref, f32[64,2,128]{2,1,0:T(2,128)S(1)} %all_to_all.17.st_ref, f32[2,1,128]{2,1,0:T(1,128)S(1)} %get-tuple-element.22.par_ref), custom_call_target="tpu_custom_call" | custom-call | tf_op jit(solution)/shard_map/k3/pallas_call | solution.py:403
Async XLA Ops:
  27.2 7.8 %collective-permute-start = (bf16[1216,128]{1,0:T(8,128)(2,1)S(1)}, bf16[1216,128]{1,0:T(8,128)(2,1)S(1)}, u32[]{:S(2)}, u32[]{:S(2)}) collective-permute-start(bf16[1216,128]{1,0:T(8,128)(2,1)S(1)} %get-tuple-element.15.mine_ref), channel_id=1, source_target_pairs={{0,4},{4,0},{8,12},{12,8},{16,20},{20,16},{24,28},{28,24},{32,36},... | collective-permute-start | bytes 933896 | tf_op jit(solution)/shard_map/ppermute | solution.py:418
  29.5 5.4 %collective-permute-start.1 = (bf16[64,384]{1,0:T(8,128)(2,1)S(1)}, bf16[64,384]{1,0:T(8,128)(2,1)S(1)}, u32[]{:S(2)}, u32[]{:S(2)}) collective-permute-start(bf16[64,384]{1,0:T(8,128)(2,1)S(1)} %get-tuple-element.16), channel_id=1, source_target_pairs={{4,8},{8,4},{12,16},{16,12},{20,24},{24,20},{28,32},{32,28},{36,40... | collective-permute-start | bytes 147464 | tf_op jit(solution)/shard_map/ppermute | solution.py:419

commit v4 on v2

--- a/solution.py
+++ b/solution.py
@@ -24,8 +24,8 @@
 CELLS = ROWS * W
 TAPROWS = 27 * C_LAT
 HELD = 448
-PIECE = 64
-PIECES = tuple(i * 24 // 7 * 16 for i in range(8))
+HALF = HELD // 2
+EDGE = HELD + HALF
 VMEM = 48 * 1024 * 1024
 
 
@@ -64,14 +64,7 @@
     return [high, mid, v - high - mid]
 
 
-def piece_start(core, f):
-    low, high = PIECES[3], PIECES[7]
-    for i in (2, 1, 0):
-        low, high = jnp.where(f == i, PIECES[i], low), jnp.where(f == i, PIECES[4 + i], high)
-    return pl.multiple_of(jnp.where(core == 0, low, high), 16)
-
-
-def k0(tokens_hbm, w_hbm, p0, p1, p2, p3, out_ref, par_ref, tokens_ref, held_ref, in_ref, sems):
+def k0(tokens_hbm, w_hbm, p0, p1, p2, p3, out_ref, held_ref, half_ref, par_ref, tokens_ref, in_ref, sems):
     copies = [
         pltpu.make_async_copy(tokens_hbm, tokens_ref, sems.at[0]),
         pltpu.make_async_copy(w_hbm, held_ref.at[:TAPROWS], sems.at[1]),
@@ -86,41 +79,57 @@
         copy.wait()
     rows = parts3(in_ref[0]) + parts3(in_ref[1]) + [jnp.zeros((10, 128), jnp.float32)]
     held_ref[TAPROWS:, :] = jnp.concatenate(rows, axis=0).astype(jnp.bfloat16)
-    start = piece_start(lax.rem(lax.axis_index("row"), 2), lax.axis_index("frm"))
-    piece = jnp.concatenate([held_ref[pl.ds(start, 32), :], held_ref[pl.ds(start + 32, 32), :]], axis=1)
-    out_ref[:, :C_LAT, :255] = jnp.broadcast_to(tokens_ref[...][None], (16, C_LAT, 255))
-    out_ref[:, C_LAT:, :] = jnp.broadcast_to(piece[None], (16, PIECE // 2, 256))
-
-
-def k1a(g_ref, up_ref, down_ref, mine_ref):
+    start = pl.multiple_of(lax.rem(lax.axis_index("row"), 2) * HALF, 16)
+    half_ref[...] = held_ref[pl.ds(start, HALF), :]
+    out_ref[...] = jnp.broadcast_to(tokens_ref[...][None], (16, C_LAT, 255))
+
+
+def first_rows(g_ref, f):
+    return ((0, g_ref[4 * f, :, :170]), (176, g_ref[4 * f, :, 170:255]), (261, g_ref[4 * f + 1, :, :85]))
+
+
+def last_rows(g_ref, f):
+    return ((0, g_ref[4 * f + 2, :, 170:255]), (85, g_ref[4 * f + 3, :, :85]), (176, g_ref[4 * f + 3, :, 85:255]))
+
+
+def write_edge(rows, g_ref, out_ref):
     for f in range(FRAMES):
-        at = slice(16 * f, 16 * f + 16)
-
-        def src(j, lo, hi):
-            return g_ref[4 * f + j, :C_LAT, lo:hi]
-
-        up_ref[at, 0:170] = src(0, 0, 170)
-        up_ref[at, 176:261] = src(0, 170, 255)
-        up_ref[at, 261:346] = src(1, 0, 85)
-        down_ref[at, 0:85] = src(2, 170, 255)
-        down_ref[at, 85:170] = src(3, 0, 85)
-        down_ref[at, 176:346] = src(3, 85, 255)
-    for i in range(16):
-        mine_ref[i, :32] = g_ref[i, C_LAT:, :128]
-        mine_ref[i, 32:] = g_ref[i, C_LAT:, 128:]
-
-
-def k1(g_ref, above_ref, below_ref, mine_ref, other_ref, pt_ref, wall_ref, st_ref, x_ref):
+        for lane, v in rows(g_ref, f):
+            out_ref[16 * f : 16 * f + 16, lane : lane + v.shape[1]] = v
+
+
+def k1t(g_ref, next_ref):
+    next_ref[...] = jnp.zeros_like(next_ref)
     core = lax.rem(lax.axis_index("row"), 2)
-    for i in range(FRAMES):
-        mine, other = piece_start(core, i), piece_start(1 - core, i)
-        for j in range(4):
-            wall_ref[j, pl.ds(mine, PIECE), :] = mine_ref[4 * i + j]
-            wall_ref[j, pl.ds(other, PIECE), :] = other_ref[4 * i + j]
-    weight = jnp.concatenate([wall_ref[j, :TAPROWS, :] for j in range(4)], axis=1)
+
+    @pl.when(core == 0)
+    def _():
+        write_edge(first_rows, g_ref, next_ref)
+
+    @pl.when(core == 1)
+    def _():
+        write_edge(last_rows, g_ref, next_ref)
+
+
+def k1w(g_ref, side_ref, far_ref, next_ref, mate_ref, x_ref, edge_ref):
+    mate_ref[:HELD] = side_ref[...]
+    mate_ref[HELD:EDGE] = far_ref[...]
+    edge_ref[...] = jnp.zeros_like(edge_ref)
     x_ref[...] = jnp.zeros_like(x_ref)
-    pt_ref[: 2 * TAPS, :] = jnp.zeros((2 * TAPS, SPAN), jnp.bfloat16)
-
+    core = lax.rem(lax.axis_index("row"), 2)
+
+    @pl.when(core == 0)
+    def _():
+        write_edge(last_rows, g_ref, edge_ref)
+        x_ref[:, LEAD : LEAD + 2 * STRIDE] = next_ref[:, : 2 * STRIDE]
+
+    @pl.when(core == 1)
+    def _():
+        write_edge(first_rows, g_ref, edge_ref)
+        x_ref[:, LEAD + 8 * STRIDE : LEAD + 10 * STRIDE] = next_ref[:, : 2 * STRIDE]
+
+    for i in range(3):
+        mate_ref[EDGE + 64 * i : EDGE + 64 * (i + 1)] = edge_ref[:, 128 * i : 128 * (i + 1)]
     plan = (
         ((0, 0, 170),),
         ((0, 170, 255), (1, 0, 85)),
@@ -134,13 +143,32 @@
         for row, parts in enumerate(plan):
             lane = LEAD + STRIDE * (row + 2)
             for j, lo, hi in parts:
-                x_ref[at, lane : lane + hi - lo] = g_ref[4 * f + j, :C_LAT, lo:hi]
+                x_ref[at, lane : lane + hi - lo] = g_ref[4 * f + j, :, lo:hi]
                 lane += hi - lo
-        for row in range(2):
-            lane = LEAD + STRIDE * row
-            x_ref[at, lane : lane + W] = above_ref[at, STRIDE * row : STRIDE * row + W]
-            lane = LEAD + STRIDE * (row + 8)
-            x_ref[at, lane : lane + W] = below_ref[at, STRIDE * row : STRIDE * row + W]
+
+
+def k1(x_in_ref, held_ref, mine_ref, other_ref, pt_ref, wall_ref, st_ref, x_ref):
+    c, core = lax.axis_index("ch"), lax.rem(lax.axis_index("row"), 2)
+    wall_ref[c] = held_ref[...]
+    wall_ref[lax.rem(c + 1 + 2 * core, 4)] = mine_ref[:HELD, :]
+    wall_ref[lax.rem(c + 3 - 2 * core, 4)] = other_ref[:HELD, :]
+    far = lax.rem(c + 2, 4)
+    wall_ref[far, pl.ds(pl.multiple_of(core * HALF, 16), HALF), :] = mine_ref[HELD:EDGE, :]
+    wall_ref[far, pl.ds(pl.multiple_of((1 - core) * HALF, 16), HALF), :] = other_ref[HELD:EDGE, :]
+    weight = jnp.concatenate([wall_ref[j, :TAPROWS, :] for j in range(4)], axis=1)
+    x_ref[...] = x_in_ref[...]
+    pt_ref[: 2 * TAPS, :] = jnp.zeros((2 * TAPS, SPAN), jnp.bfloat16)
+    parts = [other_ref[EDGE + 64 * i : EDGE + 64 * (i + 1)] for i in range(3)]
+    edge = jnp.concatenate(parts, axis=1)[:, : 2 * STRIDE]
+
+    @pl.when(core == 0)
+    def _():
+        x_ref[:, LEAD + 8 * STRIDE : LEAD + 10 * STRIDE] = edge
+
+    @pl.when(core == 1)
+    def _():
+        x_ref[:, LEAD : LEAD + 2 * STRIDE] = edge
+
     for f in range(FRAMES):
         for b in range(3):
             for e in range(3):
@@ -299,14 +327,15 @@
     return pl.pallas_call(
         k0,
         out_shape=(
-            shape((16, C_LAT + PIECE // 2, 256), jnp.bfloat16),
+            shape((16, C_LAT, 255), jnp.bfloat16),
+            shape((HELD, 128), jnp.bfloat16),
+            shape((HALF, 128), jnp.bfloat16),
             shape((2, 1, 128), jnp.float32),
         ),
         in_specs=[INHBM] * 6,
-        out_specs=(INVMEM,) * 2,
+        out_specs=(INVMEM,) * 4,
         scratch_shapes=[
             pltpu.VMEM((C_LAT, 255), jnp.bfloat16),
-            pltpu.VMEM((HELD, 128), jnp.bfloat16),
             pltpu.VMEM((2, 1, 128), jnp.float32),
             pltpu.SemaphoreType.DMA((6,)),
         ],
@@ -315,19 +344,30 @@
     )(*[pltpu.with_memory_space_constraint(v, pltpu.HBM) for v in arrays])
 
 
-def call_k1a(g):
-    return pl.pallas_call(
-        k1a,
+def call_k1t(g):
+    return pl.pallas_call(
+        k1t,
+        out_shape=shape((16 * FRAMES, 384), jnp.bfloat16),
+        in_specs=[INVMEM],
+        out_specs=INVMEM,
+        compiler_params=pltpu.CompilerParams(vmem_limit_bytes=VMEM),
+        name="k1t",
+    )(g)
+
+
+def call_k1w(*arrays):
+    return pl.pallas_call(
+        k1w,
         out_shape=(
-            shape((16 * FRAMES, 2 * STRIDE), jnp.bfloat16),
-            shape((16 * FRAMES, 2 * STRIDE), jnp.bfloat16),
-            shape((16, PIECE, 128), jnp.bfloat16),
+            shape((EDGE + 3 * 64, 128), jnp.bfloat16),
+            shape((16 * FRAMES, XLANES), jnp.bfloat16),
         ),
-        in_specs=[INVMEM],
-        out_specs=(INVMEM,) * 3,
-        compiler_params=pltpu.CompilerParams(vmem_limit_bytes=VMEM),
-        name="k1a",
-    )(g)
+        in_specs=[INVMEM] * 4,
+        out_specs=(INVMEM,) * 2,
+        scratch_shapes=[pltpu.VMEM((16 * FRAMES, 384), jnp.bfloat16)],
+        compiler_params=pltpu.CompilerParams(vmem_limit_bytes=VMEM),
+        name="k1w",
+    )(*arrays)
 
 
 def call_k1(*arrays):
@@ -338,7 +378,7 @@
             shape((4, HELD, 128), jnp.bfloat16),
             shape((16, 8, 128), jnp.float32),
         ),
-        in_specs=[INVMEM] * 5,
+        in_specs=[INVMEM] * 4,
         out_specs=(INVMEM,) * 3,
         scratch_shapes=[pltpu.VMEM((16 * FRAMES, XLANES), jnp.bfloat16)],
         compiler_params=pltpu.CompilerParams(vmem_limit_bytes=VMEM),
@@ -376,13 +416,16 @@
 
 def per_device(latents, in_weight, in_gain, in_shift, mid_weight, mid_gain, mid_shift):
     params = [v.reshape(1, 128) for v in (in_gain, in_shift, mid_gain, mid_shift)]
-    payload, par = call_k0(latents.T, in_weight.reshape(TAPROWS, 128), *params)
+    payload, held, half, par = call_k0(latents.T, in_weight.reshape(TAPROWS, 128), *params)
     g = lax.all_to_all(payload, ("frm", "ch"), 0, 0)
-    up, down, mine = call_k1a(g)
-    below = lax.ppermute(up, "row", [(i + 1, i) for i in range(15)])
-    above = lax.ppermute(down, "row", [(i, i + 1) for i in range(15)])
+    sides = [(4 * i + (j + 1 + 2 * (i % 2)) % 4, 4 * i + j) for i in range(16) for j in range(4)]
+    side = lax.ppermute(held, ("row", "ch"), sides)
+    fars = [(4 * (i ^ 8) + (j + 2) % 4, 4 * i + j) for i in range(16) for j in range(4)]
+    far = lax.ppermute(half, ("row", "ch"), fars)
+    edge = lax.ppermute(call_k1t(g), "row", [(i, i + 2 * (i % 2) - 1) for i in range(1, 15)])
+    mine, x = call_k1w(g, side, far, edge)
     other = lax.ppermute(mine, "row", [(i, i ^ 1) for i in range(16)])
-    pt, wall, st = call_k1(g, above, below, mine, other)
+    pt, wall, st = call_k1(x, held, mine, other)
     st = lax.all_to_all(st, "row", 0, 0)
     mix, st = call_k2(pt, wall, st, mid_weight)
     st = lax.all_to_all(st, ("frm", "row"), 0, 0)

time: 75.5 us -> 69.3 us (0.918)
  blocking collectives: 50.5 us -> 24 us
  starting transfers between devices: 7.37 us -> 23.2 us
  waiting for transfers between devices: 3.48 us -> 7.8 us
    all_to_all x1 -> x0, blocking collectives: 26 us -> none  [per_device(): g = lax.all_to_all(payload, ('frm', 'ch'), 0, 0)]
    all_to_all x0 -> x1, starting transfers between devices: none -> 11.6 us  [per_device(): g = lax.all_to_all(payload, ('frm', 'ch'), 0, 0)]
    ppermute x2 -> x3, starting transfers between devices: 5.02 us -> 11.5 us  [the longest x1 6.4 us: per_device(): lax.ppermute(call_k1t(g), 'row', [(i, i + 2 * (i % 2) - 1) for i in range...]
    all_to_all x0 -> x1, waiting for transfers between devices: none -> 4.59 us  [per_device(): g = lax.all_to_all(payload, ('frm', 'ch'), 0, 0)]
    ppermute x1, starting transfers between devices: 2.35 us -> 0.09 us  [per_device(): other = lax.ppermute(mine, 'row', [(i, i ^ 1) for i in range(16)])]
    ppermute x2 -> x3, waiting for transfers between devices: 3.47 us -> 1.74 us  [the longest x1 1.74 us: per_device(): lax.ppermute(call_k1t(g), 'row', [(i, i + 2 * (i % 2) - 1) for i in range...]
    ppermute x1, waiting for transfers between devices: 0.01 us -> 1.46 us  [per_device(): other = lax.ppermute(mine, 'row', [(i, i ^ 1) for i in range(16)])]
    pallas_call x2 -> x3, Pallas kernels: 1.11 us -> 1.98 us  [the longest x1 1.64 us: call_k0(): pl.pallas_call(k0, out_shape=(shape((16, C_LAT, 255), jnp.bfloat16), shap...]
  transfers between devices with their start and end apart: 3 -> 5, of which waited for: 1 -> 3; matrix products, arithmetic and copies ran while one was open for 0% -> 0% of each run, Pallas kernels for 0% -> 0%
where the time goes in v4:
time: 69.3 us; the launch traced here: 68.9 us
  blocking collectives  24 us (35%)
  starting transfers between devices  23.2 us (33%)
  Pallas kernels  13.8 us (20%)
  waiting for transfers between devices  7.8 us (11%)
    all_to_all x1, blocking collectives, per_device(): st = lax.all_to_all(st, ('frm', 'row'), 0, 0)  13.3 us
    all_to_all x1, starting transfers between devices, per_device(): g = lax.all_to_all(payload, ('frm', 'ch'), 0, 0)  11.6 us
    all_to_all x1, blocking collectives, per_device(): st = lax.all_to_all(st, 'row', 0, 0)  10.7 us
    pallas_call x1, Pallas kernels, call_k2(): pl.pallas_call(k2, out_shape=(shape((OWN, 128), jnp.float32), shape((64,...  7.16 us
    ppermute x1, starting transfers between devices, per_device(): lax.ppermute(call_k1t(g), 'row', [(i, i + 2 * (i % 2) - 1) for i in range...  6.4 us
    all_to_all x1, waiting for transfers between devices, per_device(): g = lax.all_to_all(payload, ('frm', 'ch'), 0, 0)  4.59 us
    pallas_call x1, Pallas kernels, call_k1(): pl.pallas_call(k1, out_shape=(shape((6 * TAPS, SPAN), jnp.bfloat16), shap...  3.54 us
    ppermute x1, starting transfers between devices, per_device(): far = lax.ppermute(half, ('row', 'ch'), fars)  2.85 us
  transfers between devices with their start and end apart: 5, of which 3 were waited for; matrix products, arithmetic and copies ran while one was open for 0% of the time, Pallas kernels for 0%

profile of v4, /device:TPU:1, one launch (start us, length us, event | category | flops | bytes accessed | tf_op | source)
XLA Modules:
  0.0 68.9 jit_solution(14262841212774558139)
XLA Ops:
  0.0 1.6 %k0.1 = (bf16[16,16,255]{2,1,0:T(8,128)(2,1)}, bf16[448,128]{1,0:T(8,128)(2,1)S(1)}, bf16[224,128]{1,0:T(8,128)(2,1)S(1)}, f32[2,1,128]{2,1,0:T(1,128)S(1)}) custom-call(bf16[16,255]{1,0:T(8,128)(2,1)} %bitcast.7, bf16[432,128]{1,0:T(8,128)(2,1)} %bitcast.6, f32[1,128]{1,0:T(1,128)} %bitcast.8, f32[1,128]{1,0:T(1,128)} %bitcast.9, f32[1,128]{1,0:T(1,128)} %bitcast.10, ...), custom_call_target="tpu_custom_call" | custom-call | tf_op jit(solution)/shard_map/k0/pallas_call | solution.py:327
  1.6 11.6 %all-to-all-start = ((bf16[16,16,255]{2,1,0:T(8,128)(2,1)}), bf16[16,16,255]{2,1,0:T(8,128)(2,1)S(1)}, u32[]{:S(2)}, u32[]{:S(2)}) async-start(bf16[16,16,255]{2,1,0:T(8,128)(2,1)} %get-tuple-element.16), calls=%async_computation | async-start | bytes 262144 | tf_op jit(solution)/shard_map/all_to_all | solution.py:420
  13.2 2.3 %collective-permute-start = (bf16[448,128]{1,0:T(8,128)(2,1)S(1)}, bf16[448,128]{1,0:T(8,128)(2,1)S(1)}, u32[]{:S(2)}, u32[]{:S(2)}) collective-permute-start(bf16[448,128]{1,0:T(8,128)(2,1)S(1)} %get-tuple-element.17.held_ref), channel_id=1, source_target_pairs={{1,0},{2,1},{3,2},{0,3},{7,4},{4,5},{5,6},{6,7},{9,8},{10,9},{11,1... | collective-permute-start | bytes 344072 | tf_op jit(solution)/shard_map/ppermute | solution.py:422
  15.5 2.8 %collective-permute-start.1 = (bf16[224,128]{1,0:T(8,128)(2,1)S(1)}, bf16[224,128]{1,0:T(8,128)(2,1)S(1)}, u32[]{:S(2)}, u32[]{:S(2)}) collective-permute-start(bf16[224,128]{1,0:T(8,128)(2,1)S(1)} %get-tuple-element.18), channel_id=1, source_target_pairs={{34,0},{35,1},{32,2},{33,3},{38,4},{39,5},{36,6},{37,7},{42,8},{43... | collective-permute-start | bytes 172040 | tf_op jit(solution)/shard_map/ppermute | solution.py:424
  18.4 4.6 %all-to-all-done.g_ref = bf16[16,16,255]{2,1,0:T(8,128)(2,1)S(1)} async-done(((bf16[16,16,255]{2,1,0:T(8,128)(2,1)}), bf16[16,16,255]{2,1,0:T(8,128)(2,1)S(1)}, u32[]{:S(2)}, u32[]{:S(2)}) %all-to-all-start) | async-done | bytes 130592 | tf_op jit(solution)/shard_map/all_to_all | solution.py:420
  23.0 0.1 k1t.1
  23.1 6.4 %collective-permute-start.2 = (bf16[64,384]{1,0:T(8,128)(2,1)S(1)}, bf16[64,384]{1,0:T(8,128)(2,1)S(1)}, u32[]{:S(2)}, u32[]{:S(2)}) collective-permute-start(bf16[64,384]{1,0:T(8,128)(2,1)S(1)} %k1t.1), channel_id=1, source_target_pairs={{4,8},{8,4},{12,16},{16,12},{20,24},{24,20},{28,32},{32,28},{36,40... | collective-permute-start | bytes 147464 | tf_op jit(solution)/shard_map/ppermute | solution.py:425
  29.5 0.0 collective-permute-done.1.far_ref
  29.5 0.0 collective-permute-done.side_ref
  29.5 1.7 %collective-permute-done.2.next_ref = bf16[64,384]{1,0:T(8,128)(2,1)S(1)} collective-permute-done((bf16[64,384]{1,0:T(8,128)(2,1)S(1)}, bf16[64,384]{1,0:T(8,128)(2,1)S(1)}, u32[]{:S(2)}, u32[]{:S(2)}) %collective-permute-start.2) | collective-permute-done | bytes 49184 | tf_op jit(solution)/shard_map/ppermute | solution.py:425
  31.2 0.2 k1w.1
  31.5 0.1 collective-permute-start.3
  31.6 1.5 %collective-permute-done.3.other_ref = bf16[864,128]{1,0:T(8,128)(2,1)S(1)} collective-permute-done((bf16[864,128]{1,0:T(8,128)(2,1)S(1)}, bf16[864,128]{1,0:T(8,128)(2,1)S(1)}, u32[]{:S(2)}, u32[]{:S(2)}) %collective-permute-start.3) | collective-permute-done | bytes 221216 | tf_op jit(solution)/shard_map/ppermute | solution.py:427
  33.0 3.5 %k1.1 = (bf16[864,1408]{1,0:T(8,128)(2,1)S(1)}, bf16[4,448,128]{2,1,0:T(8,128)(2,1)S(1)}, f32[16,8,128]{2,1,0:T(8,128)S(1)}) custom-call(bf16[64,2048]{1,0:T(8,128)(2,1)S(1)} %get-tuple-element.19.x_in_ref, bf16[448,128]{1,0:T(8,128)(2,1)S(1)} %get-tuple-element.17.held_ref, bf16[864,128]{1,0:T(8,128)(2,1)S(1)} %get-tuple-element.20.mine_ref, ...), custom_call_target="tpu_custom_call" | custom-call | tf_op jit(solution)/shard_map/k1/pallas_call | solution.py:374
  36.6 10.7 %all_to_all.15.st_ref = f32[16,8,128]{2,1,0:T(8,128)S(1)} all-to-all(f32[16,8,128]{2,1,0:T(8,128)S(1)} %get-tuple-element.23), channel_id=1, replica_groups=mesh['frm'=4,'row'=16,'ch'=4] {'row'}, dimensions={0} | all-to-all | bytes 131072 | tf_op jit(solution)/shard_map/all_to_all | solution.py:429
  47.2 7.2 %k2.1 = (f32[1056,128]{1,0:T(8,128)S(1)}, f32[64,2,128]{2,1,0:T(2,128)S(1)}) custom-call(bf16[864,1408]{1,0:T(8,128)(2,1)S(1)} %get-tuple-element.21.pt_ref, bf16[4,448,128]{2,1,0:T(8,128)(2,1)S(1)} %get-tuple-element.22.wall_ref, f32[16,8,128]{2,1,0:T(8,128)S(1)} %all_to_all.15.st_ref, bf16[27,512,128]{2,1,0:T(8,128)(2,1)} %w2_hbm.1), custom_call_target="tpu_custom_call" | custom-call | tf_op jit(solution)/shard_map/k2/pallas_call | solution.py:390
  54.4 13.3 %all_to_all.16.st_ref = f32[64,2,128]{2,1,0:T(2,128)S(1)} all-to-all(f32[64,2,128]{2,1,0:T(2,128)S(1)} %get-tuple-element.25), channel_id=1, replica_groups=mesh['frm'=4,'row'=16,'ch'=4] {'frm','row'}, dimensions={0} | all-to-all | bytes 131072 | tf_op jit(solution)/shard_map/all_to_all | solution.py:431
  67.8 1.2 %k3.1 = bf16[1,6,170,128]{3,2,1,0:T(8,128)(2,1)} custom-call(f32[1056,128]{1,0:T(8,128)S(1)} %get-tuple-element.24.mix_ref, f32[64,2,128]{2,1,0:T(2,128)S(1)} %all_to_all.16.st_ref, f32[2,1,128]{2,1,0:T(1,128)S(1)} %get-tuple-element.26.par_ref), custom_call_target="tpu_custom_call" | custom-call | tf_op jit(solution)/shard_map/k3/pallas_call | solution.py:407
Async XLA Ops:
  1.6 21.3 %all-to-all-start = ((bf16[16,16,255]{2,1,0:T(8,128)(2,1)}), bf16[16,16,255]{2,1,0:T(8,128)(2,1)S(1)}, u32[]{:S(2)}, u32[]{:S(2)}) async-start(bf16[16,16,255]{2,1,0:T(8,128)(2,1)} %get-tuple-element.16), calls=%async_computation | async-start | bytes 262144 | tf_op jit(solution)/shard_map/all_to_all | solution.py:420
  13.2 16.2 %collective-permute-start = (bf16[448,128]{1,0:T(8,128)(2,1)S(1)}, bf16[448,128]{1,0:T(8,128)(2,1)S(1)}, u32[]{:S(2)}, u32[]{:S(2)}) collective-permute-start(bf16[448,128]{1,0:T(8,128)(2,1)S(1)} %get-tuple-element.17.held_ref), channel_id=1, source_target_pairs={{1,0},{2,1},{3,2},{0,3},{7,4},{4,5},{5,6},{6,7},{9,8},{10,9},{11,1... | collective-permute-start | bytes 344072 | tf_op jit(solution)/shard_map/ppermute | solution.py:422
  15.5 14.0 %collective-permute-start.1 = (bf16[224,128]{1,0:T(8,128)(2,1)S(1)}, bf16[224,128]{1,0:T(8,128)(2,1)S(1)}, u32[]{:S(2)}, u32[]{:S(2)}) collective-permute-start(bf16[224,128]{1,0:T(8,128)(2,1)S(1)} %get-tuple-element.18), channel_id=1, source_target_pairs={{34,0},{35,1},{32,2},{33,3},{38,4},{39,5},{36,6},{37,7},{42,8},{43... | collective-permute-start | bytes 172040 | tf_op jit(solution)/shard_map/ppermute | solution.py:424
  23.1 8.2 %collective-permute-start.2 = (bf16[64,384]{1,0:T(8,128)(2,1)S(1)}, bf16[64,384]{1,0:T(8,128)(2,1)S(1)}, u32[]{:S(2)}, u32[]{:S(2)}) collective-permute-start(bf16[64,384]{1,0:T(8,128)(2,1)S(1)} %k1t.1), channel_id=1, source_target_pairs={{4,8},{8,4},{12,16},{16,12},{20,24},{24,20},{28,32},{32,28},{36,40... | collective-permute-start | bytes 147464 | tf_op jit(solution)/shard_map/ppermute | solution.py:425
  31.5 1.6 %collective-permute-start.3 = (bf16[864,128]{1,0:T(8,128)(2,1)S(1)}, bf16[864,128]{1,0:T(8,128)(2,1)S(1)}, u32[]{:S(2)}, u32[]{:S(2)}) collective-permute-start(bf16[864,128]{1,0:T(8,128)(2,1)S(1)} %get-tuple-element.20.mine_ref), channel_id=1, source_target_pairs={{0,4},{4,0},{8,12},{12,8},{16,20},{20,16},{24,28},{28,24},{32,36},... | collective-permute-start | bytes 663560 | tf_op jit(solution)/shard_map/ppermute | solution.py:427

commit v5 on v4

--- a/solution.py
+++ b/solution.py
@@ -19,13 +19,12 @@
 TAPS = 9 * C_LAT
 LEAD = 128
 XLANES = 2048
-K1_CHUNKS = ((128, 384), (512, 384), (896, 384))
+K1_CHUNKS = ((128, 640), (768, 512))
 CHUNKS = ((0, 384), (384, 384), (768, 384), (1152, 256))
 CELLS = ROWS * W
 TAPROWS = 27 * C_LAT
 HELD = 448
 HALF = HELD // 2
-EDGE = HELD + HALF
 VMEM = 48 * 1024 * 1024
 
 
@@ -98,38 +97,40 @@
             out_ref[16 * f : 16 * f + 16, lane : lane + v.shape[1]] = v
 
 
-def k1t(g_ref, next_ref):
+def k1t(g_ref, next_ref, mate_ref):
     next_ref[...] = jnp.zeros_like(next_ref)
+    mate_ref[...] = jnp.zeros_like(mate_ref)
     core = lax.rem(lax.axis_index("row"), 2)
 
     @pl.when(core == 0)
     def _():
         write_edge(first_rows, g_ref, next_ref)
+        write_edge(last_rows, g_ref, mate_ref)
 
     @pl.when(core == 1)
     def _():
         write_edge(last_rows, g_ref, next_ref)
-
-
-def k1w(g_ref, side_ref, far_ref, next_ref, mate_ref, x_ref, edge_ref):
-    mate_ref[:HELD] = side_ref[...]
-    mate_ref[HELD:EDGE] = far_ref[...]
-    edge_ref[...] = jnp.zeros_like(edge_ref)
+        write_edge(first_rows, g_ref, mate_ref)
+
+
+def k1w(g_ref, side_ref, far_ref, next_ref, mate_ref, both_ref, x_ref):
+    both_ref[:HELD] = side_ref[...]
+    both_ref[HELD:] = far_ref[...]
     x_ref[...] = jnp.zeros_like(x_ref)
     core = lax.rem(lax.axis_index("row"), 2)
 
+    def edges(above_ref, below_ref):
+        x_ref[:, LEAD : LEAD + 2 * STRIDE] = above_ref[:, : 2 * STRIDE]
+        x_ref[:, LEAD + 8 * STRIDE : LEAD + 10 * STRIDE] = below_ref[:, : 2 * STRIDE]
+
     @pl.when(core == 0)
     def _():
-        write_edge(last_rows, g_ref, edge_ref)
-        x_ref[:, LEAD : LEAD + 2 * STRIDE] = next_ref[:, : 2 * STRIDE]
+        edges(next_ref, mate_ref)
 
     @pl.when(core == 1)
     def _():
-        write_edge(first_rows, g_ref, edge_ref)
-        x_ref[:, LEAD + 8 * STRIDE : LEAD + 10 * STRIDE] = next_ref[:, : 2 * STRIDE]
-
-    for i in range(3):
-        mate_ref[EDGE + 64 * i : EDGE + 64 * (i + 1)] = edge_ref[:, 128 * i : 128 * (i + 1)]
+        edges(mate_ref, next_ref)
+
     plan = (
         ((0, 0, 170),),
         ((0, 170, 255), (1, 0, 85)),
@@ -147,68 +148,77 @@
                 lane += hi - lo
 
 
-def k1(x_in_ref, held_ref, mine_ref, other_ref, pt_ref, wall_ref, st_ref, x_ref):
-    c, core = lax.axis_index("ch"), lax.rem(lax.axis_index("row"), 2)
-    wall_ref[c] = held_ref[...]
-    wall_ref[lax.rem(c + 1 + 2 * core, 4)] = mine_ref[:HELD, :]
-    wall_ref[lax.rem(c + 3 - 2 * core, 4)] = other_ref[:HELD, :]
-    far = lax.rem(c + 2, 4)
-    wall_ref[far, pl.ds(pl.multiple_of(core * HALF, 16), HALF), :] = mine_ref[HELD:EDGE, :]
-    wall_ref[far, pl.ds(pl.multiple_of((1 - core) * HALF, 16), HALF), :] = other_ref[HELD:EDGE, :]
-    weight = jnp.concatenate([wall_ref[j, :TAPROWS, :] for j in range(4)], axis=1)
-    x_ref[...] = x_in_ref[...]
+def valid(lo, size):
+    at = lo + lax.broadcasted_iota(jnp.int32, (size, 128), 0)
+    ok = (at >= STRIDE) & (at < STRIDE + OWN)
+    for row in range(1, 7):
+        gap = STRIDE * row + W
+        if lo < gap + STRIDE - W and gap < lo + size:
+            ok = ok & ((at < gap) | (at >= gap + STRIDE - W))
+    return ok
+
+
+def moments(pt_ref, weight):
+    lanes = weight.shape[1]
+    pilot = None
+    s1 = s2 = jnp.zeros((8, lanes), jnp.float32)
+    for g in range(FRAMES):
+        for lo, size in K1_CHUNKS:
+            h = lax.dot_general(
+                pt_ref[max(g, 2) * TAPS : (g + 3) * TAPS, lo : lo + size],
+                weight[max(2 - g, 0) * TAPS :],
+                (((0,), (0,)), ((), ())),
+                preferred_element_type=jnp.float32,
+            )
+            ok = jnp.concatenate([valid(lo, size)] * (lanes // 128), axis=1)
+            if pilot is None:
+                cells = sum(lo <= STRIDE * row + col < lo + size for row in range(1, 7) for col in range(W))
+                pilot = jnp.sum(jnp.where(ok, h, 0.0), axis=0, keepdims=True) * (1.0 / cells)
+            d = jnp.where(ok, h - pilot, 0.0).reshape(size // 8, 8, lanes)
+            s1 = s1 + jnp.sum(d, axis=0)
+            s2 = s2 + jnp.sum(d * d, axis=0)
+    s1 = jnp.sum(s1, axis=0, keepdims=True)
+    s2 = jnp.sum(s2, axis=0, keepdims=True)
+    d = s1 / (FRAMES * CELLS)
+    return pilot + d, s2 - s1 * d
+
+
+def k1p(x_ref, held_ref, side_ref, pt_ref, near_ref):
     pt_ref[: 2 * TAPS, :] = jnp.zeros((2 * TAPS, SPAN), jnp.bfloat16)
-    parts = [other_ref[EDGE + 64 * i : EDGE + 64 * (i + 1)] for i in range(3)]
-    edge = jnp.concatenate(parts, axis=1)[:, : 2 * STRIDE]
-
-    @pl.when(core == 0)
-    def _():
-        x_ref[:, LEAD + 8 * STRIDE : LEAD + 10 * STRIDE] = edge
-
-    @pl.when(core == 1)
-    def _():
-        x_ref[:, LEAD : LEAD + 2 * STRIDE] = edge
-
     for f in range(FRAMES):
         for b in range(3):
             for e in range(3):
                 at = (f + 2) * TAPS + (3 * b + e) * 16
                 lane = LEAD + STRIDE * b + e - 1
                 pt_ref[at : at + 16, :] = x_ref[16 * f : 16 * f + 16, lane : lane + SPAN]
-
-    def hidden(g, lo, size):
-        return lax.dot_general(
-            pt_ref[g * TAPS : (g + 3) * TAPS, lo : lo + size],
-            weight,
-            (((0,), (0,)), ((), ())),
-            preferred_element_type=jnp.float32,
-        )
-
-    def valid(lo, size):
-        at = lo + lax.broadcasted_iota(jnp.int32, (size, 128), 0)
-        ok = (at >= STRIDE) & (at < STRIDE + OWN)
-        for row in range(1, 7):
-            gap = STRIDE * row + W
-            if lo < gap + STRIDE - W and gap < lo + size:
-                ok = ok & ((at < gap) | (at >= gap + STRIDE - W))
-        return jnp.concatenate([ok] * 4, axis=1)
-
-    pilot = jnp.sum(jnp.where(valid(256, 128), hidden(0, 256, 128), 0.0), axis=0, keepdims=True) * (1.0 / 122)
-    s1 = s2 = jnp.zeros((8, CH), jnp.float32)
-    for g in range(FRAMES):
-        for lo, size in K1_CHUNKS:
-            d = jnp.where(valid(lo, size), hidden(g, lo, size) - pilot, 0.0)
-            d = d.reshape(size // 8, 8, CH)
-            s1 = s1 + jnp.sum(d, axis=0)
-            s2 = s2 + jnp.sum(d * d, axis=0)
-    n = FRAMES * CELLS
-    s1 = jnp.sum(s1, axis=0, keepdims=True)
-    s2 = jnp.sum(s2, axis=0, keepdims=True)
-    d = s1 / n
-    for i, v in enumerate((pilot + d, s2 - s1 * d)):
-        for j in range(4):
-            part = v[:, 128 * j : 128 * (j + 1)]
-            st_ref[:, 4 * i + j : 4 * i + j + 1, :] = jnp.broadcast_to(part[None], (16, 1, 128))
+    mean, squares = moments(pt_ref, jnp.concatenate([held_ref[:TAPROWS], side_ref[:TAPROWS]], axis=1))
+    for i in range(2):
+        near_ref[i : i + 1] = mean[:, 128 * i : 128 * (i + 1)]
+        near_ref[2 + i : 3 + i] = squares[:, 128 * i : 128 * (i + 1)]
+    near_ref[4:] = jnp.zeros((4, 128), jnp.float32)
+
+
+def k1q(pt_ref, near_ref, held_ref, mine_ref, other_ref, wall_ref, st_ref):
+    c, core = lax.axis_index("ch"), lax.rem(lax.axis_index("row"), 2)
+    side, side_x, far = (lax.rem(c + i, 4) for i in (1 + 2 * core, 3 - 2 * core, 2))
+    wall_ref[c] = held_ref[...]
+    wall_ref[side] = mine_ref[:HELD, :]
+    wall_ref[side_x] = other_ref[:HELD, :]
+    wall_ref[far, pl.ds(pl.multiple_of(core * HALF, 16), HALF), :] = mine_ref[HELD:, :]
+    wall_ref[far, pl.ds(pl.multiple_of((1 - core) * HALF, 16), HALF), :] = other_ref[HELD:, :]
+    mean, squares = moments(pt_ref, jnp.concatenate([other_ref[:TAPROWS], wall_ref[far][:TAPROWS]], axis=1))
+
+    def send(at, v):
+        st_ref[:, pl.ds(at, 1), :] = jnp.broadcast_to(v[None], (16, 1, 128))
+
+    for at, m, q in (
+        (c, near_ref[0:1], near_ref[2:3]),
+        (side, near_ref[1:2], near_ref[3:4]),
+        (side_x, mean[:, :128], squares[:, :128]),
+        (far, mean[:, 128:], squares[:, 128:]),
+    ):
+        send(at, m)
+        send(4 + at, q)
 
 
 def k2(pt_ref, wall_ref, st_ref, w2_hbm, mix_ref, so_ref, a_ref, w2_ref, y_ref, sem):
@@ -284,9 +294,9 @@
         product(STRIDE * b, OWN + 32, (b, 0), (b, 2))
         part = y_ref[15 : 15 + OWN, :128] + y_ref[17 : 17 + OWN, 128:]
         mix_ref[...] = part if b == 0 else mix_ref[...] + part
-    product(16, SPAN, (0, 1), (2, 1))
-    mix_ref[...] += y_ref[0:OWN, :128] + y_ref[2 * STRIDE : 2 * STRIDE + OWN, 128:]
-    product(16 + STRIDE, OWN, (1, 1))
+    product(16, OWN + STRIDE, (0, 1), (1, 1))
+    mix_ref[...] += y_ref[0:OWN, :128] + y_ref[STRIDE : STRIDE + OWN, 128:]
+    product(16 + 2 * STRIDE, OWN, (2, 1))
     v = (mix_ref[...] + y_ref[0:OWN, :128]).reshape(ROWS, STRIDE, 128)
     mix_ref[...] = v.reshape(OWN, 128)
     ok = lax.broadcasted_iota(jnp.int32, (ROWS, STRIDE, 128), 1) < W
@@ -344,45 +354,14 @@
     )(*[pltpu.with_memory_space_constraint(v, pltpu.HBM) for v in arrays])
 
 
-def call_k1t(g):
+def call(kernel, name, outs, *arrays):
     return pl.pallas_call(
-        k1t,
-        out_shape=shape((16 * FRAMES, 384), jnp.bfloat16),
-        in_specs=[INVMEM],
-        out_specs=INVMEM,
+        kernel,
+        out_shape=tuple(shape(*out) for out in outs),
+        in_specs=[INVMEM] * len(arrays),
+        out_specs=(INVMEM,) * len(outs),
         compiler_params=pltpu.CompilerParams(vmem_limit_bytes=VMEM),
-        name="k1t",
-    )(g)
-
-
-def call_k1w(*arrays):
-    return pl.pallas_call(
-        k1w,
-        out_shape=(
-            shape((EDGE + 3 * 64, 128), jnp.bfloat16),
-            shape((16 * FRAMES, XLANES), jnp.bfloat16),
-        ),
-        in_specs=[INVMEM] * 4,
-        out_specs=(INVMEM,) * 2,
-        scratch_shapes=[pltpu.VMEM((16 * FRAMES, 384), jnp.bfloat16)],
-        compiler_params=pltpu.CompilerParams(vmem_limit_bytes=VMEM),
-        name="k1w",
-    )(*arrays)
-
-
-def call_k1(*arrays):
-    return pl.pallas_call(
-        k1,
-        out_shape=(
-            shape((6 * TAPS, SPAN), jnp.bfloat16),
-            shape((4, HELD, 128), jnp.bfloat16),
-            shape((16, 8, 128), jnp.float32),
-        ),
-        in_specs=[INVMEM] * 4,
-        out_specs=(INVMEM,) * 3,
-        scratch_shapes=[pltpu.VMEM((16 * FRAMES, XLANES), jnp.bfloat16)],
-        compiler_params=pltpu.CompilerParams(vmem_limit_bytes=VMEM),
-        name="k1",
+        name=name,
     )(*arrays)
 
 
@@ -422,10 +401,17 @@
     side = lax.ppermute(held, ("row", "ch"), sides)
     fars = [(4 * (i ^ 8) + (j + 2) % 4, 4 * i + j) for i in range(16) for j in range(4)]
     far = lax.ppermute(half, ("row", "ch"), fars)
-    edge = lax.ppermute(call_k1t(g), "row", [(i, i + 2 * (i % 2) - 1) for i in range(1, 15)])
-    mine, x = call_k1w(g, side, far, edge)
-    other = lax.ppermute(mine, "row", [(i, i ^ 1) for i in range(16)])
-    pt, wall, st = call_k1(x, held, mine, other)
+    cores = [(i, i ^ 1) for i in range(16)]
+    edge = ((16 * FRAMES, 384), jnp.bfloat16)
+    to_next, to_mate = call(k1t, "k1t", [edge] * 2, g)
+    to_next = lax.ppermute(to_next, "row", [(i, i + 2 * (i % 2) - 1) for i in range(1, 15)])
+    to_mate = lax.ppermute(to_mate, "row", cores)
+    both = ((HELD + HALF, 128), jnp.bfloat16)
+    mine, x = call(k1w, "k1w", [both, ((16 * FRAMES, XLANES), jnp.bfloat16)], g, side, far, to_next, to_mate)
+    other = lax.ppermute(mine, "row", cores)
+    pt, near = call(k1p, "k1p", [((6 * TAPS, SPAN), jnp.bfloat16), ((8, 128), jnp.float32)], x, held, side)
+    outs = [((4, HELD, 128), jnp.bfloat16), ((16, 8, 128), jnp.float32)]
+    wall, st = call(k1q, "k1q", outs, pt, near, held, mine, other)
     st = lax.all_to_all(st, "row", 0, 0)
     mix, st = call_k2(pt, wall, st, mid_weight)
     st = lax.all_to_all(st, ("frm", "row"), 0, 0)

time: 69.3 us -> 67.7 us (0.977)
  waiting for transfers between devices: 7.8 us -> 6.24 us
    ppermute x2 -> x3, waiting for transfers between devices: 3.2 us -> 1.64 us  [the longest x1 1.64 us: per_device(): lax.ppermute(to_next, 'row', [(i, i + 2 * (i % 2) - 1) for i in range(1,...]
    ppermute x2 -> x3, starting transfers between devices: 6.49 us -> 6.59 us  [the longest x1 6.41 us: per_device(): lax.ppermute(to_next, 'row', [(i, i + 2 * (i % 2) - 1) for i in range(1,...]
    pallas_call x3 -> x4, Pallas kernels: 3.88 us -> 3.97 us  [call(): pl.pallas_call(kernel, out_shape=tuple((shape(*out) for out in outs)), in...]
  transfers between devices with their start and end apart: 5 -> 6, of which waited for: 3 -> 2; matrix products, arithmetic and copies ran while one was open for 0% -> 0% of each run, Pallas kernels for 0% -> 3%
where the time goes in v5:
time: 67.7 us; the launch traced here: 67.4 us
  blocking collectives  24.1 us (36%)
  starting transfers between devices  23.3 us (34%)
  Pallas kernels  13.7 us (20%)
  waiting for transfers between devices  6.24 us (9%)
    all_to_all x1, blocking collectives, per_device(): st = lax.all_to_all(st, ('frm', 'row'), 0, 0)  13.3 us
    all_to_all x1, starting transfers between devices, per_device(): g = lax.all_to_all(payload, ('frm', 'ch'), 0, 0)  11.6 us
    all_to_all x1, blocking collectives, per_device(): st = lax.all_to_all(st, 'row', 0, 0)  10.8 us
    pallas_call x1, Pallas kernels, call_k2(): pl.pallas_call(k2, out_shape=(shape((OWN, 128), jnp.float32), shape((64,...  6.89 us
    ppermute x1, starting transfers between devices, per_device(): lax.ppermute(to_next, 'row', [(i, i + 2 * (i % 2) - 1) for i in range(1,...  6.41 us
    all_to_all x1, waiting for transfers between devices, per_device(): g = lax.all_to_all(payload, ('frm', 'ch'), 0, 0)  4.59 us
    pallas_call x4, Pallas kernels, call(): pl.pallas_call(kernel, out_shape=tuple((shape(*out) for out in outs)), in...  3.97 us
    ppermute x1, starting transfers between devices, per_device(): far = lax.ppermute(half, ('row', 'ch'), fars)  2.85 us
  transfers between devices with their start and end apart: 6, of which 2 were waited for; matrix products, arithmetic and copies ran while one was open for 0% of the time, Pallas kernels for 3%

profile of v5, /device:TPU:1, one launch (start us, length us, event | category | flops | bytes accessed | tf_op | source)
XLA Modules:
  0.0 67.4 jit_solution(13862827127237421206)
XLA Ops:
  0.0 1.6 %k0.1 = (bf16[16,16,255]{2,1,0:T(8,128)(2,1)}, bf16[448,128]{1,0:T(8,128)(2,1)S(1)}, bf16[224,128]{1,0:T(8,128)(2,1)S(1)}, f32[2,1,128]{2,1,0:T(1,128)S(1)}) custom-call(bf16[16,255]{1,0:T(8,128)(2,1)} %bitcast.7, bf16[432,128]{1,0:T(8,128)(2,1)} %bitcast.6, f32[1,128]{1,0:T(1,128)} %bitcast.8, f32[1,128]{1,0:T(1,128)} %bitcast.9, f32[1,128]{1,0:T(1,128)} %bitcast.10, ...), custom_call_target="tpu_custom_call" | custom-call | tf_op jit(solution)/shard_map/k0/pallas_call | solution.py:337
  1.6 11.6 %all-to-all-start = ((bf16[16,16,255]{2,1,0:T(8,128)(2,1)}), bf16[16,16,255]{2,1,0:T(8,128)(2,1)S(1)}, u32[]{:S(2)}, u32[]{:S(2)}) async-start(bf16[16,16,255]{2,1,0:T(8,128)(2,1)} %get-tuple-element.19), calls=%async_computation | async-start | bytes 262144 | tf_op jit(solution)/shard_map/all_to_all | solution.py:399
  13.2 2.3 %collective-permute-start = (bf16[448,128]{1,0:T(8,128)(2,1)S(1)}, bf16[448,128]{1,0:T(8,128)(2,1)S(1)}, u32[]{:S(2)}, u32[]{:S(2)}) collective-permute-start(bf16[448,128]{1,0:T(8,128)(2,1)S(1)} %get-tuple-element.20.held_ref), channel_id=1, source_target_pairs={{1,0},{2,1},{3,2},{0,3},{7,4},{4,5},{5,6},{6,7},{9,8},{10,9},{11,1... | collective-permute-start | bytes 344072 | tf_op jit(solution)/shard_map/ppermute | solution.py:401
  15.5 2.8 %collective-permute-start.1 = (bf16[224,128]{1,0:T(8,128)(2,1)S(1)}, bf16[224,128]{1,0:T(8,128)(2,1)S(1)}, u32[]{:S(2)}, u32[]{:S(2)}) collective-permute-start(bf16[224,128]{1,0:T(8,128)(2,1)S(1)} %get-tuple-element.21), channel_id=1, source_target_pairs={{34,0},{35,1},{32,2},{33,3},{38,4},{39,5},{36,6},{37,7},{42,8},{43... | collective-permute-start | bytes 172040 | tf_op jit(solution)/shard_map/ppermute | solution.py:403
  18.4 4.6 %all-to-all-done.g_ref = bf16[16,16,255]{2,1,0:T(8,128)(2,1)S(1)} async-done(((bf16[16,16,255]{2,1,0:T(8,128)(2,1)}), bf16[16,16,255]{2,1,0:T(8,128)(2,1)S(1)}, u32[]{:S(2)}, u32[]{:S(2)}) %all-to-all-start) | async-done | bytes 130592 | tf_op jit(solution)/shard_map/all_to_all | solution.py:399
  23.0 0.1 k1t.1
  23.1 6.4 %collective-permute-start.2 = (bf16[64,384]{1,0:T(8,128)(2,1)S(1)}, bf16[64,384]{1,0:T(8,128)(2,1)S(1)}, u32[]{:S(2)}, u32[]{:S(2)}) collective-permute-start(bf16[64,384]{1,0:T(8,128)(2,1)S(1)} %get-tuple-element.22), channel_id=1, source_target_pairs={{4,8},{8,4},{12,16},{16,12},{20,24},{24,20},{28,32},{32,28},{36,40... | collective-permute-start | bytes 147464 | tf_op jit(solution)/shard_map/ppermute | solution.py:407
  29.5 0.1 collective-permute-start.3
  29.6 0.0 collective-permute-done.1.far_ref
  29.6 0.0 collective-permute-done.side_ref
  29.6 1.6 %collective-permute-done.2.next_ref = bf16[64,384]{1,0:T(8,128)(2,1)S(1)} collective-permute-done((bf16[64,384]{1,0:T(8,128)(2,1)S(1)}, bf16[64,384]{1,0:T(8,128)(2,1)S(1)}, u32[]{:S(2)}, u32[]{:S(2)}) %collective-permute-start.2) | collective-permute-done | bytes 49184 | tf_op jit(solution)/shard_map/ppermute | solution.py:407
  31.3 0.0 collective-permute-done.3.mate_ref
  31.3 0.2 k1w.1
  31.4 0.1 collective-permute-start.4
  31.5 2.2 %k1p.1 = (bf16[864,1408]{1,0:T(8,128)(2,1)S(1)}, f32[8,128]{1,0:T(8,128)S(1)}) custom-call(bf16[64,2048]{1,0:T(8,128)(2,1)S(1)} %get-tuple-element.24.x_ref, bf16[448,128]{1,0:T(8,128)(2,1)S(1)} %get-tuple-element.20.held_ref, bf16[448,128]{1,0:T(8,128)(2,1)S(1)} %collective-permute-done.side_ref), custom_call_target="tpu_custom_call" | custom-call | tf_op jit(solution)/shard_map/k1p/pallas_call | solution.py:358
  33.8 0.0 collective-permute-done.4.other_ref
  33.8 1.5 %k1q.1 = (bf16[4,448,128]{2,1,0:T(8,128)(2,1)S(1)}, f32[16,8,128]{2,1,0:T(8,128)S(1)}) custom-call(bf16[864,1408]{1,0:T(8,128)(2,1)S(1)} %get-tuple-element.25.pt_ref, f32[8,128]{1,0:T(8,128)S(1)} %get-tuple-element.26.near_ref, bf16[448,128]{1,0:T(8,128)(2,1)S(1)} %get-tuple-element.20.held_ref, bf16[672,128]{1,0:T(8,128)(2,1)S(1)} %get-tuple-element.27.mine_ref, ...), custom_call_target="tpu_custom_call" | custom-call | tf_op jit(solution)/shard_map/k1q/pallas_call | solution.py:358
  35.2 10.8 %all_to_all.15.st_ref = f32[16,8,128]{2,1,0:T(8,128)S(1)} all-to-all(f32[16,8,128]{2,1,0:T(8,128)S(1)} %get-tuple-element.29), channel_id=1, replica_groups=mesh['frm'=4,'row'=16,'ch'=4] {'row'}, dimensions={0} | all-to-all | bytes 131072 | tf_op jit(solution)/shard_map/all_to_all | solution.py:415
  46.0 6.9 %k2.1 = (f32[1056,128]{1,0:T(8,128)S(1)}, f32[64,2,128]{2,1,0:T(2,128)S(1)}) custom-call(bf16[864,1408]{1,0:T(8,128)(2,1)S(1)} %get-tuple-element.25.pt_ref, bf16[4,448,128]{2,1,0:T(8,128)(2,1)S(1)} %get-tuple-element.28.wall_ref, f32[16,8,128]{2,1,0:T(8,128)S(1)} %all_to_all.15.st_ref, bf16[27,512,128]{2,1,0:T(8,128)(2,1)} %w2_hbm.1), custom_call_target="tpu_custom_call" | custom-call | tf_op jit(solution)/shard_map/k2/pallas_call | solution.py:369
  52.9 13.3 %all_to_all.16.st_ref = f32[64,2,128]{2,1,0:T(2,128)S(1)} all-to-all(f32[64,2,128]{2,1,0:T(2,128)S(1)} %get-tuple-element.31), channel_id=1, replica_groups=mesh['frm'=4,'row'=16,'ch'=4] {'frm','row'}, dimensions={0} | all-to-all | bytes 131072 | tf_op jit(solution)/shard_map/all_to_all | solution.py:417
  66.2 1.2 %k3.1 = bf16[1,6,170,128]{3,2,1,0:T(8,128)(2,1)} custom-call(f32[1056,128]{1,0:T(8,128)S(1)} %get-tuple-element.30.mix_ref, f32[64,2,128]{2,1,0:T(2,128)S(1)} %all_to_all.16.st_ref, f32[2,1,128]{2,1,0:T(1,128)S(1)} %get-tuple-element.32.par_ref), custom_call_target="tpu_custom_call" | custom-call | tf_op jit(solution)/shard_map/k3/pallas_call | solution.py:386
Async XLA Ops:
  1.6 21.3 %all-to-all-start = ((bf16[16,16,255]{2,1,0:T(8,128)(2,1)}), bf16[16,16,255]{2,1,0:T(8,128)(2,1)S(1)}, u32[]{:S(2)}, u32[]{:S(2)}) async-start(bf16[16,16,255]{2,1,0:T(8,128)(2,1)} %get-tuple-element.19), calls=%async_computation | async-start | bytes 262144 | tf_op jit(solution)/shard_map/all_to_all | solution.py:399
  13.2 16.4 %collective-permute-start = (bf16[448,128]{1,0:T(8,128)(2,1)S(1)}, bf16[448,128]{1,0:T(8,128)(2,1)S(1)}, u32[]{:S(2)}, u32[]{:S(2)}) collective-permute-start(bf16[448,128]{1,0:T(8,128)(2,1)S(1)} %get-tuple-element.20.held_ref), channel_id=1, source_target_pairs={{1,0},{2,1},{3,2},{0,3},{7,4},{4,5},{5,6},{6,7},{9,8},{10,9},{11,1... | collective-permute-start | bytes 344072 | tf_op jit(solution)/shard_map/ppermute | solution.py:401
  15.5 14.1 %collective-permute-start.1 = (bf16[224,128]{1,0:T(8,128)(2,1)S(1)}, bf16[224,128]{1,0:T(8,128)(2,1)S(1)}, u32[]{:S(2)}, u32[]{:S(2)}) collective-permute-start(bf16[224,128]{1,0:T(8,128)(2,1)S(1)} %get-tuple-element.21), channel_id=1, source_target_pairs={{34,0},{35,1},{32,2},{33,3},{38,4},{39,5},{36,6},{37,7},{42,8},{43... | collective-permute-start | bytes 172040 | tf_op jit(solution)/shard_map/ppermute | solution.py:403
  23.1 8.2 %collective-permute-start.2 = (bf16[64,384]{1,0:T(8,128)(2,1)S(1)}, bf16[64,384]{1,0:T(8,128)(2,1)S(1)}, u32[]{:S(2)}, u32[]{:S(2)}) collective-permute-start(bf16[64,384]{1,0:T(8,128)(2,1)S(1)} %get-tuple-element.22), channel_id=1, source_target_pairs={{4,8},{8,4},{12,16},{16,12},{20,24},{24,20},{28,32},{32,28},{36,40... | collective-permute-start | bytes 147464 | tf_op jit(solution)/shard_map/ppermute | solution.py:407
  29.5 1.8 %collective-permute-start.3 = (bf16[64,384]{1,0:T(8,128)(2,1)S(1)}, bf16[64,384]{1,0:T(8,128)(2,1)S(1)}, u32[]{:S(2)}, u32[]{:S(2)}) collective-permute-start(bf16[64,384]{1,0:T(8,128)(2,1)S(1)} %get-tuple-element.23), channel_id=1, source_target_pairs={{0,4},{4,0},{8,12},{12,8},{16,20},{20,16},{24,28},{28,24},{32,36},... | collective-permute-start | bytes 147464 | tf_op jit(solution)/shard_map/ppermute | solution.py:408
  31.4 2.3 %collective-permute-start.4 = (bf16[672,128]{1,0:T(8,128)(2,1)S(1)}, bf16[672,128]{1,0:T(8,128)(2,1)S(1)}, u32[]{:S(2)}, u32[]{:S(2)}) collective-permute-start(bf16[672,128]{1,0:T(8,128)(2,1)S(1)} %get-tuple-element.27.mine_ref), channel_id=1, source_target_pairs={{0,4},{4,0},{8,12},{12,8},{16,20},{20,16},{24,28},{28,24},{32,36},... | collective-permute-start | bytes 516104 | tf_op jit(solution)/shard_map/ppermute | solution.py:411

commit v6 on v5

--- a/solution.py
+++ b/solution.py
@@ -19,8 +19,8 @@
 TAPS = 9 * C_LAT
 LEAD = 128
 XLANES = 2048
-K1_CHUNKS = ((128, 640), (768, 512))
-CHUNKS = ((0, 384), (384, 384), (768, 384), (1152, 256))
+MID = (384, 640)
+SIDES = 384
 CELLS = ROWS * W
 TAPROWS = 27 * C_LAT
 HELD = 448
@@ -63,14 +63,20 @@
     return [high, mid, v - high - mid]
 
 
-def k0(tokens_hbm, w_hbm, p0, p1, p2, p3, out_ref, held_ref, half_ref, par_ref, tokens_ref, in_ref, sems):
+def k0(tokens_hbm, out_ref, tokens_ref, sem):
+    copy = pltpu.make_async_copy(tokens_hbm, tokens_ref, sem)
+    copy.start()
+    copy.wait()
+    out_ref[...] = jnp.broadcast_to(tokens_ref[...][None], (16, C_LAT, 255))
+
+
+def k0w(w_hbm, p0, p1, p2, p3, held_ref, half_ref, par_ref, in_ref, sems):
     copies = [
-        pltpu.make_async_copy(tokens_hbm, tokens_ref, sems.at[0]),
-        pltpu.make_async_copy(w_hbm, held_ref.at[:TAPROWS], sems.at[1]),
-        pltpu.make_async_copy(p0, in_ref.at[0], sems.at[2]),
-        pltpu.make_async_copy(p1, in_ref.at[1], sems.at[3]),
-        pltpu.make_async_copy(p2, par_ref.at[0], sems.at[4]),
-        pltpu.make_async_copy(p3, par_ref.at[1], sems.at[5]),
+        pltpu.make_async_copy(w_hbm, held_ref.at[:TAPROWS], sems.at[0]),
+        pltpu.make_async_copy(p0, in_ref.at[0], sems.at[1]),
+        pltpu.make_async_copy(p1, in_ref.at[1], sems.at[2]),
+        pltpu.make_async_copy(p2, par_ref.at[0], sems.at[3]),
+        pltpu.make_async_copy(p3, par_ref.at[1], sems.at[4]),
     ]
     for copy in copies:
         copy.start()
@@ -80,7 +86,6 @@
     held_ref[TAPROWS:, :] = jnp.concatenate(rows, axis=0).astype(jnp.bfloat16)
     start = pl.multiple_of(lax.rem(lax.axis_index("row"), 2) * HALF, 16)
     half_ref[...] = held_ref[pl.ds(start, HALF), :]
-    out_ref[...] = jnp.broadcast_to(tokens_ref[...][None], (16, C_LAT, 255))
 
 
 def first_rows(g_ref, f):
@@ -113,24 +118,8 @@
         write_edge(first_rows, g_ref, mate_ref)
 
 
-def k1w(g_ref, side_ref, far_ref, next_ref, mate_ref, both_ref, x_ref):
-    both_ref[:HELD] = side_ref[...]
-    both_ref[HELD:] = far_ref[...]
+def k1i(g_ref, held_ref, side_ref, x_ref, mid_ref, acc_ref):
     x_ref[...] = jnp.zeros_like(x_ref)
-    core = lax.rem(lax.axis_index("row"), 2)
-
-    def edges(above_ref, below_ref):
-        x_ref[:, LEAD : LEAD + 2 * STRIDE] = above_ref[:, : 2 * STRIDE]
-        x_ref[:, LEAD + 8 * STRIDE : LEAD + 10 * STRIDE] = below_ref[:, : 2 * STRIDE]
-
-    @pl.when(core == 0)
-    def _():
-        edges(next_ref, mate_ref)
-
-    @pl.when(core == 1)
-    def _():
-        edges(mate_ref, next_ref)
-
     plan = (
         ((0, 0, 170),),
         ((0, 170, 255), (1, 0, 85)),
@@ -146,6 +135,41 @@
             for j, lo, hi in parts:
                 x_ref[at, lane : lane + hi - lo] = g_ref[4 * f + j, :, lo:hi]
                 lane += hi - lo
+    mid_ref[: 2 * TAPS, :] = jnp.zeros((2 * TAPS, MID[1]), jnp.bfloat16)
+    patches(x_ref, mid_ref, 0, *MID)
+    weight = jnp.concatenate([held_ref[:TAPROWS], side_ref[:TAPROWS]], axis=1)
+    pilot, s1, s2 = moments(weight, ((mid_ref, 0, *MID),))
+    acc_ref[0:8] = s1
+    acc_ref[8:16] = s2
+    acc_ref[16:24] = jnp.broadcast_to(pilot, (8, 256))
+
+
+def k1w(x_in_ref, side_ref, far_ref, next_ref, mate_ref, both_ref, x_ref):
+    both_ref[:HELD] = side_ref[...]
+    both_ref[HELD:] = far_ref[...]
+    x_ref[...] = x_in_ref[...]
+    core = lax.rem(lax.axis_index("row"), 2)
+
+    def edges(above_ref, below_ref):
+        x_ref[:, LEAD : LEAD + 2 * STRIDE] = above_ref[:, : 2 * STRIDE]
+        x_ref[:, LEAD + 8 * STRIDE : LEAD + 10 * STRIDE] = below_ref[:, : 2 * STRIDE]
+
+    @pl.when(core == 0)
+    def _():
+        edges(next_ref, mate_ref)
+
+    @pl.when(core == 1)
+    def _():
+        edges(mate_ref, next_ref)
+
+
+def patches(x_ref, out_ref, lane, lo, size):
+    for f in range(FRAMES):
+        for b in range(3):
+            for e in range(3):
+                at = (f + 2) * TAPS + (3 * b + e) * 16
+                start = LEAD + lo + STRIDE * b + e - 1
+                out_ref[at : at + 16, lane : lane + size] = x_ref[16 * f : 16 * f + 16, start : start + size]
 
 
 def valid(lo, size):
@@ -158,14 +182,14 @@
     return ok
 
 
-def moments(pt_ref, weight):
+def moments(weight, chunks, carry=None):
     lanes = weight.shape[1]
-    pilot = None
-    s1 = s2 = jnp.zeros((8, lanes), jnp.float32)
+    zero = jnp.zeros((8, lanes), jnp.float32)
+    pilot, s1, s2 = carry or (None, zero, zero)
     for g in range(FRAMES):
-        for lo, size in K1_CHUNKS:
+        for ref, lane, lo, size in chunks:
             h = lax.dot_general(
-                pt_ref[max(g, 2) * TAPS : (g + 3) * TAPS, lo : lo + size],
+                ref[max(g, 2) * TAPS : (g + 3) * TAPS, lane : lane + size],
                 weight[max(2 - g, 0) * TAPS :],
                 (((0,), (0,)), ((), ())),
                 preferred_element_type=jnp.float32,
@@ -177,28 +201,33 @@
             d = jnp.where(ok, h - pilot, 0.0).reshape(size // 8, 8, lanes)
             s1 = s1 + jnp.sum(d, axis=0)
             s2 = s2 + jnp.sum(d * d, axis=0)
+    return pilot, s1, s2
+
+
+def centred(pilot, s1, s2):
     s1 = jnp.sum(s1, axis=0, keepdims=True)
     s2 = jnp.sum(s2, axis=0, keepdims=True)
     d = s1 / (FRAMES * CELLS)
     return pilot + d, s2 - s1 * d
 
 
-def k1p(x_ref, held_ref, side_ref, pt_ref, near_ref):
-    pt_ref[: 2 * TAPS, :] = jnp.zeros((2 * TAPS, SPAN), jnp.bfloat16)
-    for f in range(FRAMES):
-        for b in range(3):
-            for e in range(3):
-                at = (f + 2) * TAPS + (3 * b + e) * 16
-                lane = LEAD + STRIDE * b + e - 1
-                pt_ref[at : at + 16, :] = x_ref[16 * f : 16 * f + 16, lane : lane + SPAN]
-    mean, squares = moments(pt_ref, jnp.concatenate([held_ref[:TAPROWS], side_ref[:TAPROWS]], axis=1))
+def outer(ref):
+    return ((ref, 128, 128, 256), (ref, SIDES, SPAN - SIDES, 256))
+
+
+def k1p(x_ref, held_ref, side_ref, acc_ref, out_ref, near_ref):
+    out_ref[: 2 * TAPS, :] = jnp.zeros((2 * TAPS, 2 * SIDES), jnp.bfloat16)
+    patches(x_ref, out_ref, 0, 0, SIDES)
+    patches(x_ref, out_ref, SIDES, SPAN - SIDES, SIDES)
+    weight = jnp.concatenate([held_ref[:TAPROWS], side_ref[:TAPROWS]], axis=1)
+    mean, squares = centred(*moments(weight, outer(out_ref), (acc_ref[16:17], acc_ref[0:8], acc_ref[8:16])))
     for i in range(2):
         near_ref[i : i + 1] = mean[:, 128 * i : 128 * (i + 1)]
         near_ref[2 + i : 3 + i] = squares[:, 128 * i : 128 * (i + 1)]
     near_ref[4:] = jnp.zeros((4, 128), jnp.float32)
 
 
-def k1q(pt_ref, near_ref, held_ref, mine_ref, other_ref, wall_ref, st_ref):
+def k1q(mid_ref, out_ref, near_ref, held_ref, mine_ref, other_ref, wall_ref, st_ref):
     c, core = lax.axis_index("ch"), lax.rem(lax.axis_index("row"), 2)
     side, side_x, far = (lax.rem(c + i, 4) for i in (1 + 2 * core, 3 - 2 * core, 2))
     wall_ref[c] = held_ref[...]
@@ -206,7 +235,8 @@
     wall_ref[side_x] = other_ref[:HELD, :]
     wall_ref[far, pl.ds(pl.multiple_of(core * HALF, 16), HALF), :] = mine_ref[HELD:, :]
     wall_ref[far, pl.ds(pl.multiple_of((1 - core) * HALF, 16), HALF), :] = other_ref[HELD:, :]
-    mean, squares = moments(pt_ref, jnp.concatenate([other_ref[:TAPROWS], wall_ref[far][:TAPROWS]], axis=1))
+    weight = jnp.concatenate([other_ref[:TAPROWS], wall_ref[far][:TAPROWS]], axis=1)
+    mean, squares = centred(*moments(weight, ((mid_ref, 0, *MID), *outer(out_ref))))
 
     def send(at, v):
         st_ref[:, pl.ds(at, 1), :] = jnp.broadcast_to(v[None], (16, 1, 128))
@@ -221,7 +251,7 @@
         send(4 + at, q)
 
 
-def k2(pt_ref, wall_ref, st_ref, w2_hbm, mix_ref, so_ref, a_ref, w2_ref, y_ref, sem):
+def k2(mid_ref, out_ref, wall_ref, st_ref, w2_hbm, mix_ref, so_ref, a_ref, w2_ref, y_ref, sem):
     copy = pltpu.make_async_copy(w2_hbm, w2_ref, sem)
     copy.start()
     f, r = lax.axis_index("frm"), lax.axis_index("row")
@@ -253,9 +283,13 @@
         @pl.when(g >= 0)
         def _():
             at = pl.multiple_of(g * TAPS, 16)
-            for lo, size in CHUNKS:
+            for ref, lane, lo, size in (
+                (out_ref, 0, 0, SIDES),
+                (mid_ref, 0, *MID),
+                (out_ref, SIDES, SPAN - SIDES, SIDES),
+            ):
                 h = lax.dot_general(
-                    pt_ref[pl.ds(at, 3 * TAPS), lo : lo + size],
+                    ref[pl.ds(at, 3 * TAPS), lane : lane + size],
                     weight,
                     (((0,), (0,)), ((), ())),
                     preferred_element_type=jnp.float32,
@@ -333,25 +367,36 @@
 INVMEM = pl.BlockSpec(memory_space=pltpu.VMEM)
 
 
-def call_k0(*arrays):
+def in_hbm(v):
+    return pltpu.with_memory_space_constraint(v, pltpu.HBM)
+
+
+def call_k0(tokens):
     return pl.pallas_call(
         k0,
+        out_shape=shape((16, C_LAT, 255), jnp.bfloat16),
+        in_specs=[INHBM],
+        out_specs=INVMEM,
+        scratch_shapes=[pltpu.VMEM((C_LAT, 255), jnp.bfloat16), pltpu.SemaphoreType.DMA],
+        compiler_params=pltpu.CompilerParams(vmem_limit_bytes=VMEM),
+        name="k0",
+    )(in_hbm(tokens))
+
+
+def call_k0w(*arrays):
+    return pl.pallas_call(
+        k0w,
         out_shape=(
-            shape((16, C_LAT, 255), jnp.bfloat16),
             shape((HELD, 128), jnp.bfloat16),
             shape((HALF, 128), jnp.bfloat16),
             shape((2, 1, 128), jnp.float32),
         ),
-        in_specs=[INHBM] * 6,
-        out_specs=(INVMEM,) * 4,
-        scratch_shapes=[
-            pltpu.VMEM((C_LAT, 255), jnp.bfloat16),
-            pltpu.VMEM((2, 1, 128), jnp.float32),
-            pltpu.SemaphoreType.DMA((6,)),
-        ],
+        in_specs=[INHBM] * 5,
+        out_specs=(INVMEM,) * 3,
+        scratch_shapes=[pltpu.VMEM((2, 1, 128), jnp.float32), pltpu.SemaphoreType.DMA((5,))],
         compiler_params=pltpu.CompilerParams(vmem_limit_bytes=VMEM),
-        name="k0",
-    )(*[pltpu.with_memory_space_constraint(v, pltpu.HBM) for v in arrays])
+        name="k0w",
+    )(*[in_hbm(v) for v in arrays])
 
 
 def call(kernel, name, outs, *arrays):
@@ -365,11 +410,11 @@
     )(*arrays)
 
 
-def call_k2(pt, wall, st, w2):
+def call_k2(*arrays):
     return pl.pallas_call(
         k2,
         out_shape=(shape((OWN, 128), jnp.float32), shape((64, 2, 128), jnp.float32)),
-        in_specs=[INVMEM] * 3 + [INHBM],
+        in_specs=[INVMEM] * 4 + [INHBM],
         out_specs=(INVMEM,) * 2,
         scratch_shapes=[
             pltpu.VMEM((SPAN + 32, 3 * CH), jnp.bfloat16),
@@ -379,7 +424,7 @@
         ],
         compiler_params=pltpu.CompilerParams(vmem_limit_bytes=VMEM),
         name="k2",
-    )(pt, wall, st, pltpu.with_memory_space_constraint(w2, pltpu.HBM))
+    )(*arrays[:4], in_hbm(arrays[4]))
 
 
 def call_k3(mix, st, par):
@@ -395,8 +440,8 @@
 
 def per_device(latents, in_weight, in_gain, in_shift, mid_weight, mid_gain, mid_shift):
     params = [v.reshape(1, 128) for v in (in_gain, in_shift, mid_gain, mid_shift)]
-    payload, held, half, par = call_k0(latents.T, in_weight.reshape(TAPROWS, 128), *params)
-    g = lax.all_to_all(payload, ("frm", "ch"), 0, 0)
+    g = lax.all_to_all(call_k0(latents.T), ("frm", "ch"), 0, 0)
+    held, half, par = call_k0w(in_weight.reshape(TAPROWS, 128), *params)
     sides = [(4 * i + (j + 1 + 2 * (i % 2)) % 4, 4 * i + j) for i in range(16) for j in range(4)]
     side = lax.ppermute(held, ("row", "ch"), sides)
     fars = [(4 * (i ^ 8) + (j + 2) % 4, 4 * i + j) for i in range(16) for j in range(4)]
@@ -406,14 +451,17 @@
     to_next, to_mate = call(k1t, "k1t", [edge] * 2, g)
     to_next = lax.ppermute(to_next, "row", [(i, i + 2 * (i % 2) - 1) for i in range(1, 15)])
     to_mate = lax.ppermute(to_mate, "row", cores)
-    both = ((HELD + HALF, 128), jnp.bfloat16)
-    mine, x = call(k1w, "k1w", [both, ((16 * FRAMES, XLANES), jnp.bfloat16)], g, side, far, to_next, to_mate)
+    own = ((16 * FRAMES, XLANES), jnp.bfloat16)
+    outs = [own, ((6 * TAPS, MID[1]), jnp.bfloat16), ((24, 256), jnp.float32)]
+    x, mid, acc = call(k1i, "k1i", outs, g, held, side)
+    mine, x = call(k1w, "k1w", [((HELD + HALF, 128), jnp.bfloat16), own], x, side, far, to_next, to_mate)
     other = lax.ppermute(mine, "row", cores)
-    pt, near = call(k1p, "k1p", [((6 * TAPS, SPAN), jnp.bfloat16), ((8, 128), jnp.float32)], x, held, side)
+    outs = [((6 * TAPS, 2 * SIDES), jnp.bfloat16), ((8, 128), jnp.float32)]
+    outer_patches, near = call(k1p, "k1p", outs, x, held, side, acc)
     outs = [((4, HELD, 128), jnp.bfloat16), ((16, 8, 128), jnp.float32)]
-    wall, st = call(k1q, "k1q", outs, pt, near, held, mine, other)
+    wall, st = call(k1q, "k1q", outs, mid, outer_patches, near, held, mine, other)
     st = lax.all_to_all(st, "row", 0, 0)
-    mix, st = call_k2(pt, wall, st, mid_weight)
+    mix, st = call_k2(mid, outer_patches, wall, st, mid_weight)
     st = lax.all_to_all(st, ("frm", "row"), 0, 0)
     return call_k3(mix, st, par)
 

time: 67.7 us -> 66 us (0.975)
  waiting for transfers between devices: 6.24 us -> 3.48 us
  Pallas kernels: 13.7 us -> 15 us
    ppermute x1, waiting for transfers between devices: 1.64 us -> 0.01 us  [per_device(): lax.ppermute(to_next, 'row', [(i, i + 2 * (i % 2) - 1) for i in range(1,...]
    all_to_all x1, waiting for transfers between devices: 4.59 us -> 3.47 us  [per_device(): g = lax.all_to_all(call_k0(latents.T), ('frm', 'ch'), 0, 0)]
    pallas_call x1 -> x2, Pallas kernels: 1.64 us -> 2.34 us  [the longest x1 1.37 us: call_k0(): pl.pallas_call(k0, out_shape=shape((16, C_LAT, 255), jnp.bfloat16), in_sp...]
    pallas_call x4 -> x5, Pallas kernels: 3.97 us -> 4.56 us  [call(): pl.pallas_call(kernel, out_shape=tuple((shape(*out) for out in outs)), in...]
  transfers between devices with their start and end apart: 6 -> 6, of which waited for: 2 -> 1; matrix products, arithmetic and copies ran while one was open for 0% -> 0% of each run, Pallas kernels for 3% -> 6%
where the time goes in v6:
time: 66 us; the launch traced here: 65.7 us
  blocking collectives  23.8 us (36%)
  starting transfers between devices  23.3 us (35%)
  Pallas kernels  15 us (23%)
  waiting for transfers between devices  3.48 us (5%)
    all_to_all x1, blocking collectives, per_device(): st = lax.all_to_all(st, ('frm', 'row'), 0, 0)  13.5 us
    all_to_all x1, starting transfers between devices, per_device(): g = lax.all_to_all(call_k0(latents.T), ('frm', 'ch'), 0, 0)  11.6 us
    all_to_all x1, blocking collectives, per_device(): st = lax.all_to_all(st, 'row', 0, 0)  10.3 us
    pallas_call x1, Pallas kernels, call_k2(): pl.pallas_call(k2, out_shape=(shape((OWN, 128), jnp.float32), shape((64,...  6.9 us
    ppermute x1, starting transfers between devices, per_device(): lax.ppermute(to_next, 'row', [(i, i + 2 * (i % 2) - 1) for i in range(1,...  5.85 us
    pallas_call x5, Pallas kernels, call(): pl.pallas_call(kernel, out_shape=tuple((shape(*out) for out in outs)), in...  4.56 us
    all_to_all x1, waiting for transfers between devices, per_device(): g = lax.all_to_all(call_k0(latents.T), ('frm', 'ch'), 0, 0)  3.47 us
    ppermute x1, starting transfers between devices, per_device(): far = lax.ppermute(half, ('row', 'ch'), fars)  2.85 us
  transfers between devices with their start and end apart: 6, of which 1 were waited for; matrix products, arithmetic and copies ran while one was open for 0% of the time, Pallas kernels for 6%

profile of v6, /device:TPU:1, one launch (start us, length us, event | category | flops | bytes accessed | tf_op | source)
XLA Modules:
  0.0 65.7 jit_solution(15451366793000000636)
XLA Ops:
  0.0 1.4 %k0.1 = bf16[16,16,255]{2,1,0:T(8,128)(2,1)} custom-call(bf16[16,255]{1,0:T(8,128)(2,1)} %bitcast.7), custom_call_target="tpu_custom_call" | custom-call | tf_op jit(solution)/shard_map/k0/pallas_call | solution.py:375
  1.4 11.6 %all-to-all-start = ((bf16[16,16,255]{2,1,0:T(8,128)(2,1)}), bf16[16,16,255]{2,1,0:T(8,128)(2,1)S(1)}, u32[]{:S(2)}, u32[]{:S(2)}) async-start(bf16[16,16,255]{2,1,0:T(8,128)(2,1)} %k0.1), calls=%async_computation | async-start | bytes 262144 | tf_op jit(solution)/shard_map/all_to_all | solution.py:443
  13.0 1.0 %k0w.1 = (bf16[448,128]{1,0:T(8,128)(2,1)S(1)}, bf16[224,128]{1,0:T(8,128)(2,1)S(1)}, f32[2,1,128]{2,1,0:T(1,128)S(1)}) custom-call(bf16[432,128]{1,0:T(8,128)(2,1)} %bitcast.6, f32[1,128]{1,0:T(1,128)} %bitcast.8, f32[1,128]{1,0:T(1,128)} %bitcast.9, f32[1,128]{1,0:T(1,128)} %bitcast.10, f32[1,128]{1,0:T(1,128)} %bitcast.11), custom_call_target="tpu_custom_call" | custom-call | tf_op jit(solution)/shard_map/k0w/pallas_call | solution.py:387
  14.0 2.3 %collective-permute-start = (bf16[448,128]{1,0:T(8,128)(2,1)S(1)}, bf16[448,128]{1,0:T(8,128)(2,1)S(1)}, u32[]{:S(2)}, u32[]{:S(2)}) collective-permute-start(bf16[448,128]{1,0:T(8,128)(2,1)S(1)} %get-tuple-element.21.held_ref), channel_id=1, source_target_pairs={{1,0},{2,1},{3,2},{0,3},{7,4},{4,5},{5,6},{6,7},{9,8},{10,9},{11,1... | collective-permute-start | bytes 344072 | tf_op jit(solution)/shard_map/ppermute | solution.py:446
  16.3 2.8 %collective-permute-start.1 = (bf16[224,128]{1,0:T(8,128)(2,1)S(1)}, bf16[224,128]{1,0:T(8,128)(2,1)S(1)}, u32[]{:S(2)}, u32[]{:S(2)}) collective-permute-start(bf16[224,128]{1,0:T(8,128)(2,1)S(1)} %get-tuple-element.24), channel_id=1, source_target_pairs={{34,0},{35,1},{32,2},{33,3},{38,4},{39,5},{36,6},{37,7},{42,8},{43... | collective-permute-start | bytes 172040 | tf_op jit(solution)/shard_map/ppermute | solution.py:448
  19.1 3.5 %all-to-all-done.g_ref = bf16[16,16,255]{2,1,0:T(8,128)(2,1)S(1)} async-done(((bf16[16,16,255]{2,1,0:T(8,128)(2,1)}), bf16[16,16,255]{2,1,0:T(8,128)(2,1)S(1)}, u32[]{:S(2)}, u32[]{:S(2)}) %all-to-all-start) | async-done | bytes 130592 | tf_op jit(solution)/shard_map/all_to_all | solution.py:443
  22.6 0.1 k1t.1
  22.7 5.9 %collective-permute-start.2 = (bf16[64,384]{1,0:T(8,128)(2,1)S(1)}, bf16[64,384]{1,0:T(8,128)(2,1)S(1)}, u32[]{:S(2)}, u32[]{:S(2)}) collective-permute-start(bf16[64,384]{1,0:T(8,128)(2,1)S(1)} %get-tuple-element.25), channel_id=1, source_target_pairs={{4,8},{8,4},{12,16},{16,12},{20,24},{24,20},{28,32},{32,28},{36,40... | collective-permute-start | bytes 147464 | tf_op jit(solution)/shard_map/ppermute | solution.py:452
  28.6 0.1 collective-permute-start.3
  28.7 0.0 collective-permute-done.side_ref
  28.7 1.8 %k1i.1 = (bf16[64,2048]{1,0:T(8,128)(2,1)S(1)}, bf16[864,640]{1,0:T(8,128)(2,1)S(1)}, f32[24,256]{1,0:T(8,128)S(1)}) custom-call(bf16[16,16,255]{2,1,0:T(8,128)(2,1)S(1)} %all-to-all-done.g_ref, bf16[448,128]{1,0:T(8,128)(2,1)S(1)} %get-tuple-element.21.held_ref, bf16[448,128]{1,0:T(8,128)(2,1)S(1)} %collective-permute-done.side_ref), custom_call_target="tpu_custom_call" | custom-call | tf_op jit(solution)/shard_map/k1i/pallas_call | solution.py:403
  30.5 0.0 collective-permute-done.1.far_ref
  30.5 0.0 collective-permute-done.2.next_ref
  30.5 0.0 collective-permute-done.3.mate_ref
  30.6 0.6 collective-permute-start.4
  31.1 1.1 %k1p.1 = (bf16[864,768]{1,0:T(8,128)(2,1)S(1)}, f32[8,128]{1,0:T(8,128)S(1)}) custom-call(bf16[64,2048]{1,0:T(8,128)(2,1)S(1)} %get-tuple-element.27.x_ref, bf16[448,128]{1,0:T(8,128)(2,1)S(1)} %get-tuple-element.21.held_ref, bf16[448,128]{1,0:T(8,128)(2,1)S(1)} %collective-permute-done.side_ref, f32[24,256]{1,0:T(8,128)S(1)} %get-tuple-element.28.acc_ref), custom_call_target="tpu_custom_call" | custom-call | tf_op jit(solution)/shard_map/k1p/pallas_call | solution.py:403
  32.3 0.0 collective-permute-done.4.other_ref
  32.3 1.5 %k1q.1 = (bf16[4,448,128]{2,1,0:T(8,128)(2,1)S(1)}, f32[16,8,128]{2,1,0:T(8,128)S(1)}) custom-call(bf16[864,640]{1,0:T(8,128)(2,1)S(1)} %get-tuple-element.22.mid_ref, bf16[864,768]{1,0:T(8,128)(2,1)S(1)} %get-tuple-element.29.out_ref, f32[8,128]{1,0:T(8,128)S(1)} %get-tuple-element.30.near_ref, bf16[448,128]{1,0:T(8,128)(2,1)S(1)} %get-tuple-element.21.held_ref, ...), custom_call_target="tpu_custom_call" | custom-call | tf_op jit(solution)/shard_map/k1q/pallas_call | solution.py:403
  33.8 10.3 %all_to_all.15.st_ref = f32[16,8,128]{2,1,0:T(8,128)S(1)} all-to-all(f32[16,8,128]{2,1,0:T(8,128)S(1)} %get-tuple-element.33), channel_id=1, replica_groups=mesh['frm'=4,'row'=16,'ch'=4] {'row'}, dimensions={0} | all-to-all | bytes 131072 | tf_op jit(solution)/shard_map/all_to_all | solution.py:463
  44.1 6.9 %k2.1 = (f32[1056,128]{1,0:T(8,128)S(1)}, f32[64,2,128]{2,1,0:T(2,128)S(1)}) custom-call(bf16[864,640]{1,0:T(8,128)(2,1)S(1)} %get-tuple-element.22.mid_ref, bf16[864,768]{1,0:T(8,128)(2,1)S(1)} %get-tuple-element.29.out_ref, bf16[4,448,128]{2,1,0:T(8,128)(2,1)S(1)} %get-tuple-element.32.wall_ref, f32[16,8,128]{2,1,0:T(8,128)S(1)} %all_to_all.15.st_ref, ...), custom_call_target="tpu_custom_call" | custom-call | tf_op jit(solution)/shard_map/k2/pallas_call | solution.py:414
  51.0 13.5 %all_to_all.16.st_ref = f32[64,2,128]{2,1,0:T(2,128)S(1)} all-to-all(f32[64,2,128]{2,1,0:T(2,128)S(1)} %get-tuple-element.35), channel_id=1, replica_groups=mesh['frm'=4,'row'=16,'ch'=4] {'frm','row'}, dimensions={0} | all-to-all | bytes 131072 | tf_op jit(solution)/shard_map/all_to_all | solution.py:465
  64.5 1.2 %k3.1 = bf16[1,6,170,128]{3,2,1,0:T(8,128)(2,1)} custom-call(f32[1056,128]{1,0:T(8,128)S(1)} %get-tuple-element.34.mix_ref, f32[64,2,128]{2,1,0:T(2,128)S(1)} %all_to_all.16.st_ref, f32[2,1,128]{2,1,0:T(1,128)S(1)} %get-tuple-element.36.par_ref), custom_call_target="tpu_custom_call" | custom-call | tf_op jit(solution)/shard_map/k3/pallas_call | solution.py:431
  (1 shorter events, 0.0 us)
Async XLA Ops:
  1.4 21.2 %all-to-all-start = ((bf16[16,16,255]{2,1,0:T(8,128)(2,1)}), bf16[16,16,255]{2,1,0:T(8,128)(2,1)S(1)}, u32[]{:S(2)}, u32[]{:S(2)}) async-start(bf16[16,16,255]{2,1,0:T(8,128)(2,1)} %k0.1), calls=%async_computation | async-start | bytes 262144 | tf_op jit(solution)/shard_map/all_to_all | solution.py:443
  14.0 14.7 %collective-permute-start = (bf16[448,128]{1,0:T(8,128)(2,1)S(1)}, bf16[448,128]{1,0:T(8,128)(2,1)S(1)}, u32[]{:S(2)}, u32[]{:S(2)}) collective-permute-start(bf16[448,128]{1,0:T(8,128)(2,1)S(1)} %get-tuple-element.21.held_ref), channel_id=1, source_target_pairs={{1,0},{2,1},{3,2},{0,3},{7,4},{4,5},{5,6},{6,7},{9,8},{10,9},{11,1... | collective-permute-start | bytes 344072 | tf_op jit(solution)/shard_map/ppermute | solution.py:446
  16.3 14.2 %collective-permute-start.1 = (bf16[224,128]{1,0:T(8,128)(2,1)S(1)}, bf16[224,128]{1,0:T(8,128)(2,1)S(1)}, u32[]{:S(2)}, u32[]{:S(2)}) collective-permute-start(bf16[224,128]{1,0:T(8,128)(2,1)S(1)} %get-tuple-element.24), channel_id=1, source_target_pairs={{34,0},{35,1},{32,2},{33,3},{38,4},{39,5},{36,6},{37,7},{42,8},{43... | collective-permute-start | bytes 172040 | tf_op jit(solution)/shard_map/ppermute | solution.py:448
  22.7 7.7 %collective-permute-start.2 = (bf16[64,384]{1,0:T(8,128)(2,1)S(1)}, bf16[64,384]{1,0:T(8,128)(2,1)S(1)}, u32[]{:S(2)}, u32[]{:S(2)}) collective-permute-start(bf16[64,384]{1,0:T(8,128)(2,1)S(1)} %get-tuple-element.25), channel_id=1, source_target_pairs={{4,8},{8,4},{12,16},{16,12},{20,24},{24,20},{28,32},{32,28},{36,40... | collective-permute-start | bytes 147464 | tf_op jit(solution)/shard_map/ppermute | solution.py:452
  28.6 1.9 %collective-permute-start.3 = (bf16[64,384]{1,0:T(8,128)(2,1)S(1)}, bf16[64,384]{1,0:T(8,128)(2,1)S(1)}, u32[]{:S(2)}, u32[]{:S(2)}) collective-permute-start(bf16[64,384]{1,0:T(8,128)(2,1)S(1)} %get-tuple-element.26), channel_id=1, source_target_pairs={{0,4},{4,0},{8,12},{12,8},{16,20},{20,16},{24,28},{28,24},{32,36},... | collective-permute-start | bytes 147464 | tf_op jit(solution)/shard_map/ppermute | solution.py:453
  30.6 1.7 %collective-permute-start.4 = (bf16[672,128]{1,0:T(8,128)(2,1)S(1)}, bf16[672,128]{1,0:T(8,128)(2,1)S(1)}, u32[]{:S(2)}, u32[]{:S(2)}) collective-permute-start(bf16[672,128]{1,0:T(8,128)(2,1)S(1)} %get-tuple-element.31.mine_ref), channel_id=1, source_target_pairs={{0,4},{4,0},{8,12},{12,8},{16,20},{20,16},{24,28},{28,24},{32,36},... | collective-permute-start | bytes 516104 | tf_op jit(solution)/shard_map/ppermute | solution.py:458

commit v7 on v6

--- a/solution.py
+++ b/solution.py
@@ -229,7 +229,8 @@
 
 def k1q(mid_ref, out_ref, near_ref, held_ref, mine_ref, other_ref, wall_ref, st_ref):
     c, core = lax.axis_index("ch"), lax.rem(lax.axis_index("row"), 2)
-    side, side_x, far = (lax.rem(c + i, 4) for i in (1 + 2 * core, 3 - 2 * core, 2))
+    up = jnp.where((lax.axis_index("row") >= 8) == (core == 0), 1, 3)
+    side, side_x, far = (lax.rem(c + i, 4) for i in (up, 4 - up, 2))
     wall_ref[c] = held_ref[...]
     wall_ref[side] = mine_ref[:HELD, :]
     wall_ref[side_x] = other_ref[:HELD, :]
@@ -442,7 +443,13 @@
     params = [v.reshape(1, 128) for v in (in_gain, in_shift, mid_gain, mid_shift)]
     g = lax.all_to_all(call_k0(latents.T), ("frm", "ch"), 0, 0)
     held, half, par = call_k0w(in_weight.reshape(TAPROWS, 128), *params)
-    sides = [(4 * i + (j + 1 + 2 * (i % 2)) % 4, 4 * i + j) for i in range(16) for j in range(4)]
+    sides = []
+    for i in range(16):
+        zl, core = i // 8, i % 2
+        for j in range(4):
+            up = (zl == 0) if core else (zl == 1)
+            source = i if core else i ^ 8
+            sides.append((4 * source + (j + (1 if up else 3)) % 4, 4 * i + j))
     side = lax.ppermute(held, ("row", "ch"), sides)
     fars = [(4 * (i ^ 8) + (j + 2) % 4, 4 * i + j) for i in range(16) for j in range(4)]
     far = lax.ppermute(half, ("row", "ch"), fars)

time: 66 us -> 65.7 us (level)
  starting transfers between devices: 23.3 us -> 22.6 us
    ppermute x1, starting transfers between devices: 2.85 us -> 1.64 us  [per_device(): far = lax.ppermute(half, ('row', 'ch'), fars)]
    ppermute x1, starting transfers between devices: 2.34 us -> 3.55 us  [per_device(): side = lax.ppermute(held, ('row', 'ch'), sides)]
    ppermute x1, starting transfers between devices: 5.85 us -> 5.17 us  [per_device(): lax.ppermute(to_next, 'row', [(i, i + 2 * (i % 2) - 1) for i in range(1,...]
where the time goes in v7:
time: 65.7 us; the launch traced here: 65.4 us
  blocking collectives  24.3 us (37%)
  starting transfers between devices  22.6 us (34%)
  Pallas kernels  15 us (23%)
  waiting for transfers between devices  3.39 us (5%)
    all_to_all x1, blocking collectives, per_device(): st = lax.all_to_all(st, ('frm', 'row'), 0, 0)  13.6 us
    all_to_all x1, starting transfers between devices, per_device(): g = lax.all_to_all(call_k0(latents.T), ('frm', 'ch'), 0, 0)  11.6 us
    all_to_all x1, blocking collectives, per_device(): st = lax.all_to_all(st, 'row', 0, 0)  10.7 us
    pallas_call x1, Pallas kernels, call_k2(): pl.pallas_call(k2, out_shape=(shape((OWN, 128), jnp.float32), shape((64,...  6.89 us
    ppermute x1, starting transfers between devices, per_device(): lax.ppermute(to_next, 'row', [(i, i + 2 * (i % 2) - 1) for i in range(1,...  5.17 us
    pallas_call x5, Pallas kernels, call(): pl.pallas_call(kernel, out_shape=tuple((shape(*out) for out in outs)), in...  4.56 us
    ppermute x1, starting transfers between devices, per_device(): side = lax.ppermute(held, ('row', 'ch'), sides)  3.55 us
    all_to_all x1, waiting for transfers between devices, per_device(): g = lax.all_to_all(call_k0(latents.T), ('frm', 'ch'), 0, 0)  3.38 us
  transfers between devices with their start and end apart: 6, of which 1 were waited for; matrix products, arithmetic and copies ran while one was open for 0% of the time, Pallas kernels for 6%

profile of v7, /device:TPU:1, one launch (start us, length us, event | category | flops | bytes accessed | tf_op | source)
XLA Modules:
  0.0 65.4 jit_solution(10960283020822540420)
XLA Ops:
  0.0 1.4 %k0.1 = bf16[16,16,255]{2,1,0:T(8,128)(2,1)} custom-call(bf16[16,255]{1,0:T(8,128)(2,1)} %bitcast.7), custom_call_target="tpu_custom_call" | custom-call | tf_op jit(solution)/shard_map/k0/pallas_call | solution.py:376
  1.4 11.6 %all-to-all-start = ((bf16[16,16,255]{2,1,0:T(8,128)(2,1)}), bf16[16,16,255]{2,1,0:T(8,128)(2,1)S(1)}, u32[]{:S(2)}, u32[]{:S(2)}) async-start(bf16[16,16,255]{2,1,0:T(8,128)(2,1)} %k0.1), calls=%async_computation | async-start | bytes 262144 | tf_op jit(solution)/shard_map/all_to_all | solution.py:444
  13.0 1.0 %k0w.1 = (bf16[448,128]{1,0:T(8,128)(2,1)S(1)}, bf16[224,128]{1,0:T(8,128)(2,1)S(1)}, f32[2,1,128]{2,1,0:T(1,128)S(1)}) custom-call(bf16[432,128]{1,0:T(8,128)(2,1)} %bitcast.6, f32[1,128]{1,0:T(1,128)} %bitcast.8, f32[1,128]{1,0:T(1,128)} %bitcast.9, f32[1,128]{1,0:T(1,128)} %bitcast.10, f32[1,128]{1,0:T(1,128)} %bitcast.11), custom_call_target="tpu_custom_call" | custom-call | tf_op jit(solution)/shard_map/k0w/pallas_call | solution.py:388
  14.0 3.5 %collective-permute-start = (bf16[448,128]{1,0:T(8,128)(2,1)S(1)}, bf16[448,128]{1,0:T(8,128)(2,1)S(1)}, u32[]{:S(2)}, u32[]{:S(2)}) collective-permute-start(bf16[448,128]{1,0:T(8,128)(2,1)S(1)} %get-tuple-element.21.held_ref), channel_id=1, source_target_pairs={{35,0},{32,1},{33,2},{34,3},{5,4},{6,5},{7,6},{4,7},{43,8},{40,9},... | collective-permute-start | bytes 344072 | tf_op jit(solution)/shard_map/ppermute | solution.py:453
  17.5 1.6 %collective-permute-start.1 = (bf16[224,128]{1,0:T(8,128)(2,1)S(1)}, bf16[224,128]{1,0:T(8,128)(2,1)S(1)}, u32[]{:S(2)}, u32[]{:S(2)}) collective-permute-start(bf16[224,128]{1,0:T(8,128)(2,1)S(1)} %get-tuple-element.24), channel_id=1, source_target_pairs={{34,0},{35,1},{32,2},{33,3},{38,4},{39,5},{36,6},{37,7},{42,8},{43... | collective-permute-start | bytes 172040 | tf_op jit(solution)/shard_map/ppermute | solution.py:455
  19.1 3.4 %all-to-all-done.g_ref = bf16[16,16,255]{2,1,0:T(8,128)(2,1)S(1)} async-done(((bf16[16,16,255]{2,1,0:T(8,128)(2,1)}), bf16[16,16,255]{2,1,0:T(8,128)(2,1)S(1)}, u32[]{:S(2)}, u32[]{:S(2)}) %all-to-all-start) | async-done | bytes 130592 | tf_op jit(solution)/shard_map/all_to_all | solution.py:444
  22.5 0.1 k1t.1
  22.6 5.2 %collective-permute-start.2 = (bf16[64,384]{1,0:T(8,128)(2,1)S(1)}, bf16[64,384]{1,0:T(8,128)(2,1)S(1)}, u32[]{:S(2)}, u32[]{:S(2)}) collective-permute-start(bf16[64,384]{1,0:T(8,128)(2,1)S(1)} %get-tuple-element.25), channel_id=1, source_target_pairs={{4,8},{8,4},{12,16},{16,12},{20,24},{24,20},{28,32},{32,28},{36,40... | collective-permute-start | bytes 147464 | tf_op jit(solution)/shard_map/ppermute | solution.py:459
  27.8 0.1 collective-permute-start.3
  27.9 0.0 collective-permute-done.side_ref
  27.9 1.8 %k1i.1 = (bf16[64,2048]{1,0:T(8,128)(2,1)S(1)}, bf16[864,640]{1,0:T(8,128)(2,1)S(1)}, f32[24,256]{1,0:T(8,128)S(1)}) custom-call(bf16[16,16,255]{2,1,0:T(8,128)(2,1)S(1)} %all-to-all-done.g_ref, bf16[448,128]{1,0:T(8,128)(2,1)S(1)} %get-tuple-element.21.held_ref, bf16[448,128]{1,0:T(8,128)(2,1)S(1)} %collective-permute-done.side_ref), custom_call_target="tpu_custom_call" | custom-call | tf_op jit(solution)/shard_map/k1i/pallas_call | solution.py:404
  29.7 0.0 collective-permute-done.1.far_ref
  29.7 0.0 collective-permute-done.2.next_ref
  29.7 0.0 collective-permute-done.3.mate_ref
  29.8 0.6 collective-permute-start.4
  30.3 1.1 %k1p.1 = (bf16[864,768]{1,0:T(8,128)(2,1)S(1)}, f32[8,128]{1,0:T(8,128)S(1)}) custom-call(bf16[64,2048]{1,0:T(8,128)(2,1)S(1)} %get-tuple-element.27.x_ref, bf16[448,128]{1,0:T(8,128)(2,1)S(1)} %get-tuple-element.21.held_ref, bf16[448,128]{1,0:T(8,128)(2,1)S(1)} %collective-permute-done.side_ref, f32[24,256]{1,0:T(8,128)S(1)} %get-tuple-element.28.acc_ref), custom_call_target="tpu_custom_call" | custom-call | tf_op jit(solution)/shard_map/k1p/pallas_call | solution.py:404
  31.5 0.0 collective-permute-done.4.other_ref
  31.5 1.5 %k1q.1 = (bf16[4,448,128]{2,1,0:T(8,128)(2,1)S(1)}, f32[16,8,128]{2,1,0:T(8,128)S(1)}) custom-call(bf16[864,640]{1,0:T(8,128)(2,1)S(1)} %get-tuple-element.22.mid_ref, bf16[864,768]{1,0:T(8,128)(2,1)S(1)} %get-tuple-element.29.out_ref, f32[8,128]{1,0:T(8,128)S(1)} %get-tuple-element.30.near_ref, bf16[448,128]{1,0:T(8,128)(2,1)S(1)} %get-tuple-element.21.held_ref, ...), custom_call_target="tpu_custom_call" | custom-call | tf_op jit(solution)/shard_map/k1q/pallas_call | solution.py:404
  33.0 10.7 %all_to_all.15.st_ref = f32[16,8,128]{2,1,0:T(8,128)S(1)} all-to-all(f32[16,8,128]{2,1,0:T(8,128)S(1)} %get-tuple-element.33), channel_id=1, replica_groups=mesh['frm'=4,'row'=16,'ch'=4] {'row'}, dimensions={0} | all-to-all | bytes 131072 | tf_op jit(solution)/shard_map/all_to_all | solution.py:470
  43.8 6.9 %k2.1 = (f32[1056,128]{1,0:T(8,128)S(1)}, f32[64,2,128]{2,1,0:T(2,128)S(1)}) custom-call(bf16[864,640]{1,0:T(8,128)(2,1)S(1)} %get-tuple-element.22.mid_ref, bf16[864,768]{1,0:T(8,128)(2,1)S(1)} %get-tuple-element.29.out_ref, bf16[4,448,128]{2,1,0:T(8,128)(2,1)S(1)} %get-tuple-element.32.wall_ref, f32[16,8,128]{2,1,0:T(8,128)S(1)} %all_to_all.15.st_ref, ...), custom_call_target="tpu_custom_call" | custom-call | tf_op jit(solution)/shard_map/k2/pallas_call | solution.py:415
  50.7 13.6 %all_to_all.16.st_ref = f32[64,2,128]{2,1,0:T(2,128)S(1)} all-to-all(f32[64,2,128]{2,1,0:T(2,128)S(1)} %get-tuple-element.35), channel_id=1, replica_groups=mesh['frm'=4,'row'=16,'ch'=4] {'frm','row'}, dimensions={0} | all-to-all | bytes 131072 | tf_op jit(solution)/shard_map/all_to_all | solution.py:472
  64.2 1.2 %k3.1 = bf16[1,6,170,128]{3,2,1,0:T(8,128)(2,1)} custom-call(f32[1056,128]{1,0:T(8,128)S(1)} %get-tuple-element.34.mix_ref, f32[64,2,128]{2,1,0:T(2,128)S(1)} %all_to_all.16.st_ref, f32[2,1,128]{2,1,0:T(1,128)S(1)} %get-tuple-element.36.par_ref), custom_call_target="tpu_custom_call" | custom-call | tf_op jit(solution)/shard_map/k3/pallas_call | solution.py:432
  (1 shorter events, 0.0 us)
Async XLA Ops:
  1.4 21.1 %all-to-all-start = ((bf16[16,16,255]{2,1,0:T(8,128)(2,1)}), bf16[16,16,255]{2,1,0:T(8,128)(2,1)S(1)}, u32[]{:S(2)}, u32[]{:S(2)}) async-start(bf16[16,16,255]{2,1,0:T(8,128)(2,1)} %k0.1), calls=%async_computation | async-start | bytes 262144 | tf_op jit(solution)/shard_map/all_to_all | solution.py:444
  14.0 14.0 %collective-permute-start = (bf16[448,128]{1,0:T(8,128)(2,1)S(1)}, bf16[448,128]{1,0:T(8,128)(2,1)S(1)}, u32[]{:S(2)}, u32[]{:S(2)}) collective-permute-start(bf16[448,128]{1,0:T(8,128)(2,1)S(1)} %get-tuple-element.21.held_ref), channel_id=1, source_target_pairs={{35,0},{32,1},{33,2},{34,3},{5,4},{6,5},{7,6},{4,7},{43,8},{40,9},... | collective-permute-start | bytes 344072 | tf_op jit(solution)/shard_map/ppermute | solution.py:453
  17.5 12.2 %collective-permute-start.1 = (bf16[224,128]{1,0:T(8,128)(2,1)S(1)}, bf16[224,128]{1,0:T(8,128)(2,1)S(1)}, u32[]{:S(2)}, u32[]{:S(2)}) collective-permute-start(bf16[224,128]{1,0:T(8,128)(2,1)S(1)} %get-tuple-element.24), channel_id=1, source_target_pairs={{34,0},{35,1},{32,2},{33,3},{38,4},{39,5},{36,6},{37,7},{42,8},{43... | collective-permute-start | bytes 172040 | tf_op jit(solution)/shard_map/ppermute | solution.py:455
  22.6 7.1 %collective-permute-start.2 = (bf16[64,384]{1,0:T(8,128)(2,1)S(1)}, bf16[64,384]{1,0:T(8,128)(2,1)S(1)}, u32[]{:S(2)}, u32[]{:S(2)}) collective-permute-start(bf16[64,384]{1,0:T(8,128)(2,1)S(1)} %get-tuple-element.25), channel_id=1, source_target_pairs={{4,8},{8,4},{12,16},{16,12},{20,24},{24,20},{28,32},{32,28},{36,40... | collective-permute-start | bytes 147464 | tf_op jit(solution)/shard_map/ppermute | solution.py:459
  27.8 1.9 %collective-permute-start.3 = (bf16[64,384]{1,0:T(8,128)(2,1)S(1)}, bf16[64,384]{1,0:T(8,128)(2,1)S(1)}, u32[]{:S(2)}, u32[]{:S(2)}) collective-permute-start(bf16[64,384]{1,0:T(8,128)(2,1)S(1)} %get-tuple-element.26), channel_id=1, source_target_pairs={{0,4},{4,0},{8,12},{12,8},{16,20},{20,16},{24,28},{28,24},{32,36},... | collective-permute-start | bytes 147464 | tf_op jit(solution)/shard_map/ppermute | solution.py:460
  29.8 1.7 %collective-permute-start.4 = (bf16[672,128]{1,0:T(8,128)(2,1)S(1)}, bf16[672,128]{1,0:T(8,128)(2,1)S(1)}, u32[]{:S(2)}, u32[]{:S(2)}) collective-permute-start(bf16[672,128]{1,0:T(8,128)(2,1)S(1)} %get-tuple-element.31.mine_ref), channel_id=1, source_target_pairs={{0,4},{4,0},{8,12},{12,8},{16,20},{20,16},{24,28},{28,24},{32,36},... | collective-permute-start | bytes 516104 | tf_op jit(solution)/shard_map/ppermute | solution.py:465
